TPU v7x, 32 devices: a whole 2x2x4 slice. The times are simulated.
32 devices in a mesh: dp: 8 (over y, x, core), seq: 4 (over z).
Axes of the slice: x: 2, y: 2, z: 4, core: 2. Of those that a mesh axis runs over, the one named last changes fastest.
Arguments:
- img_qkv: bfloat16 [8, 448, 3, 512], P('dp', 'seq'), may hold values from -6 to 6
- txt_qkv: bfloat16 [8, 64, 3, 512], P('dp', 'seq'), may hold values from -6 to 6
- img_cot: bfloat16 [8, 448, 512], P('dp', 'seq'), may hold values from -48 to 48
- txt_cot: bfloat16 [8, 64, 512], P('dp', 'seq'), may hold values from -48 to 48
- norm_gains: float32 [4, 128], replicated, may hold values from 0.5 to 2
Outputs:
- img_out: bfloat16 [8, 448, 512], P('dp', 'seq')
- txt_out: bfloat16 [8, 64, 512], P('dp', 'seq')
- img_grad: bfloat16 [8, 448, 3, 512], P('dp', 'seq')
- txt_grad: bfloat16 [8, 64, 3, 512], P('dp', 'seq')
- gain_grad: float32 [512], P('dp')
All inputs are finite; a program needn't handle non-finite values.
Results may differ from a plain program's by a relative error of at most 0.012.
The roundings to bfloat16 on the way count: a program that leaves them out, or rounds other values in their place, can miss the bound.
Values may be sent and summed in bfloat16 or wider, within the bound.
No kernel may reach another device: no remote copies, remote signals or barrier semaphores. Data moves between devices by JAX's collectives and lax.ppermute only.
A program may use at most 128 MiB of HBM per device.

v0:
```python
import math

import jax
import jax.numpy as jnp
from jax import lax
from jax.sharding import PartitionSpec as P

HD = 128
GRID_W = 64


EPSILON = 1e-06


def rope_tables(seq_len, text_len, grid_w, head_dim):
    position = jnp.arange(seq_len, dtype=jnp.int32)
    image_pos = jnp.maximum(position - text_len, 0)
    image_col = (position >= text_len).astype(jnp.float32)
    row_pos = (image_pos // grid_w).astype(jnp.float32) * image_col
    col_pos = (image_pos % grid_w).astype(jnp.float32) * image_col
    time_dims = head_dim // 8
    axis_dims = (head_dim - time_dims) // 2
    channel = jnp.arange(head_dim, dtype=jnp.int32)
    in_rows = (channel >= time_dims) & (channel < time_dims + axis_dims)
    in_cols = channel >= time_dims + axis_dims
    within = jnp.where(in_cols, channel - time_dims - axis_dims, channel - time_dims)
    within = jnp.maximum(within, 0) // 2
    frequency = jnp.power(jnp.float32(10000.0), -2.0 * within.astype(jnp.float32) / axis_dims)
    angles = jnp.where(in_rows[None, :], row_pos[:, None] * frequency[None, :], jnp.float32(0.0))
    angles = jnp.where(in_cols[None, :], col_pos[:, None] * frequency[None, :], angles)
    even_lane = (channel % 2 == 0)[None, :]
    return (jnp.cos(angles), jnp.sin(angles), even_lane, image_col[:, None])


def rms_rows(values_in):
    inverse = lax.rsqrt(jnp.mean(values_in * values_in, axis=-1, keepdims=True) + EPSILON)
    return (values_in * inverse, inverse)


def rms_back(grad_hat, hat_vals, inverse):
    middle = jnp.mean(grad_hat * hat_vals, axis=-1, keepdims=True)
    return (grad_hat - hat_vals * middle) * inverse


def rotate(values_in, tables):
    cos_t, sin_t, even_lane, image_col = tables
    following = jnp.roll(values_in, -1, axis=-1)
    preceding = jnp.roll(values_in, 1, axis=-1)
    turned = jnp.where(even_lane, -following, preceding)
    return values_in * cos_t + turned * sin_t


def unrotate(grad_in, tables):
    cos_t, sin_t, even_lane, image_col = tables
    scaled = grad_in * sin_t
    following = jnp.roll(scaled, -1, axis=-1)
    preceding = jnp.roll(scaled, 1, axis=-1)
    turned = jnp.where(even_lane, following, -preceding)
    return grad_in * cos_t + turned


def head_pass(q_raw, k_raw, value, d_out, norm_gains, tables, n_blocks):
    image_col = tables[3]
    seq_len, head_dim = q_raw.shape
    attn_scale = 1.0 / math.sqrt(head_dim)
    q_hat, q_inv = rms_rows(q_raw)
    k_hat, k_inv = rms_rows(k_raw)
    q_gain = jnp.where(image_col > 0.5, norm_gains[0][None, :], norm_gains[2][None, :])
    k_gain = jnp.where(image_col > 0.5, norm_gains[1][None, :], norm_gains[3][None, :])
    q_rot = rotate(q_hat * q_gain, tables).astype(jnp.bfloat16)
    k_rot = rotate(k_hat * k_gain, tables).astype(jnp.bfloat16)
    block_rows = seq_len // n_blocks
    contract_last = (((1,), (1,)), ((), ()))
    contract_first = (((0,), (0,)), ((), ()))

    def block_step(pieces):
        q_block, d_block = pieces
        scores = (
            lax.dot_general(q_block, k_rot, contract_last, preferred_element_type=jnp.float32)
            * attn_scale
        )
        exp_scores = jnp.exp(scores)
        row_sum = jnp.sum(exp_scores, axis=1, keepdims=True)
        prob_half = (exp_scores / row_sum).astype(jnp.bfloat16)
        out_block = jnp.dot(prob_half, value, preferred_element_type=jnp.float32).astype(
            jnp.bfloat16
        )
        row_delta = jnp.sum(
            d_block.astype(jnp.float32) * out_block.astype(jnp.float32), axis=1, keepdims=True
        )
        d_prob = lax.dot_general(d_block, value, contract_last, preferred_element_type=jnp.float32)
        d_score = (exp_scores / row_sum * (d_prob - row_delta) * attn_scale).astype(jnp.bfloat16)
        return (out_block, prob_half, d_score)

    q_blocks = q_rot.reshape(n_blocks, block_rows, head_dim)
    d_blocks = d_out.reshape(n_blocks, block_rows, head_dim)
    out_blocks, prob_blocks, score_blocks = lax.map(block_step, (q_blocks, d_blocks))
    attn_out = out_blocks.reshape(seq_len, head_dim)
    prob_all = prob_blocks.reshape(seq_len, seq_len)
    d_score_all = score_blocks.reshape(seq_len, seq_len)
    d_value = lax.dot_general(prob_all, d_out, contract_first, preferred_element_type=jnp.float32)
    dq_rot = jnp.dot(d_score_all, k_rot, preferred_element_type=jnp.float32)
    dk_rot = lax.dot_general(d_score_all, q_rot, contract_first, preferred_element_type=jnp.float32)
    dq_norm = unrotate(dq_rot, tables)
    dk_norm = unrotate(dk_rot, tables)
    text_col = 1.0 - image_col
    gain_terms = jnp.stack(
        [
            jnp.sum(dq_norm * q_hat * image_col, axis=0),
            jnp.sum(dk_norm * k_hat * image_col, axis=0),
            jnp.sum(dq_norm * q_hat * text_col, axis=0),
            jnp.sum(dk_norm * k_hat * text_col, axis=0),
        ]
    )
    d_query = rms_back(dq_norm * q_gain, q_hat, q_inv).astype(jnp.bfloat16)
    d_key = rms_back(dk_norm * k_gain, k_hat, k_inv).astype(jnp.bfloat16)
    packed = jnp.stack([d_query, d_key, d_value.astype(jnp.bfloat16), attn_out], axis=1)
    return (packed, gain_terms)


def per_device(img_qkv, txt_qkv, img_cot, txt_cot, norm_gains):
    seq_devices = lax.axis_size("seq")
    data_devices = lax.axis_size("dp")
    img_pack = jnp.concatenate([img_qkv, img_cot[:, :, None, :]], axis=2)
    txt_pack = jnp.concatenate([txt_qkv, txt_cot[:, :, None, :]], axis=2)
    img_heads, txt_heads = (
        lax.all_to_all(img_pack, "seq", split_axis=3, concat_axis=1, tiled=True),
        lax.all_to_all(txt_pack, "seq", split_axis=3, concat_axis=1, tiled=True),
    )
    img_proj = img_heads[:, :, 0:3, :]
    txt_proj = txt_heads[:, :, 0:3, :]
    img_grad_in = img_heads[:, :, 3, :]
    txt_grad_in = txt_heads[:, :, 3, :]
    text_len = txt_proj.shape[1]
    joint = jnp.concatenate([txt_proj[0], img_proj[0]], axis=0)
    joint_cot = jnp.concatenate([txt_grad_in[0], img_grad_in[0]], axis=0)
    seq_len = joint.shape[0]
    head_dim = HD
    local_heads = joint.shape[2] // head_dim
    tables = rope_tables(seq_len, text_len, GRID_W, head_dim)
    n_blocks = max(1, seq_len // 512)
    packed, gain_terms = head_pass(
        joint[:, 0, 0:head_dim].astype(jnp.float32),
        joint[:, 1, 0:head_dim].astype(jnp.float32),
        joint[:, 2, 0:head_dim],
        joint_cot,
        norm_gains,
        tables,
        n_blocks,
    )
    txt_back = packed[None, :text_len]
    img_back = packed[None, text_len:]
    img_tokens, txt_tokens = (
        lax.all_to_all(img_back, "seq", split_axis=1, concat_axis=3, tiled=True),
        lax.all_to_all(txt_back, "seq", split_axis=1, concat_axis=3, tiled=True),
    )
    img_out = img_tokens[:, :, 3, :]
    txt_out = txt_tokens[:, :, 3, :]
    img_grad = img_tokens[:, :, 0:3, :]
    txt_grad = txt_tokens[:, :, 0:3, :]
    grad_scale = 1.0 / math.sqrt(data_devices * seq_len * local_heads * seq_devices)
    partial_grad = (gain_terms * grad_scale).reshape(4 * head_dim)
    summed = lax.psum(partial_grad, "seq")
    gain_grad = lax.psum_scatter(summed, "dp", scatter_dimension=0, tiled=True)
    return (img_out, txt_out, img_grad, txt_grad, gain_grad)


def solution(mesh):
    in_specs = (
        P("dp", "seq", None, None),
        P("dp", "seq", None, None),
        P("dp", "seq", None),
        P("dp", "seq", None),
        P(),
    )
    out_specs = (
        P("dp", "seq", None),
        P("dp", "seq", None),
        P("dp", "seq", None, None),
        P("dp", "seq", None, None),
        P("dp"),
    )
    return jax.shard_map(
        per_device, mesh=mesh, in_specs=in_specs, out_specs=out_specs, check_vma=False
    )
```

profile of v0, /device:TPU:0, one launch (start us, length us, event | category | flops | bytes accessed | tf_op | source)
XLA Modules:
  0.0 86.9 jit_solution(9350787687641201949)
XLA Ops:
  0.6 0.8 pad_maximum_fusion.4
  1.5 0.3 copy.49
  1.8 1.2 %reshape.673 = bf16[4,2,4096]{2,1,0:T(2,128)(2,1)} reshape(bf16[512,1,4,16]{3,2,1,0:T(4,128)(2,1)S(1)} %bitcast.164) | data formatting | bytes 131072
  3.0 6.4 %all-to-all-start = ((bf16[4,2,4096]{2,1,0:T(2,128)(2,1)}), bf16[4,2,4096]{2,1,0:T(2,128)(2,1)S(1)}, u32[]{:S(2)}, u32[]{:S(2)}) async-start(bf16[4,2,4096]{2,1,0:T(2,128)(2,1)} %reshape.673), calls=%async_computation | async-start | bytes 131072 | tf_op jit(solution)/shard_map/all_to_all | solution.py:128
  9.5 1.1 %copy.51 = bf16[1,112,4,512]{1,2,0,3:T(4,128)(2,1)} copy(bf16[1,112,4,512]{3,1,2,0:T(8,128)(2,1)S(1)} %pad_maximum_fusion.1) | data formatting | bytes 917504 | tf_op jit(solution)/shard_map/concatenate | solution.py:124
  10.6 4.6 %all-to-all-done = bf16[4,2,4096]{2,1,0:T(2,128)(2,1)S(1)} async-done(((bf16[4,2,4096]{2,1,0:T(2,128)(2,1)}), bf16[4,2,4096]{2,1,0:T(2,128)(2,1)S(1)}, u32[]{:S(2)}, u32[]{:S(2)}) %all-to-all-start) | async-done | bytes 65568 | tf_op jit(solution)/shard_map/all_to_all | solution.py:128
  15.2 3.6 %all-to-all-start.1 = ((bf16[1,112,4,512]{1,2,0,3:T(4,128)(2,1)}), bf16[1,112,4,512]{1,2,0,3:T(4,128)(2,1)S(1)}, u32[]{:S(2)}, u32[]{:S(2)}) async-start(bf16[1,112,4,512]{1,2,0,3:T(4,128)(2,1)} %copy.51), calls=%async_computation.1 | async-start | bytes 1048576 | tf_op jit(solution)/shard_map/all_to_all | solution.py:127
  18.8 0.4 reshape.674
  19.5 12.6 %all-to-all-done.1 = bf16[1,112,4,512]{1,2,0,3:T(4,128)(2,1)S(1)} async-done(((bf16[1,112,4,512]{1,2,0,3:T(4,128)(2,1)}), bf16[1,112,4,512]{1,2,0,3:T(4,128)(2,1)S(1)}, u32[]{:S(2)}, u32[]{:S(2)}) %all-to-all-start.1) | async-done | bytes 458784 | tf_op jit(solution)/shard_map/all_to_all | solution.py:127
  32.1 0.4 copy.52
  33.6 2.6 %fusion.118 = (f32[512]{0:T(512)S(1)}, f32[512,512]{0,1:T(8,128)S(1)}) fusion(f32[512,1,127]{2,0,1:T(8,128)S(1)} %get-tuple-element.67, f32[512,1,1]{2,0,1:T(8,128)S(1)} %get-tuple-element.64, f32[512,1,1]{2,0,1:T(8,128)S(1)} %get-tuple-element.63, f32[512,1,127]{2,0,1:T(8,128)S(1)} %get-tuple-element.68, f32[128]{0:T(128)S(1)} %get-tuple-element.74, ...), kind=kOutput, calls=%fused_computation.182 | convolution fusion | flops 69729792 | bytes 2372992 | tf_op jit(solution)/shard_map/while/body/eval_jaxpr/dot_general | solution.py:79
  36.3 0.4 multiply_reduce_fusion.4
  36.7 0.3 fusion.4
  37.0 0.3 fusion.3
  37.4 1.6 %fusion.78 = f32[512,128]{1,0:T(8,128)S(1)} fusion(bf16[512,512]{0,1:T(8,128)(2,1)S(1)} %fusion.3, f32[512,1]{1,0:T(8,128)S(1)} %get-tuple-element.65, f32[512,127]{1,0:T(8,128)S(1)} %get-tuple-element.69, f32[512,127]{1,0:T(8,128)S(1)} %get-tuple-element.66, f32[512,1]{1,0:T(8,128)S(1)} %get-tuple-element.62, f32[512]{0:T(512)S(1)} %get-tuple-element.88, ...), kind=kOutput, calls=%fused_computation.113 | convolution fusion | flops 68157440 | bytes 1450368 | tf_op jit(solution)/shard_map/dot_general | solution.py:102
  38.9 2.2 %fusion.50 = (f32[512,128]{1,0:T(8,128)S(1)}, f32[512,128]{1,0:T(8,128)S(1)}, f32[512,128]{1,0:T(8,128)S(1)}) fusion(f32[512]{0:T(512)S(1)} %get-tuple-element.88, f32[128]{0:T(128)S(1)} %multiply_power_fusion, f32[512]{0:T(512)S(1)} %get-tuple-element.87, pred[128]{0:T(512)(128)(4,1)S(1)} %get-tuple-element.89, pred[128]{0:T(512)(128)(4,1)S(1)} %iota_compare_fusion.1, ...), kind=kOutput, calls=%fused_computation.84 | convolution fusion | flops 68550656 | bytes 2236800 | tf_op jit(solution)/shard_map/dot_general | solution.py:103
  41.7 1.8 %multiply_reduce_fusion.2 = (f32[128]{0:T(128)S(1)}, f32[128]{0:T(128)S(1)}, f32[512]{0:T(512)S(1)}, f32[512]{0:T(512)S(1)}, f32[128]{0:T(128)S(1)}, /*index=5*/...) fusion(bf16[512,1,128]{2,0,1:T(8,128)(2,1)S(1)} %get-tuple-element.45, f32[512]{0:T(512)S(1)} %get-tuple-element.91, ...), kind=kLoop, calls=%fused_computation.79 | loop fusion | flops 2488832 | bytes 2381184 | tf_op jit(solution)/shard_map/reduce_sum | solution.py:110
  43.5 0.4 fusion.55
  44.0 0.7 copy.60
  44.7 3.3 %all-to-all-start.3 = ((bf16[1,64,4,128]{3,2,0,1:T(4,128)(2,1)}), bf16[1,64,4,128]{3,2,0,1:T(4,128)(2,1)S(1)}, u32[]{:S(2)}, u32[]{:S(2)}) async-start(bf16[1,64,4,128]{3,2,0,1:T(4,128)(2,1)} %copy.60), calls=%async_computation.3 | async-start | bytes 131072 | tf_op jit(solution)/shard_map/all_to_all | solution.py:155
  48.0 1.1 %copy.58 = bf16[1,448,4,128]{3,2,0,1:T(4,128)(2,1)} copy(bf16[1,448,4,128]{3,1,2,0:T(8,128)(2,1)S(1)} %slice_bitcast_fusion) | data formatting | bytes 917504 | tf_op jit(solution)/shard_map/broadcast_in_dim | solution.py:152
  49.1 4.5 %all-to-all-done.3 = bf16[1,64,4,128]{3,2,0,1:T(4,128)(2,1)S(1)} async-done(((bf16[1,64,4,128]{3,2,0,1:T(4,128)(2,1)}), bf16[1,64,4,128]{3,2,0,1:T(4,128)(2,1)S(1)}, u32[]{:S(2)}, u32[]{:S(2)}) %all-to-all-start.3) | async-done | bytes 65568 | tf_op jit(solution)/shard_map/all_to_all | solution.py:155
  53.7 3.5 %all-to-all-start.2 = ((bf16[1,448,4,128]{3,2,0,1:T(4,128)(2,1)}), bf16[1,448,4,128]{3,2,0,1:T(4,128)(2,1)S(1)}, u32[]{:S(2)}, u32[]{:S(2)}) async-start(bf16[1,448,4,128]{3,2,0,1:T(4,128)(2,1)} %copy.58), calls=%async_computation.2 | async-start | bytes 917504 | tf_op jit(solution)/shard_map/all_to_all | solution.py:154
  57.2 0.6 copy-done.3
  57.8 0.6 dynamic-slice.2
  59.1 12.1 %all-reduce = f32[512]{0:T(512)S(1)} all-reduce(f32[512]{0:T(512)S(1)} %fusion.84), channel_id=2, replica_groups=mesh['dp'=8,'seq'=4] {'dp'}, use_global_device_ids=true, to_apply=%region_11.12.clone | all-reduce | flops 512 | bytes 4096
  71.3 12.3 %psum.8 = f32[64]{0:T(128)} all-reduce(f32[64]{0:T(128)S(1)} %dynamic-slice.3), channel_id=1, replica_groups=mesh['dp'=8,'seq'=4] {'seq'}, use_global_device_ids=true, to_apply=%region_10.11 | all-reduce | flops 64 | bytes 512 | tf_op jit(solution)/shard_map/psum | solution.py:163
  83.7 0.6 slice.176
  84.3 0.6 slice_bitcast_fusion.5
  84.9 0.4 copy.59
  85.5 0.7 slice_bitcast_fusion.2
  86.1 0.8 slice.175
  (43 shorter events, 2.6 us)
Async XLA Ops:
  1.8 7.7 %copy-start = (bf16[1,112,3,512]{3,1,2,0:T(8,128)(2,1)S(1)}, bf16[1,112,3,512]{3,1,2,0:T(8,128)(2,1)}, u32[]{:S(2)}) copy-start(bf16[1,112,3,512]{3,1,2,0:T(8,128)(2,1)} %param.5) | copy-start | bytes 1032196
  3.0 6.5 %copy-start.1 = (bf16[1,112,512]{2,1,0:T(8,128)(2,1)S(1)}, bf16[1,112,512]{2,1,0:T(8,128)(2,1)}, u32[]{:S(2)}) copy-start(bf16[1,112,512]{2,1,0:T(8,128)(2,1)} %param.7) | copy-start | bytes 344068
  3.0 12.2 %all-to-all-start = ((bf16[4,2,4096]{2,1,0:T(2,128)(2,1)}), bf16[4,2,4096]{2,1,0:T(2,128)(2,1)S(1)}, u32[]{:S(2)}, u32[]{:S(2)}) async-start(bf16[4,2,4096]{2,1,0:T(2,128)(2,1)} %reshape.673), calls=%async_computation | async-start | bytes 131072 | tf_op jit(solution)/shard_map/all_to_all | solution.py:128
  15.2 3.6 %copy-start.2 = (f32[4,128]{1,0:T(4,128)S(1)}, f32[4,128]{1,0:T(4,128)}, u32[]{:S(2)}) copy-start(f32[4,128]{1,0:T(4,128)} %param.9) | copy-start | bytes 6148
  15.2 16.9 %all-to-all-start.1 = ((bf16[1,112,4,512]{1,2,0,3:T(4,128)(2,1)}), bf16[1,112,4,512]{1,2,0,3:T(4,128)(2,1)S(1)}, u32[]{:S(2)}, u32[]{:S(2)}) async-start(bf16[1,112,4,512]{1,2,0,3:T(4,128)(2,1)} %copy.51), calls=%async_computation.1 | async-start | bytes 1048576 | tf_op jit(solution)/shard_map/all_to_all | solution.py:127
  44.7 9.0 %all-to-all-start.3 = ((bf16[1,64,4,128]{3,2,0,1:T(4,128)(2,1)}), bf16[1,64,4,128]{3,2,0,1:T(4,128)(2,1)S(1)}, u32[]{:S(2)}, u32[]{:S(2)}) async-start(bf16[1,64,4,128]{3,2,0,1:T(4,128)(2,1)} %copy.60), calls=%async_computation.3 | async-start | bytes 131072 | tf_op jit(solution)/shard_map/all_to_all | solution.py:155
  53.7 31.3 %all-to-all-start.2 = ((bf16[1,448,4,128]{3,2,0,1:T(4,128)(2,1)}), bf16[1,448,4,128]{3,2,0,1:T(4,128)(2,1)S(1)}, u32[]{:S(2)}, u32[]{:S(2)}) async-start(bf16[1,448,4,128]{3,2,0,1:T(4,128)(2,1)} %copy.58), calls=%async_computation.2 | async-start | bytes 917504 | tf_op jit(solution)/shard_map/all_to_all | solution.py:154
  57.1 0.7 copy-start.3
where the time goes:
time: 87.5 us; the launch traced here: 86.9 us
  blocking collectives  24.5 us (28%)
  waiting for transfers between devices  21.7 us (25%)
  starting transfers between devices  16.8 us (19%)
  local copies, waits for them, and re-layouts  11.1 us (13%)
  matrix products  7.37 us (8%)
  other arithmetic  3.82 us (4%)
  between operations  1.62 us (2%)
    all_to_all x1, waiting for transfers between devices, per_device(): lax.all_to_all(img_pack, 'seq', split_axis=3, concat_axis=1, tiled=True)  12.6 us
    psum x1, blocking collectives, per_device(): summed = lax.psum(partial_grad, 'seq')  12.3 us
    unnamed x1, blocking collectives  12.1 us
    all_to_all x1, starting transfers between devices, per_device(): lax.all_to_all(txt_pack, 'seq', split_axis=3, concat_axis=1, tiled=True)  6.45 us
    all_to_all x1, waiting for transfers between devices, per_device(): lax.all_to_all(txt_pack, 'seq', split_axis=3, concat_axis=1, tiled=True)  4.55 us
    all_to_all x1, waiting for transfers between devices, per_device(): lax.all_to_all(txt_back, 'seq', split_axis=1, concat_axis=3, tiled=True)  4.54 us
    all_to_all x1, starting transfers between devices, per_device(): lax.all_to_all(img_pack, 'seq', split_axis=3, concat_axis=1, tiled=True)  3.6 us
    all_to_all x1, starting transfers between devices, per_device(): lax.all_to_all(img_back, 'seq', split_axis=1, concat_axis=3, tiled=True)  3.46 us
  transfers between devices with their start and end apart: 4, of which 3 were waited for; matrix products, arithmetic and copies ran while one was open for 6% of the time, Pallas kernels for 0%

commit v1 on v0

v1 whole, which is shorter than its diff:
```python
import functools
import math

import jax
import jax.numpy as jnp
import numpy as np
from jax import lax
from jax.experimental import pallas as pl
from jax.experimental.pallas import tpu as pltpu
from jax.sharding import PartitionSpec as P

HD = 128
GRID_W = 64
EPSILON = 1e-06
LOG2_E = math.log2(math.e)
VMEM_LIMIT = 56 * 1024 * 1024
HBM = pl.BlockSpec(memory_space=pl.ANY)
VMEM = pl.BlockSpec(memory_space=pltpu.VMEM)


def rope_tables(n, txt_rows, img_rows):
    image = np.arange(n * img_rows).reshape(n, img_rows)
    time_dims = HD // 8
    axis_dims = (HD - time_dims) // 2
    channel = np.arange(HD)
    in_rows = (channel >= time_dims) & (channel < time_dims + axis_dims)
    in_cols = channel >= time_dims + axis_dims
    within = np.where(in_cols, channel - time_dims - axis_dims, channel - time_dims)
    within = np.maximum(within, 0) // 2
    frequency = np.power(10000.0, -2.0 * within / axis_dims).astype(np.float32)
    row_pos = (image // GRID_W).astype(np.float32)[..., None]
    col_pos = (image % GRID_W).astype(np.float32)[..., None]
    angles = np.where(in_rows, row_pos * frequency, np.float32(0.0))
    angles = np.where(in_cols, col_pos * frequency, angles)
    angles = np.concatenate([np.zeros((n, txt_rows, HD), np.float32), angles], axis=1)
    angles = angles.reshape(n * (txt_rows + img_rows), HD).astype(np.float64)
    sign = np.where(channel % 2 == 0, -1.0, 1.0)
    return np.cos(angles).astype(np.float32), (np.sin(angles) * sign).astype(np.float32)


def run_copies(copies):
    for copy in copies:
        copy.start()
    for copy in copies:
        copy.wait()


def pack_kernel(n, iq, tq, ic, tc, *refs):
    outs, sems = refs[:n], refs[n]
    txt_rows = tc.shape[1]
    rows = txt_rows + ic.shape[1]
    me = lax.axis_index("seq")
    copies = []
    for step in range(n):
        head = lax.rem(me + step, n)
        cols = pl.ds(pl.multiple_of(head * HD, HD), HD)
        out = outs[step]
        pairs = (
            (tq.at[0, :, :, cols], out.at[0:3, 0:txt_rows]),
            (iq.at[0, :, :, cols], out.at[0:3, txt_rows:rows]),
            (tc.at[0, :, cols], out.at[3, 0:txt_rows]),
            (ic.at[0, :, cols], out.at[3, txt_rows:rows]),
        )
        for i, (src, dst) in enumerate(pairs):
            copies.append(pltpu.make_async_copy(src, dst, sems.at[step, i]))
    run_copies(copies)


def unpack_kernel(n, *refs):
    ins = refs[:n]
    pieces, io, to, ig, tg, gain, sems = refs[n:]
    txt_rows = to.shape[1]
    rows = txt_rows + io.shape[1]
    me = lax.axis_index("seq")
    copies = []
    for step in range(n):
        head = lax.rem(me + step, n)
        cols = pl.ds(pl.multiple_of(head * HD, HD), HD)
        src = ins[step]
        pairs = (
            (src.at[0:3, 0:txt_rows], tg.at[0, :, :, cols]),
            (src.at[0:3, txt_rows:rows], ig.at[0, :, :, cols]),
            (src.at[3, 0:txt_rows], to.at[0, :, cols]),
            (src.at[3, txt_rows:rows], io.at[0, :, cols]),
        )
        for i, (a, b) in enumerate(pairs):
            copies.append(pltpu.make_async_copy(a, b, sems.at[step, i]))
    for copy in copies:
        copy.start()
    gain[...] = jnp.sum(pieces[...], axis=0, keepdims=True)
    for copy in copies:
        copy.wait()


def attend_kernel(n, txt_rows, per, grad_scale, block_rows, *refs):
    ins = refs[:n]
    cos_ref, sin_ref, gains_ref = refs[n : n + 3]
    outs = refs[n + 3 : 2 * n + 3]
    gain_out = refs[2 * n + 3]
    q_rot, k_rot, val, cot, q_hat, k_hat, dq_acc, dk_acc, dv_acc = refs[2 * n + 4 :]
    rows = ins[0].shape[1]
    seq_len = n * rows
    scale = 1.0 / math.sqrt(HD)
    me = lax.axis_index("seq")
    lane = lax.broadcasted_iota(jnp.int32, (rows, HD), 1)
    even = lane % 2 == 0
    is_txt = lax.broadcasted_iota(jnp.int32, (rows, HD), 0) < txt_rows
    gains = gains_ref[...]
    q_gain = jnp.where(is_txt, gains[2:3], gains[0:1])
    k_gain = jnp.where(is_txt, gains[3:4], gains[1:2])
    last = (((1,), (1,)), ((), ()))
    first = (((0,), (0,)), ((), ()))

    def swap(x):
        return jnp.where(even, pltpu.roll(x, HD - 1, 1), pltpu.roll(x, 1, 1))

    def table(step):
        owner = lax.rem(me + (n - step), n)
        at = pl.ds(pl.multiple_of(owner * rows, rows), rows)
        return cos_ref[at, :], sin_ref[at, :]

    inverse = []
    for step in range(n):
        cos, sin = table(step)
        at = slice(step * rows, (step + 1) * rows)
        pair = []
        for slot, gain, hat, rot in ((0, q_gain, q_hat, q_rot), (1, k_gain, k_hat, k_rot)):
            raw = ins[step][slot].astype(jnp.float32)
            inv = lax.rsqrt(jnp.mean(raw * raw, axis=1, keepdims=True) + EPSILON)
            norm = raw * inv
            hat[at] = norm
            norm = norm * gain
            rot[at] = (norm * cos + swap(norm) * sin).astype(jnp.bfloat16)
            pair.append(inv)
        inverse.append(pair)
        val[at] = ins[step][2]
        cot[at] = ins[step][3]

    def block(i, first_block):
        at = pl.ds(pl.multiple_of(i * block_rows, block_rows), block_rows)
        q_b, g_b = q_rot[at, :], cot[at, :]
        k, v = k_rot[...], val[...]
        s = lax.dot_general(q_b, k, last, preferred_element_type=jnp.float32)
        e = jnp.exp2(s * (scale * LOG2_E))
        r = 1.0 / jnp.sum(e, axis=1, keepdims=True)
        p = e * r
        pb = p.astype(jnp.bfloat16)
        o = jnp.dot(pb, v, preferred_element_type=jnp.float32).astype(jnp.bfloat16)
        delta = jnp.sum(g_b.astype(jnp.float32) * o.astype(jnp.float32), axis=1, keepdims=True)
        dp = lax.dot_general(g_b, v, last, preferred_element_type=jnp.float32)
        ds = (p * (dp - delta) * scale).astype(jnp.bfloat16)
        dv = lax.dot_general(pb, g_b, first, preferred_element_type=jnp.float32)
        dq_acc[at, :] = jnp.dot(ds, k, preferred_element_type=jnp.float32)
        dk = lax.dot_general(ds, q_b, first, preferred_element_type=jnp.float32)
        if first_block:
            dv_acc[...] = dv
            dk_acc[...] = dk
        else:
            dv_acc[...] += dv
            dk_acc[...] += dk
        return o

    n_blocks = seq_len // block_rows
    assert block_rows % rows == 0
    per_block = block_rows // rows
    for i in range(n_blocks):
        o = block(i, i == 0)
        for j in range(per_block):
            outs[i * per_block + j][3] = o[j * rows : (j + 1) * rows]

    sums = [jnp.zeros((1, HD), jnp.float32) for _ in range(4)]
    for step in range(n):
        cos, sin = table(step)
        at = slice(step * rows, (step + 1) * rows)
        outs[step][2] = dv_acc[at].astype(jnp.bfloat16)
        for slot, gain, hat_ref, acc in ((0, q_gain, q_hat, dq_acc), (1, k_gain, k_hat, dk_acc)):
            rot_grad = acc[at]
            hat = hat_ref[at]
            inv = inverse[step][slot]
            grad = rot_grad * cos - swap(rot_grad) * sin
            both = grad * hat
            sums[slot] += jnp.sum(both[txt_rows:], axis=0, keepdims=True)
            sums[2 + slot] += jnp.sum(both[:txt_rows], axis=0, keepdims=True)
            middle = jnp.mean(both * gain, axis=1, keepdims=True)
            outs[step][slot] = ((grad * gain - hat * middle) * inv).astype(jnp.bfloat16)

    groups = 4 * HD // per
    for i in range(groups):
        row, off = (i * per) // HD, (i * per) % HD
        piece = sums[row] * grad_scale
        if off:
            piece = pltpu.roll(piece, HD - off, 1)
        gain_out[i * n : (i + 1) * n, :] = jnp.broadcast_to(piece, (n, HD))


def per_device(img_qkv, txt_qkv, img_cot, txt_cot, norm_gains):
    n = lax.axis_size("seq")
    dp = lax.axis_size("dp")
    img_rows, txt_rows = img_cot.shape[1], txt_cot.shape[1]
    width = img_cot.shape[2]
    rows = img_rows + txt_rows
    seq_len = n * rows
    per = 4 * HD // dp
    bf16, f32 = jnp.bfloat16, jnp.float32
    params = pltpu.CompilerParams(vmem_limit_bytes=VMEM_LIMIT)
    block = jax.ShapeDtypeStruct((4, rows, HD), bf16)

    packed = pl.pallas_call(
        functools.partial(pack_kernel, n),
        out_shape=[block] * n,
        in_specs=[HBM] * 4,
        out_specs=[HBM] * n,
        scratch_shapes=[pltpu.SemaphoreType.DMA((n, 4))],
        compiler_params=params,
        name="pack_heads",
    )(jnp.swapaxes(img_qkv, 1, 2), jnp.swapaxes(txt_qkv, 1, 2), img_cot, txt_cot)

    blocks = [packed[0]] + [
        lax.ppermute(packed[d], "seq", [(i, (i + d) % n) for i in range(n)]) for d in range(1, n)
    ]

    cos, sin = rope_tables(n, txt_rows, img_rows)
    grad_scale = 1.0 / math.sqrt(dp * seq_len * (width // HD))
    block_rows = min(seq_len, 512)
    results = pl.pallas_call(
        functools.partial(attend_kernel, n, txt_rows, per, grad_scale, block_rows),
        out_shape=[block] * n + [jax.ShapeDtypeStruct((dp * n, HD), f32)],
        in_specs=[VMEM] * (n + 3),
        out_specs=[VMEM] * (n + 1),
        scratch_shapes=[pltpu.VMEM((seq_len, HD), bf16)] * 4
        + [pltpu.VMEM((seq_len, HD), f32)] * 5,
        compiler_params=params,
        name="attend",
    )(*blocks, jnp.asarray(cos), jnp.asarray(sin), norm_gains)

    back = [results[0]] + [
        lax.ppermute(results[d], "seq", [(i, (i - d) % n) for i in range(n)]) for d in range(1, n)
    ]
    pieces = lax.all_to_all(results[n], ("dp", "seq"), 0, 0, tiled=True)

    io, to, ig, tg, gain = pl.pallas_call(
        functools.partial(unpack_kernel, n),
        out_shape=[
            jax.ShapeDtypeStruct((1, img_rows, width), bf16),
            jax.ShapeDtypeStruct((1, txt_rows, width), bf16),
            jax.ShapeDtypeStruct((1, 3, img_rows, width), bf16),
            jax.ShapeDtypeStruct((1, 3, txt_rows, width), bf16),
            jax.ShapeDtypeStruct((1, HD), f32),
        ],
        in_specs=[HBM] * n + [VMEM],
        out_specs=[HBM] * 4 + [VMEM],
        scratch_shapes=[pltpu.SemaphoreType.DMA((n, 4))],
        compiler_params=params,
        name="unpack_heads",
    )(*back, pieces)
    return io, to, jnp.swapaxes(ig, 1, 2), jnp.swapaxes(tg, 1, 2), gain[0, :per]


def solution(mesh):
    in_specs = (
        P("dp", "seq", None, None),
        P("dp", "seq", None, None),
        P("dp", "seq", None),
        P("dp", "seq", None),
        P(),
    )
    out_specs = (
        P("dp", "seq", None),
        P("dp", "seq", None),
        P("dp", "seq", None, None),
        P("dp", "seq", None, None),
        P("dp"),
    )
    return jax.shard_map(
        per_device, mesh=mesh, in_specs=in_specs, out_specs=out_specs, check_vma=False
    )
```

time: 87.5 us -> 77.5 us (0.89)
  Pallas kernels: 0 us -> 40.5 us
  waiting for transfers between devices: 21.7 us -> 7.51 us
  blocking collectives: 24.5 us -> 14 us
  local copies, waits for them, and re-layouts: 11.1 us -> 2.57 us
  matrix products: 7.37 us -> 0 us
  starting transfers between devices: 16.8 us -> 11.9 us
  other arithmetic: 3.82 us -> 0 us
  between operations: 1.62 us -> 0.7 us
    pallas_call x0 -> x3, Pallas kernels: none -> 40.5 us  [the longest x1 18.4 us: per_device(): pl.pallas_call(functools.partial(unpack_kernel, n), out_shape=[jax.ShapeD...]
    all_to_all x4 -> x0, waiting for transfers between devices: 21.7 us -> none  [the longest x1 12.6 us: per_device(): lax.all_to_all(img_pack, 'seq', split_axis=3, concat_axis=1, tiled=True)]
    all_to_all x4 -> x0, starting transfers between devices: 16.8 us -> none  [the longest x1 6.45 us: per_device(): lax.all_to_all(txt_pack, 'seq', split_axis=3, concat_axis=1, tiled=True)]
    all_to_all x0 -> x1, blocking collectives: none -> 14 us  [per_device(): pieces = lax.all_to_all(results[n], ('dp', 'seq'), 0, 0, tiled=True)]
    psum x1 -> x0, blocking collectives: 12.3 us -> none  [per_device(): summed = lax.psum(partial_grad, 'seq')]
    unnamed x1 -> x0, blocking collectives: 12.1 us -> none
    ppermute x0 -> x6, starting transfers between devices: none -> 11.9 us  [the longest x3 7.01 us: per_device(): lax.ppermute(packed[d], 'seq', [(i, (i + d) % n) for i in range(n)])]
    ppermute x0 -> x6, waiting for transfers between devices: none -> 7.51 us  [the longest x3 7.5 us: per_device(): lax.ppermute(packed[d], 'seq', [(i, (i + d) % n) for i in range(n)])]
  transfers between devices with their start and end apart: 4 -> 6, of which waited for: 3 -> 2; matrix products, arithmetic and copies ran while one was open for 6% -> 0% of each run, Pallas kernels for 0% -> 0%
where the time goes in v1:
time: 77.5 us; the launch traced here: 77.2 us
  Pallas kernels  40.5 us (52%)
  blocking collectives  14 us (18%)
  starting transfers between devices  11.9 us (15%)
  waiting for transfers between devices  7.51 us (10%)
  local copies, waits for them, and re-layouts  2.57 us (3%)
    pallas_call x1, Pallas kernels, per_device(): pl.pallas_call(functools.partial(unpack_kernel, n), out_shape=[jax.ShapeD...  18.4 us
    pallas_call x1, Pallas kernels, per_device(): pl.pallas_call(functools.partial(pack_kernel, n), out_shape=[block] * n,...  17.1 us
    all_to_all x1, blocking collectives, per_device(): pieces = lax.all_to_all(results[n], ('dp', 'seq'), 0, 0, tiled=True)  14 us
    ppermute x3, waiting for transfers between devices, per_device(): lax.ppermute(packed[d], 'seq', [(i, (i + d) % n) for i in range(n)])  7.5 us
    ppermute x3, starting transfers between devices, per_device(): lax.ppermute(packed[d], 'seq', [(i, (i + d) % n) for i in range(n)])  7.01 us
    pallas_call x1, Pallas kernels, per_device(): pl.pallas_call(functools.partial(attend_kernel, n, txt_rows, per, grad_sc...  4.97 us
    ppermute x3, starting transfers between devices, per_device(): lax.ppermute(results[d], 'seq', [(i, (i - d) % n) for i in range(n)])  4.91 us
    unnamed x14, local copies, waits for them, and re-layouts  2.06 us
  transfers between devices with their start and end apart: 6, of which 2 were waited for; matrix products, arithmetic and copies ran while one was open for 0% of the time, Pallas kernels for 0%

profile of v1, /device:TPU:0, one launch (start us, length us, event | category | flops | bytes accessed | tf_op | source)
XLA Modules:
  0.0 77.2 jit_solution(6385594320685696873)
XLA Ops:
  0.6 17.1 %pack_heads.1 = (bf16[4,128,128]{2,1,0:T(8,128)(2,1)}, bf16[4,128,128]{2,1,0:T(8,128)(2,1)}, bf16[4,128,128]{2,1,0:T(8,128)(2,1)}, bf16[4,128,128]{2,1,0:T(8,128)(2,1)}) custom-call(bf16[1,3,112,512]{3,2,1,0:T(8,128)(2,1)} %bitcast.10, bf16[1,3,16,512]{3,2,1,0:T(8,128)(2,1)} %bitcast.12, bf16[1,112,512]{2,1,0:T(8,128)(2,1)} %ic.1, bf16[1,16,512]{2,1,0:T(8,128)(2,1)} %tc.1), custom_call_target="tpu_custom_call" | custom-call | tf_op jit(solution)/shard_map/pack_heads/pallas_call | solution.py:208
  17.8 3.1 %collective-permute-start = (bf16[4,128,128]{2,1,0:T(8,128)(2,1)}, bf16[4,128,128]{2,1,0:T(8,128)(2,1)S(1)}, u32[]{:S(2)}, u32[]{:S(2)}) collective-permute-start(bf16[4,128,128]{2,1,0:T(8,128)(2,1)} %get-tuple-element.20), channel_id=1, source_target_pairs={{0,1},{1,2},{2,3},{3,0},{4,5},{5,6},{6,7},{7,4},{8,9},{9,10},{10,1... | collective-permute-start | bytes 393224 | tf_op jit(solution)/shard_map/ppermute | solution.py:219
  20.9 2.6 %collective-permute-start.1 = (bf16[4,128,128]{2,1,0:T(8,128)(2,1)}, bf16[4,128,128]{2,1,0:T(8,128)(2,1)S(1)}, u32[]{:S(2)}, u32[]{:S(2)}) collective-permute-start(bf16[4,128,128]{2,1,0:T(8,128)(2,1)} %get-tuple-element.21), channel_id=1, source_target_pairs={{0,2},{1,3},{2,0},{3,1},{4,6},{5,7},{6,4},{7,5},{8,10},{9,11},{10,... | collective-permute-start | bytes 393224 | tf_op jit(solution)/shard_map/ppermute | solution.py:219
  23.4 1.3 %collective-permute-start.2 = (bf16[4,128,128]{2,1,0:T(8,128)(2,1)}, bf16[4,128,128]{2,1,0:T(8,128)(2,1)S(1)}, u32[]{:S(2)}, u32[]{:S(2)}) collective-permute-start(bf16[4,128,128]{2,1,0:T(8,128)(2,1)} %get-tuple-element.22), channel_id=1, source_target_pairs={{0,3},{1,0},{2,1},{3,2},{4,7},{5,4},{6,5},{7,6},{8,11},{9,8},{10,9... | collective-permute-start | bytes 393224 | tf_op jit(solution)/shard_map/ppermute | solution.py:219
  24.8 2.7 %collective-permute-done.refs_1_ = bf16[4,128,128]{2,1,0:T(8,128)(2,1)S(1)} collective-permute-done((bf16[4,128,128]{2,1,0:T(8,128)(2,1)}, bf16[4,128,128]{2,1,0:T(8,128)(2,1)S(1)}, u32[]{:S(2)}, u32[]{:S(2)}) %collective-permute-start) | collective-permute-done | bytes 131104 | tf_op jit(solution)/shard_map/ppermute | solution.py:219
  27.5 0.0 copy-start.3
  27.5 4.8 %collective-permute-done.1.refs_2_ = bf16[4,128,128]{2,1,0:T(8,128)(2,1)S(1)} collective-permute-done((bf16[4,128,128]{2,1,0:T(8,128)(2,1)}, bf16[4,128,128]{2,1,0:T(8,128)(2,1)S(1)}, u32[]{:S(2)}, u32[]{:S(2)}) %collective-permute-start.1) | collective-permute-done | bytes 131104 | tf_op jit(solution)/shard_map/ppermute | solution.py:219
  32.3 0.0 copy-start.4
  32.3 0.0 collective-permute-done.2.refs_3_
  32.3 0.0 copy-start.5
  32.3 0.0 copy-done.3
  32.3 0.6 copy-done.4
  33.0 0.1 copy-done.5
  33.0 5.0 %attend.1 = (bf16[4,128,128]{2,1,0:T(8,128)(2,1)}, bf16[4,128,128]{2,1,0:T(8,128)(2,1)}, bf16[4,128,128]{2,1,0:T(8,128)(2,1)}, bf16[4,128,128]{2,1,0:T(8,128)(2,1)}, f32[32,128]{1,0:T(8,128)}) custom-call(bf16[4,128,128]{2,1,0:T(8,128)(2,1)} %get-tuple-element.19.refs_0_, bf16[4,128,128]{2,1,0:T(8,128)(2,1)} %copy-done.3, bf16[4,128,128]{2,1,0:T(8,128)(2,1)} %copy-done.4, ...), custom_call_target="tpu_custom_call" | custom-call | tf_op jit(solution)/shard_map/attend/pallas_call | solution.py:225
  38.0 4.3 %collective-permute-start.3 = (bf16[4,128,128]{2,1,0:T(8,128)(2,1)}, bf16[4,128,128]{2,1,0:T(8,128)(2,1)S(1)}, u32[]{:S(2)}, u32[]{:S(2)}) collective-permute-start(bf16[4,128,128]{2,1,0:T(8,128)(2,1)} %get-tuple-element.24), channel_id=1, source_target_pairs={{0,3},{1,0},{2,1},{3,2},{4,7},{5,4},{6,5},{7,6},{8,11},{9,8},{10,9... | collective-permute-start | bytes 393224 | tf_op jit(solution)/shard_map/ppermute | solution.py:237
  42.3 0.3 collective-permute-start.4
  42.7 0.2 collective-permute-start.5
  42.9 14.0 %all_to_all.11 = f32[32,1,128]{2,1,0:T(1,128)} all-to-all(f32[32,1,128]{2,1,0:T(1,128)} %bitcast.13), channel_id=1, replica_groups=mesh['dp'=8,'seq'=4] {'dp','seq'}, dimensions={0} | all-to-all | bytes 32768 | tf_op jit(solution)/shard_map/all_to_all | solution.py:239
  56.9 0.0 collective-permute-done.3.refs_1_
  56.9 0.0 copy-start
  56.9 0.0 collective-permute-done.4.refs_2_
  56.9 0.0 copy-start.1
  56.9 0.0 collective-permute-done.5.refs_3_
  57.0 0.0 copy-start.2
  57.0 0.6 copy-done
  57.6 0.1 copy-done.1
  57.6 0.0 copy-done.2
  57.7 18.4 %unpack_heads.1 = (bf16[1,112,512]{2,1,0:T(8,128)(2,1)}, bf16[1,16,512]{2,1,0:T(8,128)(2,1)}, bf16[1,3,112,512]{3,2,1,0:T(8,128)(2,1)}, bf16[1,3,16,512]{3,2,1,0:T(8,128)(2,1)}, f32[1,128]{1,0:T(1,128)}) custom-call(bf16[4,128,128]{2,1,0:T(8,128)(2,1)} %get-tuple-element.23.refs_0_, bf16[4,128,128]{2,1,0:T(8,128)(2,1)} %copy-done, ...), custom_call_target="tpu_custom_call" | custom-call | tf_op jit(solution)/shard_map/unpack_heads/pallas_call | solution.py:241
  76.0 0.0 copy-start.6
  76.0 0.6 copy-done.6
  76.7 0.5 slice_bitcast_fusion
Async XLA Ops:
  17.8 9.7 %collective-permute-start = (bf16[4,128,128]{2,1,0:T(8,128)(2,1)}, bf16[4,128,128]{2,1,0:T(8,128)(2,1)S(1)}, u32[]{:S(2)}, u32[]{:S(2)}) collective-permute-start(bf16[4,128,128]{2,1,0:T(8,128)(2,1)} %get-tuple-element.20), channel_id=1, source_target_pairs={{0,1},{1,2},{2,3},{3,0},{4,5},{5,6},{6,7},{7,4},{8,9},{9,10},{10,1... | collective-permute-start | bytes 393224 | tf_op jit(solution)/shard_map/ppermute | solution.py:219
  20.9 11.4 %collective-permute-start.1 = (bf16[4,128,128]{2,1,0:T(8,128)(2,1)}, bf16[4,128,128]{2,1,0:T(8,128)(2,1)S(1)}, u32[]{:S(2)}, u32[]{:S(2)}) collective-permute-start(bf16[4,128,128]{2,1,0:T(8,128)(2,1)} %get-tuple-element.21), channel_id=1, source_target_pairs={{0,2},{1,3},{2,0},{3,1},{4,6},{5,7},{6,4},{7,5},{8,10},{9,11},{10,... | collective-permute-start | bytes 393224 | tf_op jit(solution)/shard_map/ppermute | solution.py:219
  23.4 8.9 %collective-permute-start.2 = (bf16[4,128,128]{2,1,0:T(8,128)(2,1)}, bf16[4,128,128]{2,1,0:T(8,128)(2,1)S(1)}, u32[]{:S(2)}, u32[]{:S(2)}) collective-permute-start(bf16[4,128,128]{2,1,0:T(8,128)(2,1)} %get-tuple-element.22), channel_id=1, source_target_pairs={{0,3},{1,0},{2,1},{3,2},{4,7},{5,4},{6,5},{7,6},{8,11},{9,8},{10,9... | collective-permute-start | bytes 393224 | tf_op jit(solution)/shard_map/ppermute | solution.py:219
  27.5 4.8 %copy-start.3 = (bf16[4,128,128]{2,1,0:T(8,128)(2,1)}, bf16[4,128,128]{2,1,0:T(8,128)(2,1)S(1)}, u32[]{:S(2)}) copy-start(bf16[4,128,128]{2,1,0:T(8,128)(2,1)S(1)} %collective-permute-done.refs_1_) | copy-start | bytes 393220
  32.3 0.6 copy-start.4
  32.3 0.7 copy-start.5
  38.0 18.9 %collective-permute-start.3 = (bf16[4,128,128]{2,1,0:T(8,128)(2,1)}, bf16[4,128,128]{2,1,0:T(8,128)(2,1)S(1)}, u32[]{:S(2)}, u32[]{:S(2)}) collective-permute-start(bf16[4,128,128]{2,1,0:T(8,128)(2,1)} %get-tuple-element.24), channel_id=1, source_target_pairs={{0,3},{1,0},{2,1},{3,2},{4,7},{5,4},{6,5},{7,6},{8,11},{9,8},{10,9... | collective-permute-start | bytes 393224 | tf_op jit(solution)/shard_map/ppermute | solution.py:237
  42.3 14.6 %collective-permute-start.4 = (bf16[4,128,128]{2,1,0:T(8,128)(2,1)}, bf16[4,128,128]{2,1,0:T(8,128)(2,1)S(1)}, u32[]{:S(2)}, u32[]{:S(2)}) collective-permute-start(bf16[4,128,128]{2,1,0:T(8,128)(2,1)} %get-tuple-element.25), channel_id=1, source_target_pairs={{0,2},{1,3},{2,0},{3,1},{4,6},{5,7},{6,4},{7,5},{8,10},{9,11},{10,... | collective-permute-start | bytes 393224 | tf_op jit(solution)/shard_map/ppermute | solution.py:237
  42.7 14.3 %collective-permute-start.5 = (bf16[4,128,128]{2,1,0:T(8,128)(2,1)}, bf16[4,128,128]{2,1,0:T(8,128)(2,1)S(1)}, u32[]{:S(2)}, u32[]{:S(2)}) collective-permute-start(bf16[4,128,128]{2,1,0:T(8,128)(2,1)} %get-tuple-element.26), channel_id=1, source_target_pairs={{0,1},{1,2},{2,3},{3,0},{4,5},{5,6},{6,7},{7,4},{8,9},{9,10},{10,1... | collective-permute-start | bytes 393224 | tf_op jit(solution)/shard_map/ppermute | solution.py:237
  56.9 0.7 copy-start
  56.9 0.7 copy-start.1
  57.0 0.7 copy-start.2
  76.0 0.7 copy-start.6

commit v2 on v1

--- a/solution.py
+++ b/solution.py
@@ -13,8 +13,7 @@
 GRID_W = 64
 EPSILON = 1e-06
 LOG2_E = math.log2(math.e)
-VMEM_LIMIT = 56 * 1024 * 1024
-HBM = pl.BlockSpec(memory_space=pl.ANY)
+MIB = 1024 * 1024
 VMEM = pl.BlockSpec(memory_space=pltpu.VMEM)
 
 
@@ -38,58 +37,44 @@
     return np.cos(angles).astype(np.float32), (np.sin(angles) * sign).astype(np.float32)
 
 
-def run_copies(copies):
+def pack_kernel(n, iq, tq, ic, tc, *refs):
+    outs = refs[:n]
+    held, sems = refs[n:-1], refs[-1]
+    txt_rows = tc.shape[1]
+    me = lax.axis_index("seq")
+    copies = [
+        pltpu.make_async_copy(src, dst, sems.at[i])
+        for i, (src, dst) in enumerate(zip((iq, tq, ic, tc), held))
+    ]
     for copy in copies:
         copy.start()
     for copy in copies:
         copy.wait()
-
-
-def pack_kernel(n, iq, tq, ic, tc, *refs):
-    outs, sems = refs[:n], refs[n]
-    txt_rows = tc.shape[1]
-    rows = txt_rows + ic.shape[1]
-    me = lax.axis_index("seq")
-    copies = []
+    iq, tq, ic, tc = held
     for step in range(n):
         head = lax.rem(me + step, n)
         cols = pl.ds(pl.multiple_of(head * HD, HD), HD)
         out = outs[step]
-        pairs = (
-            (tq.at[0, :, :, cols], out.at[0:3, 0:txt_rows]),
-            (iq.at[0, :, :, cols], out.at[0:3, txt_rows:rows]),
-            (tc.at[0, :, cols], out.at[3, 0:txt_rows]),
-            (ic.at[0, :, cols], out.at[3, txt_rows:rows]),
-        )
-        for i, (src, dst) in enumerate(pairs):
-            copies.append(pltpu.make_async_copy(src, dst, sems.at[step, i]))
-    run_copies(copies)
+        out[0:3, :txt_rows] = tq[0, :, :, cols]
+        out[0:3, txt_rows:] = iq[0, :, :, cols]
+        out[3, :txt_rows] = tc[0, :, cols]
+        out[3, txt_rows:] = ic[0, :, cols]
 
 
 def unpack_kernel(n, *refs):
     ins = refs[:n]
-    pieces, io, to, ig, tg, gain, sems = refs[n:]
+    pieces, io, to, ig, tg, gain = refs[n:]
     txt_rows = to.shape[1]
-    rows = txt_rows + io.shape[1]
     me = lax.axis_index("seq")
-    copies = []
+    gain[...] = jnp.sum(pieces[...], axis=0, keepdims=True)[:, : gain.shape[1]]
     for step in range(n):
         head = lax.rem(me + step, n)
         cols = pl.ds(pl.multiple_of(head * HD, HD), HD)
         src = ins[step]
-        pairs = (
-            (src.at[0:3, 0:txt_rows], tg.at[0, :, :, cols]),
-            (src.at[0:3, txt_rows:rows], ig.at[0, :, :, cols]),
-            (src.at[3, 0:txt_rows], to.at[0, :, cols]),
-            (src.at[3, txt_rows:rows], io.at[0, :, cols]),
-        )
-        for i, (a, b) in enumerate(pairs):
-            copies.append(pltpu.make_async_copy(a, b, sems.at[step, i]))
-    for copy in copies:
-        copy.start()
-    gain[...] = jnp.sum(pieces[...], axis=0, keepdims=True)
-    for copy in copies:
-        copy.wait()
+        tg[0, :, :, cols] = src[0:3, :txt_rows]
+        ig[0, :, :, cols] = src[0:3, txt_rows:]
+        to[0, :, cols] = src[3, :txt_rows]
+        io[0, :, cols] = src[3, txt_rows:]
 
 
 def attend_kernel(n, txt_rows, per, grad_scale, block_rows, *refs):
@@ -202,18 +187,20 @@
     seq_len = n * rows
     per = 4 * HD // dp
     bf16, f32 = jnp.bfloat16, jnp.float32
-    params = pltpu.CompilerParams(vmem_limit_bytes=VMEM_LIMIT)
+    block_rows = min(seq_len, 512)
+    params = pltpu.CompilerParams(vmem_limit_bytes=8 * MIB + 32 * block_rows * seq_len)
     block = jax.ShapeDtypeStruct((4, rows, HD), bf16)
 
+    parts = (jnp.swapaxes(img_qkv, 1, 2), jnp.swapaxes(txt_qkv, 1, 2), img_cot, txt_cot)
     packed = pl.pallas_call(
         functools.partial(pack_kernel, n),
         out_shape=[block] * n,
-        in_specs=[HBM] * 4,
-        out_specs=[HBM] * n,
-        scratch_shapes=[pltpu.SemaphoreType.DMA((n, 4))],
+        in_specs=[pl.BlockSpec(memory_space=pltpu.HBM)] * 4,
+        out_specs=[VMEM] * n,
+        scratch_shapes=[pltpu.VMEM(x.shape, bf16) for x in parts] + [pltpu.SemaphoreType.DMA((4,))],
         compiler_params=params,
         name="pack_heads",
-    )(jnp.swapaxes(img_qkv, 1, 2), jnp.swapaxes(txt_qkv, 1, 2), img_cot, txt_cot)
+    )(*(pltpu.with_memory_space_constraint(x, pltpu.HBM) for x in parts))
 
     blocks = [packed[0]] + [
         lax.ppermute(packed[d], "seq", [(i, (i + d) % n) for i in range(n)]) for d in range(1, n)
@@ -221,7 +208,6 @@
 
     cos, sin = rope_tables(n, txt_rows, img_rows)
     grad_scale = 1.0 / math.sqrt(dp * seq_len * (width // HD))
-    block_rows = min(seq_len, 512)
     results = pl.pallas_call(
         functools.partial(attend_kernel, n, txt_rows, per, grad_scale, block_rows),
         out_shape=[block] * n + [jax.ShapeDtypeStruct((dp * n, HD), f32)],
@@ -245,15 +231,14 @@
             jax.ShapeDtypeStruct((1, txt_rows, width), bf16),
             jax.ShapeDtypeStruct((1, 3, img_rows, width), bf16),
             jax.ShapeDtypeStruct((1, 3, txt_rows, width), bf16),
-            jax.ShapeDtypeStruct((1, HD), f32),
+            jax.ShapeDtypeStruct((1, per), f32),
         ],
-        in_specs=[HBM] * n + [VMEM],
-        out_specs=[HBM] * 4 + [VMEM],
-        scratch_shapes=[pltpu.SemaphoreType.DMA((n, 4))],
+        in_specs=[VMEM] * (n + 1),
+        out_specs=[VMEM] * 5,
         compiler_params=params,
         name="unpack_heads",
     )(*back, pieces)
-    return io, to, jnp.swapaxes(ig, 1, 2), jnp.swapaxes(tg, 1, 2), gain[0, :per]
+    return io, to, jnp.swapaxes(ig, 1, 2), jnp.swapaxes(tg, 1, 2), gain.reshape(per)
 
 
 def solution(mesh):

time: 77.5 us -> 39.1 us (0.50)
  Pallas kernels: 40.5 us -> 5.14 us
  local copies, waits for them, and re-layouts: 2.57 us -> 0.02 us
    pallas_call x1, Pallas kernels: 18.4 us -> 0.9 us  [per_device(): pl.pallas_call(functools.partial(unpack_kernel, n), out_shape=[jax.ShapeD...]
    pallas_call x1, Pallas kernels: 17.1 us -> 1.21 us  [per_device(): pl.pallas_call(functools.partial(pack_kernel, n), out_shape=[block] * n,...]
    unnamed x14 -> x6, local copies, waits for them, and re-layouts: 2.06 us -> 0.02 us
    pallas_call x1, Pallas kernels: 4.97 us -> 3.03 us  [per_device(): pl.pallas_call(functools.partial(attend_kernel, n, txt_rows, per, grad_sc...]
where the time goes in v2:
time: 39.1 us; the launch traced here: 38.9 us
  blocking collectives  13.7 us (35%)
  starting transfers between devices  12.1 us (31%)
  waiting for transfers between devices  7.3 us (19%)
  Pallas kernels  5.14 us (13%)
  between operations  0.68 us (2%)
    all_to_all x1, blocking collectives, per_device(): pieces = lax.all_to_all(results[n], ('dp', 'seq'), 0, 0, tiled=True)  13.7 us
    ppermute x3, waiting for transfers between devices, per_device(): lax.ppermute(packed[d], 'seq', [(i, (i + d) % n) for i in range(n)])  7.29 us
    ppermute x3, starting transfers between devices, per_device(): lax.ppermute(packed[d], 'seq', [(i, (i + d) % n) for i in range(n)])  7.01 us
    ppermute x3, starting transfers between devices, per_device(): lax.ppermute(results[d], 'seq', [(i, (i - d) % n) for i in range(n)])  5.04 us
    pallas_call x1, Pallas kernels, per_device(): pl.pallas_call(functools.partial(attend_kernel, n, txt_rows, per, grad_sc...  3.03 us
    pallas_call x1, Pallas kernels, per_device(): pl.pallas_call(functools.partial(pack_kernel, n), out_shape=[block] * n,...  1.21 us
    pallas_call x1, Pallas kernels, per_device(): pl.pallas_call(functools.partial(unpack_kernel, n), out_shape=[jax.ShapeD...  0.9 us
  transfers between devices with their start and end apart: 6, of which 2 were waited for; matrix products, arithmetic and copies ran while one was open for 0% of the time, Pallas kernels for 0%

profile of v2, /device:TPU:0, one launch (start us, length us, event | category | flops | bytes accessed | tf_op | source)
XLA Modules:
  0.0 38.9 jit_solution(11873847228897647598)
XLA Ops:
  0.6 0.0 copy-start
  0.6 0.0 copy-start.1
  0.7 1.2 %pack_heads.1 = (bf16[4,128,128]{2,1,0:T(8,128)(2,1)S(1)}, bf16[4,128,128]{2,1,0:T(8,128)(2,1)S(1)}, bf16[4,128,128]{2,1,0:T(8,128)(2,1)S(1)}, bf16[4,128,128]{2,1,0:T(8,128)(2,1)S(1)}) custom-call(bf16[1,3,112,512]{3,2,1,0:T(8,128)(2,1)} %bitcast.11, bf16[1,3,16,512]{3,2,1,0:T(8,128)(2,1)} %bitcast.12, bf16[1,112,512]{2,1,0:T(8,128)(2,1)} %ic.1, ...), custom_call_target="tpu_custom_call" | custom-call | tf_op jit(solution)/shard_map/pack_heads/pallas_call | solution.py:195
  1.9 3.1 %collective-permute-start = (bf16[4,128,128]{2,1,0:T(8,128)(2,1)S(1)}, bf16[4,128,128]{2,1,0:T(8,128)(2,1)S(1)}, u32[]{:S(2)}, u32[]{:S(2)}) collective-permute-start(bf16[4,128,128]{2,1,0:T(8,128)(2,1)S(1)} %get-tuple-element.20), channel_id=1, source_target_pairs={{0,1},{1,2},{2,3},{3,0},{4,5},{5,6},{6,7},{7,4},{8,9},{9,10},{10,1... | collective-permute-start | bytes 393224 | tf_op jit(solution)/shard_map/ppermute | solution.py:206
  5.0 0.0 copy-start.2
  5.0 2.6 %collective-permute-start.1 = (bf16[4,128,128]{2,1,0:T(8,128)(2,1)S(1)}, bf16[4,128,128]{2,1,0:T(8,128)(2,1)S(1)}, u32[]{:S(2)}, u32[]{:S(2)}) collective-permute-start(bf16[4,128,128]{2,1,0:T(8,128)(2,1)S(1)} %get-tuple-element.21), channel_id=1, source_target_pairs={{0,2},{1,3},{2,0},{3,1},{4,6},{5,7},{6,4},{7,5},{8,10},{9,11},{10,... | collective-permute-start | bytes 393224 | tf_op jit(solution)/shard_map/ppermute | solution.py:206
  7.5 1.3 %collective-permute-start.2 = (bf16[4,128,128]{2,1,0:T(8,128)(2,1)S(1)}, bf16[4,128,128]{2,1,0:T(8,128)(2,1)S(1)}, u32[]{:S(2)}, u32[]{:S(2)}) collective-permute-start(bf16[4,128,128]{2,1,0:T(8,128)(2,1)S(1)} %get-tuple-element.22), channel_id=1, source_target_pairs={{0,3},{1,0},{2,1},{3,2},{4,7},{5,4},{6,5},{7,6},{8,11},{9,8},{10,9... | collective-permute-start | bytes 393224 | tf_op jit(solution)/shard_map/ppermute | solution.py:206
  8.9 2.5 %collective-permute-done.refs_1_ = bf16[4,128,128]{2,1,0:T(8,128)(2,1)S(1)} collective-permute-done((bf16[4,128,128]{2,1,0:T(8,128)(2,1)S(1)}, bf16[4,128,128]{2,1,0:T(8,128)(2,1)S(1)}, u32[]{:S(2)}, u32[]{:S(2)}) %collective-permute-start) | collective-permute-done | bytes 131104 | tf_op jit(solution)/shard_map/ppermute | solution.py:206
  11.4 4.8 %collective-permute-done.1.refs_2_ = bf16[4,128,128]{2,1,0:T(8,128)(2,1)S(1)} collective-permute-done((bf16[4,128,128]{2,1,0:T(8,128)(2,1)S(1)}, bf16[4,128,128]{2,1,0:T(8,128)(2,1)S(1)}, u32[]{:S(2)}, u32[]{:S(2)}) %collective-permute-start.1) | collective-permute-done | bytes 131104 | tf_op jit(solution)/shard_map/ppermute | solution.py:206
  16.2 0.0 collective-permute-done.2.refs_3_
  16.2 0.0 copy-done
  16.2 0.0 copy-done.1
  16.2 0.0 copy-done.2
  16.2 3.0 %attend.1 = (bf16[4,128,128]{2,1,0:T(8,128)(2,1)S(1)}, bf16[4,128,128]{2,1,0:T(8,128)(2,1)S(1)}, bf16[4,128,128]{2,1,0:T(8,128)(2,1)S(1)}, bf16[4,128,128]{2,1,0:T(8,128)(2,1)S(1)}, f32[32,128]{1,0:T(8,128)S(1)}) custom-call(bf16[4,128,128]{2,1,0:T(8,128)(2,1)S(1)} %get-tuple-element.19.refs_0_, bf16[4,128,128]{2,1,0:T(8,128)(2,1)S(1)} %collective-permute-done.refs_1_, ...), custom_call_target="tpu_custom_call" | custom-call | tf_op jit(solution)/shard_map/attend/pallas_call | solution.py:211
  19.2 4.4 %collective-permute-start.3 = (bf16[4,128,128]{2,1,0:T(8,128)(2,1)S(1)}, bf16[4,128,128]{2,1,0:T(8,128)(2,1)S(1)}, u32[]{:S(2)}, u32[]{:S(2)}) collective-permute-start(bf16[4,128,128]{2,1,0:T(8,128)(2,1)S(1)} %get-tuple-element.24), channel_id=1, source_target_pairs={{0,3},{1,0},{2,1},{3,2},{4,7},{5,4},{6,5},{7,6},{8,11},{9,8},{10,9... | collective-permute-start | bytes 393224 | tf_op jit(solution)/shard_map/ppermute | solution.py:223
  23.6 0.4 collective-permute-start.4
  24.0 0.3 collective-permute-start.5
  24.3 13.7 %all_to_all.11 = f32[32,1,128]{2,1,0:T(1,128)S(1)} all-to-all(f32[32,1,128]{2,1,0:T(1,128)S(1)} %bitcast.10), channel_id=1, replica_groups=mesh['dp'=8,'seq'=4] {'dp','seq'}, dimensions={0} | all-to-all | bytes 32768 | tf_op jit(solution)/shard_map/all_to_all | solution.py:225
  38.0 0.0 collective-permute-done.3.refs_1_
  38.0 0.0 collective-permute-done.4.refs_2_
  38.0 0.0 collective-permute-done.5.refs_3_
  38.0 0.9 %unpack_heads.1 = (bf16[1,112,512]{2,1,0:T(8,128)(2,1)}, bf16[1,16,512]{2,1,0:T(8,128)(2,1)}, bf16[1,3,112,512]{3,2,1,0:T(8,128)(2,1)}, bf16[1,3,16,512]{3,2,1,0:T(8,128)(2,1)}, f32[1,64]{1,0:T(1,128)}) custom-call(bf16[4,128,128]{2,1,0:T(8,128)(2,1)S(1)} %get-tuple-element.23.refs_0_, bf16[4,128,128]{2,1,0:T(8,128)(2,1)S(1)} %collective-permute-done.3.refs_1_, ...), custom_call_target="tpu_custom_call" | custom-call | tf_op jit(solution)/shard_map/unpack_heads/pallas_call | solution.py:227
Async XLA Ops:
  0.6 15.6 %copy-start = (f32[512,128]{1,0:T(8,128)S(1)}, f32[512,128]{1,0:T(8,128)}, u32[]{:S(2)}) copy-start(f32[512,128]{1,0:T(8,128)} %constant.5.clone.refs_5_) | copy-start | bytes 786436
  0.6 15.5 %copy-start.1 = (f32[512,128]{1,0:T(8,128)S(1)}, f32[512,128]{1,0:T(8,128)}, u32[]{:S(2)}) copy-start(f32[512,128]{1,0:T(8,128)} %constant.4.clone.refs_4_) | copy-start | bytes 786436
  1.9 9.5 %collective-permute-start = (bf16[4,128,128]{2,1,0:T(8,128)(2,1)S(1)}, bf16[4,128,128]{2,1,0:T(8,128)(2,1)S(1)}, u32[]{:S(2)}, u32[]{:S(2)}) collective-permute-start(bf16[4,128,128]{2,1,0:T(8,128)(2,1)S(1)} %get-tuple-element.20), channel_id=1, source_target_pairs={{0,1},{1,2},{2,3},{3,0},{4,5},{5,6},{6,7},{7,4},{8,9},{9,10},{10,1... | collective-permute-start | bytes 393224 | tf_op jit(solution)/shard_map/ppermute | solution.py:206
  5.0 11.2 %copy-start.2 = (f32[4,128]{1,0:T(4,128)S(1)}, f32[4,128]{1,0:T(4,128)}, u32[]{:S(2)}) copy-start(f32[4,128]{1,0:T(4,128)} %refs_6_.1) | copy-start | bytes 6148
  5.0 11.2 %collective-permute-start.1 = (bf16[4,128,128]{2,1,0:T(8,128)(2,1)S(1)}, bf16[4,128,128]{2,1,0:T(8,128)(2,1)S(1)}, u32[]{:S(2)}, u32[]{:S(2)}) collective-permute-start(bf16[4,128,128]{2,1,0:T(8,128)(2,1)S(1)} %get-tuple-element.21), channel_id=1, source_target_pairs={{0,2},{1,3},{2,0},{3,1},{4,6},{5,7},{6,4},{7,5},{8,10},{9,11},{10,... | collective-permute-start | bytes 393224 | tf_op jit(solution)/shard_map/ppermute | solution.py:206
  7.5 8.6 %collective-permute-start.2 = (bf16[4,128,128]{2,1,0:T(8,128)(2,1)S(1)}, bf16[4,128,128]{2,1,0:T(8,128)(2,1)S(1)}, u32[]{:S(2)}, u32[]{:S(2)}) collective-permute-start(bf16[4,128,128]{2,1,0:T(8,128)(2,1)S(1)} %get-tuple-element.22), channel_id=1, source_target_pairs={{0,3},{1,0},{2,1},{3,2},{4,7},{5,4},{6,5},{7,6},{8,11},{9,8},{10,9... | collective-permute-start | bytes 393224 | tf_op jit(solution)/shard_map/ppermute | solution.py:206
  19.2 18.7 %collective-permute-start.3 = (bf16[4,128,128]{2,1,0:T(8,128)(2,1)S(1)}, bf16[4,128,128]{2,1,0:T(8,128)(2,1)S(1)}, u32[]{:S(2)}, u32[]{:S(2)}) collective-permute-start(bf16[4,128,128]{2,1,0:T(8,128)(2,1)S(1)} %get-tuple-element.24), channel_id=1, source_target_pairs={{0,3},{1,0},{2,1},{3,2},{4,7},{5,4},{6,5},{7,6},{8,11},{9,8},{10,9... | collective-permute-start | bytes 393224 | tf_op jit(solution)/shard_map/ppermute | solution.py:223
  23.6 14.3 %collective-permute-start.4 = (bf16[4,128,128]{2,1,0:T(8,128)(2,1)S(1)}, bf16[4,128,128]{2,1,0:T(8,128)(2,1)S(1)}, u32[]{:S(2)}, u32[]{:S(2)}) collective-permute-start(bf16[4,128,128]{2,1,0:T(8,128)(2,1)S(1)} %get-tuple-element.25), channel_id=1, source_target_pairs={{0,2},{1,3},{2,0},{3,1},{4,6},{5,7},{6,4},{7,5},{8,10},{9,11},{10,... | collective-permute-start | bytes 393224 | tf_op jit(solution)/shard_map/ppermute | solution.py:223
  24.0 14.0 %collective-permute-start.5 = (bf16[4,128,128]{2,1,0:T(8,128)(2,1)S(1)}, bf16[4,128,128]{2,1,0:T(8,128)(2,1)S(1)}, u32[]{:S(2)}, u32[]{:S(2)}) collective-permute-start(bf16[4,128,128]{2,1,0:T(8,128)(2,1)S(1)} %get-tuple-element.26), channel_id=1, source_target_pairs={{0,1},{1,2},{2,3},{3,0},{4,5},{5,6},{6,7},{7,4},{8,9},{9,10},{10,1... | collective-permute-start | bytes 393224 | tf_op jit(solution)/shard_map/ppermute | solution.py:223

commit v3 on v2

v3 whole, which is shorter than its diff:
```python
import functools
import math

import jax
import jax.numpy as jnp
import numpy as np
from jax import lax
from jax.experimental import pallas as pl
from jax.experimental.pallas import tpu as pltpu
from jax.sharding import PartitionSpec as P

HD = 128
GRID_W = 64
EPSILON = 1e-06
LOG2_E = math.log2(math.e)
SCALE = 1.0 / math.sqrt(HD)
MIB = 1024 * 1024
VMEM = pl.BlockSpec(memory_space=pltpu.VMEM)
LAST = (((1,), (1,)), ((), ()))
FIRST = (((0,), (0,)), ((), ()))
bf16, f32 = jnp.bfloat16, jnp.float32


def rope_tables(n, txt_rows, img_rows):
    image = np.arange(n * img_rows).reshape(n, img_rows)
    time_dims = HD // 8
    axis_dims = (HD - time_dims) // 2
    channel = np.arange(HD)
    in_rows = (channel >= time_dims) & (channel < time_dims + axis_dims)
    in_cols = channel >= time_dims + axis_dims
    within = np.where(in_cols, channel - time_dims - axis_dims, channel - time_dims)
    within = np.maximum(within, 0) // 2
    frequency = np.power(10000.0, -2.0 * within / axis_dims).astype(np.float32)
    row_pos = (image // GRID_W).astype(np.float32)[..., None]
    col_pos = (image % GRID_W).astype(np.float32)[..., None]
    angles = np.where(in_rows, row_pos * frequency, np.float32(0.0))
    angles = np.where(in_cols, col_pos * frequency, angles)
    angles = np.concatenate([np.zeros((n, txt_rows, HD), np.float32), angles], axis=1)
    angles = angles.reshape(n * (txt_rows + img_rows), HD).astype(np.float64)
    sign = np.where(channel % 2 == 0, -1.0, 1.0)
    return np.cos(angles).astype(np.float32), (np.sin(angles) * sign).astype(np.float32)


def pair_swap():
    row = lax.broadcasted_iota(jnp.int32, (HD, HD), 0)
    col = lax.broadcasted_iota(jnp.int32, (HD, HD), 1)
    other = jnp.where(col % 2 == 0, col + 1, col - 1)
    return (row == other).astype(f32).astype(bf16)


def lane_sum(x):
    high = x.astype(bf16)
    low = (x - high.astype(f32)).astype(bf16)
    return jnp.dot(
        jnp.concatenate([high, low], axis=1),
        jnp.ones((2 * HD, HD), bf16),
        preferred_element_type=f32,
    )


def wide(x, width):
    return jnp.concatenate([x] * (width // HD), axis=1)


def pack_kernel(n, iq, tq, ic, tc, *refs):
    outs, cots = refs[:n], refs[n : 2 * n - 2]
    held, sems = refs[2 * n - 2 : -1], refs[-1]
    txt_rows = tc.shape[1]
    me = lax.axis_index("seq")
    copies = [
        pltpu.make_async_copy(src, dst, sems.at[i])
        for i, (src, dst) in enumerate(zip((iq, tq, ic, tc), held))
    ]
    for copy in copies:
        copy.start()
    for copy in copies:
        copy.wait()
    iq, tq, ic, tc = held
    for step in range(n):
        head = lax.rem(me + step, n)
        cols = pl.ds(pl.multiple_of(head * HD, HD), HD)
        outs[step][:3, :txt_rows] = tq[0, :, :, cols]
        outs[step][:3, txt_rows:] = iq[0, :, :, cols]
        cot = outs[step].at[3] if step < 2 else cots[step - 2]
        cot[:txt_rows] = tc[0, :, cols]
        cot[txt_rows:] = ic[0, :, cols]


def unpack_kernel(n, *refs):
    ins = refs[:n]
    pieces, io, to, ig, tg, gain = refs[n:]
    txt_rows = to.shape[1]
    me = lax.axis_index("seq")
    gain[...] = jnp.sum(pieces[...], axis=0, keepdims=True)[:, : gain.shape[1]]
    for step in range(n):
        head = lax.rem(me + step, n)
        cols = pl.ds(pl.multiple_of(head * HD, HD), HD)
        src = ins[step]
        tg[0, :, :, cols] = src[0:3, :txt_rows]
        ig[0, :, :, cols] = src[0:3, txt_rows:]
        to[0, :, cols] = src[3, :txt_rows]
        io[0, :, cols] = src[3, txt_rows:]


def table_kernel(n, txt_rows, cos_ref, sin_ref, gains_ref, cos_out, sin_out, *gain_tables):
    rows = cos_ref.shape[0] // n
    me = lax.axis_index("seq")
    gains = gains_ref[...]
    lane = lax.broadcasted_iota(jnp.int32, gains.shape, 1)
    swapped = jnp.where(lane % 2 == 0, pltpu.roll(gains, HD - 1, 1), pltpu.roll(gains, 1, 1))
    is_txt = lax.broadcasted_iota(jnp.int32, (rows, HD), 0) < txt_rows
    for step in range(n):
        owner = lax.rem(me + (n - step), n)
        src = pl.ds(pl.multiple_of(owner * rows, rows), rows)
        dst = slice(step * rows, (step + 1) * rows)
        cos, sin = cos_ref[src, :], sin_ref[src, :]
        cos_out[dst] = cos
        sin_out[dst] = sin
        for slot in range(2):
            gain_tables[2 * slot][dst] = cos * jnp.where(
                is_txt, gains[2 + slot : 3 + slot], gains[slot : slot + 1]
            )
            gain_tables[2 * slot + 1][dst] = sin * jnp.where(
                is_txt, swapped[2 + slot : 3 + slot], swapped[slot : slot + 1]
            )


def forward_kernel(n, block_rows, *refs):
    ins, tables = refs[:n], refs[n : n + 4]
    outs = refs[n + 4 : 2 * n + 4]
    q_rot, k_rot, q_inv, k_inv, prob = refs[2 * n + 4 :]
    rows = ins[0].shape[1]
    seq_len = n * rows
    swap = pair_swap()
    for slot, rot_ref, inv_ref in ((0, q_rot, q_inv), (1, k_rot, k_inv)):
        raw = jnp.concatenate([ins[step][slot] for step in range(n)], axis=0)
        wide_raw = raw.astype(f32)
        inv = lax.rsqrt(lane_sum(wide_raw * wide_raw) * (1.0 / HD) + EPSILON)
        other = jnp.dot(raw, swap, preferred_element_type=f32)
        rot = wide_raw * tables[2 * slot][...] + other * tables[2 * slot + 1][...]
        rot = (rot * inv).astype(bf16)
        inv_ref[...] = inv
        rot_ref[:, :HD] = rot
        rot_ref[:, HD:] = jnp.dot(rot, swap, preferred_element_type=f32).astype(bf16)
    k = k_rot[:, :HD]
    v = jnp.concatenate([ins[step][2] for step in range(n)], axis=0)
    per_block = block_rows // rows
    for i in range(seq_len // block_rows):
        at = slice(i * block_rows, (i + 1) * block_rows)
        s = lax.dot_general(q_rot[at, :HD], k, LAST, preferred_element_type=f32)
        e = jnp.exp2(s * (SCALE * LOG2_E))
        total = sum(e[:, j * HD : (j + 1) * HD] for j in range(seq_len // HD))
        p = e * wide(1.0 / lane_sum(total), seq_len)
        prob[at, :] = p
        o = jnp.dot(p.astype(bf16), v, preferred_element_type=f32).astype(bf16)
        for j in range(per_block):
            outs[i * per_block + j][...] = o[j * rows : (j + 1) * rows]


def backward_kernel(n, txt_rows, per, grad_scale, block_rows, *refs):
    ins, cots, refs = refs[:n], refs[n : 2 * n - 2], refs[2 * n - 2 :]
    cots = [ins[j].at[3] for j in range(2)] + list(cots)
    outs, refs = refs[:n], refs[n:]
    q_rot, k_rot, q_inv, k_inv, prob, cos_ref, sin_ref, gains_ref = refs[:8]
    grads, gain_out = refs[8 : n + 8], refs[n + 8]
    q_acc, k_acc, v_acc = refs[n + 9 :]
    rows = ins[0].shape[1]
    seq_len = n * rows
    v = jnp.concatenate([ins[step][2] for step in range(n)], axis=0)
    per_block = block_rows // rows
    for i in range(seq_len // block_rows):
        at = slice(i * block_rows, (i + 1) * block_rows)
        mine = range(i * per_block, (i + 1) * per_block)
        g = jnp.concatenate([cots[j][...] for j in mine], axis=0)
        o = jnp.concatenate([outs[j][...] for j in mine], axis=0)
        delta = lane_sum(g.astype(f32) * o.astype(f32))
        p = prob[at, :]
        dp = lax.dot_general(g, v, LAST, preferred_element_type=f32)
        ds = (p * (dp - wide(delta, seq_len)) * SCALE).astype(bf16)
        dv = lax.dot_general(p.astype(bf16), g, FIRST, preferred_element_type=f32)
        q_acc[at, :] = jnp.dot(ds, k_rot[...], preferred_element_type=f32)
        dk = lax.dot_general(ds, q_rot[at, :], FIRST, preferred_element_type=f32)
        if i == 0:
            v_acc[...] = dv
            k_acc[...] = dk
        else:
            v_acc[...] += dv
            k_acc[...] += dk

    gains = gains_ref[...]
    is_txt = lax.broadcasted_iota(jnp.int32, (rows, HD), 0) < txt_rows
    sums = [jnp.zeros((1, HD), f32) for _ in range(4)]
    for slot, acc, inv_ref in ((0, q_acc, q_inv), (1, k_acc, k_inv)):
        gain = jnp.where(is_txt, gains[2 + slot : 3 + slot], gains[slot : slot + 1])
        for step in range(n):
            at = slice(step * rows, (step + 1) * rows)
            inv = inv_ref[at, :]
            hat = ins[step][slot].astype(f32) * inv
            grad = acc[at, :HD] * cos_ref[at, :] - acc[at, HD:] * sin_ref[at, :]
            both = grad * hat
            sums[slot] += jnp.sum(both[txt_rows:], axis=0, keepdims=True)
            sums[2 + slot] += jnp.sum(both[:txt_rows], axis=0, keepdims=True)
            middle = lane_sum(both * gain) * (1.0 / HD)
            grads[step][slot] = ((grad * gain - hat * middle) * inv).astype(bf16)
    for step in range(n):
        grads[step][2] = v_acc[step * rows : (step + 1) * rows].astype(bf16)
        grads[step][3] = outs[step][...]

    for i in range(4 * HD // per):
        row, off = (i * per) // HD, (i * per) % HD
        piece = sums[row] * grad_scale
        if off:
            piece = pltpu.roll(piece, HD - off, 1)
        gain_out[i * n : (i + 1) * n, :] = jnp.broadcast_to(piece, (n, HD))


def per_device(img_qkv, txt_qkv, img_cot, txt_cot, norm_gains):
    n = lax.axis_size("seq")
    dp = lax.axis_size("dp")
    img_rows, txt_rows = img_cot.shape[1], txt_cot.shape[1]
    width = img_cot.shape[2]
    rows = img_rows + txt_rows
    seq_len = n * rows
    per = 4 * HD // dp
    block_rows = min(seq_len, 512)
    limit = 8 * MIB + 32 * block_rows * seq_len + 4 * seq_len * seq_len

    def call(kernel, name, operands, out_shape, scratch=(), in_specs=None):
        return pl.pallas_call(
            kernel,
            out_shape=out_shape,
            in_specs=in_specs or [VMEM] * len(operands),
            out_specs=[VMEM] * len(out_shape),
            scratch_shapes=list(scratch),
            compiler_params=pltpu.CompilerParams(vmem_limit_bytes=limit),
            name=name,
        )(*operands)

    def send(block, d, sign):
        return lax.ppermute(block, "seq", [(i, (i + sign * d) % n) for i in range(n)])

    def exchange(blocks, sign):
        return [blocks[0]] + [send(blocks[d], d, sign) for d in range(1, n)]

    def shape(dims, dtype=f32):
        return jax.ShapeDtypeStruct(dims, dtype)

    block = shape((4, rows, HD), bf16)
    three, one = shape((3, rows, HD), bf16), shape((rows, HD), bf16)
    parts = (jnp.swapaxes(img_qkv, 1, 2), jnp.swapaxes(txt_qkv, 1, 2), img_cot, txt_cot)
    packed = call(
        functools.partial(pack_kernel, n),
        "pack_heads",
        [pltpu.with_memory_space_constraint(x, pltpu.HBM) for x in parts],
        [block] * 2 + [three] * (n - 2) + [one] * (n - 2),
        [pltpu.VMEM(x.shape, bf16) for x in parts] + [pltpu.SemaphoreType.DMA((4,))],
        [pl.BlockSpec(memory_space=pltpu.HBM)] * 4,
    )
    cos, sin = rope_tables(n, txt_rows, img_rows)
    qkv = exchange(packed[:n], 1)
    cot = [send(packed[n + i], 2 + i, 1) for i in range(n - 2)]
    tables = call(
        functools.partial(table_kernel, n, txt_rows),
        "rope_tables",
        (jnp.asarray(cos), jnp.asarray(sin), norm_gains),
        [shape((seq_len, HD))] * 6,
    )
    forward = call(
        functools.partial(forward_kernel, n, block_rows),
        "forward",
        (*qkv, *tables[2:]),
        [one] * n
        + [shape((seq_len, 2 * HD), bf16)] * 2
        + [shape((seq_len, HD))] * 2
        + [shape((seq_len, seq_len))],
    )
    grad_scale = 1.0 / math.sqrt(dp * seq_len * (width // HD))
    backward = call(
        functools.partial(backward_kernel, n, txt_rows, per, grad_scale, block_rows),
        "backward",
        (*qkv, *cot, *forward, *tables[:2], norm_gains),
        [block] * n + [shape((dp * n, HD))],
        [pltpu.VMEM((seq_len, 2 * HD), f32)] * 2 + [pltpu.VMEM((seq_len, HD), f32)],
    )
    grads = exchange(backward[:n], -1)
    pieces = lax.all_to_all(backward[n], ("dp", "seq"), 0, 0, tiled=True)
    io, to, ig, tg, gain = call(
        functools.partial(unpack_kernel, n),
        "unpack_heads",
        (*grads, pieces),
        [
            shape((1, img_rows, width), bf16),
            shape((1, txt_rows, width), bf16),
            shape((1, 3, img_rows, width), bf16),
            shape((1, 3, txt_rows, width), bf16),
            shape((1, per)),
        ],
    )
    return io, to, jnp.swapaxes(ig, 1, 2), jnp.swapaxes(tg, 1, 2), gain.reshape(per)


def solution(mesh):
    in_specs = (
        P("dp", "seq", None, None),
        P("dp", "seq", None, None),
        P("dp", "seq", None),
        P("dp", "seq", None),
        P(),
    )
    out_specs = (
        P("dp", "seq", None),
        P("dp", "seq", None),
        P("dp", "seq", None, None),
        P("dp", "seq", None, None),
        P("dp"),
    )
    return jax.shard_map(
        per_device, mesh=mesh, in_specs=in_specs, out_specs=out_specs, check_vma=False
    )
```

time: 39.1 us -> 37.1 us (0.949)
  waiting for transfers between devices: 7.3 us -> 4.98 us
  starting transfers between devices: 12.1 us -> 13.9 us
  blocking collectives: 13.7 us -> 12.8 us
  Pallas kernels: 5.14 us -> 4.51 us
    ppermute x6 -> x8, waiting for transfers between devices: 7.3 us -> 4.98 us  [send(): lax.ppermute(block, 'seq', [(i, (i + sign * d) % n) for i in range(n)])]
    ppermute x6 -> x8, starting transfers between devices: 12.1 us -> 13.9 us  [send(): lax.ppermute(block, 'seq', [(i, (i + sign * d) % n) for i in range(n)])]
    all_to_all x1, blocking collectives: 13.7 us -> 12.8 us  [per_device(): pieces = lax.all_to_all(backward[n], ('dp', 'seq'), 0, 0, tiled=True)]
    pallas_call x3 -> x5, Pallas kernels: 5.14 us -> 4.51 us  [call(): pl.pallas_call(kernel, out_shape=out_shape, in_specs=in_specs or [VMEM] *...]
  transfers between devices with their start and end apart: 6 -> 8, of which waited for: 2 -> 2; matrix products, arithmetic and copies ran while one was open for 0% -> 0% of each run, Pallas kernels for 0% -> 4%
where the time goes in v3:
time: 37.1 us; the launch traced here: 36.9 us
  starting transfers between devices  13.9 us (37%)
  blocking collectives  12.8 us (35%)
  waiting for transfers between devices  4.98 us (13%)
  Pallas kernels  4.51 us (12%)
  between operations  0.69 us (2%)
    ppermute x8, starting transfers between devices, send(): lax.ppermute(block, 'seq', [(i, (i + sign * d) % n) for i in range(n)])  13.9 us
    all_to_all x1, blocking collectives, per_device(): pieces = lax.all_to_all(backward[n], ('dp', 'seq'), 0, 0, tiled=True)  12.8 us
    ppermute x8, waiting for transfers between devices, send(): lax.ppermute(block, 'seq', [(i, (i + sign * d) % n) for i in range(n)])  4.98 us
    pallas_call x5, Pallas kernels, call(): pl.pallas_call(kernel, out_shape=out_shape, in_specs=in_specs or [VMEM] *...  4.51 us
  transfers between devices with their start and end apart: 8, of which 2 were waited for; matrix products, arithmetic and copies ran while one was open for 0% of the time, Pallas kernels for 4%

profile of v3, /device:TPU:0, one launch (start us, length us, event | category | flops | bytes accessed | tf_op | source)
XLA Modules:
  0.0 36.9 jit_solution(9494699930820788943)
XLA Ops:
  0.6 0.0 copy-start
  0.6 0.0 copy-start.1
  0.7 1.2 %pack_heads.1 = (bf16[4,128,128]{2,1,0:T(8,128)(2,1)S(1)}, bf16[4,128,128]{2,1,0:T(8,128)(2,1)S(1)}, bf16[3,128,128]{2,1,0:T(8,128)(2,1)S(1)}, bf16[3,128,128]{2...) custom-call(bf16[1,3,112,512]{3,2,1,0:T(8,128)(2,1)} %bitcast.11, ...), custom_call_target="tpu_custom_call" | custom-call | tf_op jit(solution)/shard_map/pack_heads/pallas_call | solution.py:229
  1.9 3.1 %collective-permute-start = (bf16[4,128,128]{2,1,0:T(8,128)(2,1)S(1)}, bf16[4,128,128]{2,1,0:T(8,128)(2,1)S(1)}, u32[]{:S(2)}, u32[]{:S(2)}) collective-permute-start(bf16[4,128,128]{2,1,0:T(8,128)(2,1)S(1)} %get-tuple-element.37), channel_id=1, source_target_pairs={{0,1},{1,2},{2,3},{3,0},{4,5},{5,6},{6,7},{7,4},{8,9},{9,10},{10,1... | collective-permute-start | bytes 393224 | tf_op jit(solution)/shard_map/ppermute | solution.py:240
  5.0 2.6 %collective-permute-start.1 = (bf16[3,128,128]{2,1,0:T(8,128)(2,1)S(1)}, bf16[3,128,128]{2,1,0:T(8,128)(2,1)S(1)}, u32[]{:S(2)}, u32[]{:S(2)}) collective-permute-start(bf16[3,128,128]{2,1,0:T(8,128)(2,1)S(1)} %get-tuple-element.38), channel_id=1, source_target_pairs={{0,2},{1,3},{2,0},{3,1},{4,6},{5,7},{6,4},{7,5},{8,10},{9,11},{10,... | collective-permute-start | bytes 294920 | tf_op jit(solution)/shard_map/ppermute | solution.py:240
  7.5 0.0 copy-start.2
  7.5 1.3 %collective-permute-start.2 = (bf16[3,128,128]{2,1,0:T(8,128)(2,1)S(1)}, bf16[3,128,128]{2,1,0:T(8,128)(2,1)S(1)}, u32[]{:S(2)}, u32[]{:S(2)}) collective-permute-start(bf16[3,128,128]{2,1,0:T(8,128)(2,1)S(1)} %get-tuple-element.39), channel_id=1, source_target_pairs={{0,3},{1,0},{2,1},{3,2},{4,7},{5,4},{6,5},{7,6},{8,11},{9,8},{10,9... | collective-permute-start | bytes 294920 | tf_op jit(solution)/shard_map/ppermute | solution.py:240
  8.9 0.2 collective-permute-start.3
  9.1 2.8 %collective-permute-start.4 = (bf16[128,128]{1,0:T(8,128)(2,1)S(1)}, bf16[128,128]{1,0:T(8,128)(2,1)S(1)}, u32[]{:S(2)}, u32[]{:S(2)}) collective-permute-start(bf16[128,128]{1,0:T(8,128)(2,1)S(1)} %get-tuple-element.41), channel_id=1, source_target_pairs={{0,3},{1,0},{2,1},{3,2},{4,7},{5,4},{6,5},{7,6},{8,11},{9,8},{10,9... | collective-permute-start | bytes 98312 | tf_op jit(solution)/shard_map/ppermute | solution.py:240
  11.9 0.0 copy-done
  11.9 0.0 copy-done.1
  11.9 0.0 copy-done.2
  11.9 0.1 rope_tables.1
  12.1 3.1 %collective-permute-done.1.refs_2_ = bf16[3,128,128]{2,1,0:T(8,128)(2,1)S(1)} collective-permute-done((bf16[3,128,128]{2,1,0:T(8,128)(2,1)S(1)}, bf16[3,128,128]{2,1,0:T(8,128)(2,1)S(1)}, u32[]{:S(2)}, u32[]{:S(2)}) %collective-permute-start.1) | collective-permute-done | bytes 98336 | tf_op jit(solution)/shard_map/ppermute | solution.py:240
  15.1 0.0 collective-permute-done.2.refs_3_
  15.1 0.0 collective-permute-done.refs_1_
  15.1 1.2 %forward.1 = (bf16[128,128]{1,0:T(8,128)(2,1)S(1)}, bf16[128,128]{1,0:T(8,128)(2,1)S(1)}, bf16[128,128]{1,0:T(8,128)(2,1)S(1)}, bf16[128,128]{1,0:T(8,128)(2,1)S...) custom-call(bf16[4,128,128]{2,1,0:T(8,128)(2,1)S(1)} %get-tuple-elem, ...), custom_call_target="tpu_custom_call" | custom-call | tf_op jit(solution)/shard_map/forward/pallas_call | solution.py:229
  16.4 1.9 %collective-permute-done.3.refs_4_ = bf16[128,128]{1,0:T(8,128)(2,1)S(1)} collective-permute-done((bf16[128,128]{1,0:T(8,128)(2,1)S(1)}, bf16[128,128]{1,0:T(8,128)(2,1)S(1)}, u32[]{:S(2)}, u32[]{:S(2)}) %collective-permute-start.3) | collective-permute-done | bytes 32800 | tf_op jit(solution)/shard_map/ppermute | solution.py:240
  18.3 0.0 collective-permute-done.4.refs_5_
  18.3 1.0 %backward.1 = (bf16[4,128,128]{2,1,0:T(8,128)(2,1)S(1)}, bf16[4,128,128]{2,1,0:T(8,128)(2,1)S(1)}, bf16[4,128,128]{2,1,0:T(8,128)(2,1)S(1)}, bf16[4,128,128]{2,1,0:T(8,128)(2,1)S(1)}, f32[32,128]{1,0:T(8,128)S(1)}) custom-call(bf16[4,128,128]{2,1,0:T(8,128)(2,1)S(1)} %get-tuple-element.36.refs_0_, bf16[4,128,128]{2,1,0:T(8,128)(2,1)S(1)} %collective-permute-done.refs_1_, ...), custom_call_target="tpu_custom_call" | custom-call | tf_op jit(solution)/shard_map/backward/pallas_call | solution.py:229
  19.3 3.2 %collective-permute-start.5 = (bf16[4,128,128]{2,1,0:T(8,128)(2,1)S(1)}, bf16[4,128,128]{2,1,0:T(8,128)(2,1)S(1)}, u32[]{:S(2)}, u32[]{:S(2)}) collective-permute-start(bf16[4,128,128]{2,1,0:T(8,128)(2,1)S(1)} %get-tuple-element.58), channel_id=1, source_target_pairs={{0,3},{1,0},{2,1},{3,2},{4,7},{5,4},{6,5},{7,6},{8,11},{9,8},{10,9... | collective-permute-start | bytes 393224 | tf_op jit(solution)/shard_map/ppermute | solution.py:240
  22.6 0.0 collective-permute-start.6
  22.6 0.6 %collective-permute-start.7 = (bf16[4,128,128]{2,1,0:T(8,128)(2,1)S(1)}, bf16[4,128,128]{2,1,0:T(8,128)(2,1)S(1)}, u32[]{:S(2)}, u32[]{:S(2)}) collective-permute-start(bf16[4,128,128]{2,1,0:T(8,128)(2,1)S(1)} %get-tuple-element.60), channel_id=1, source_target_pairs={{0,1},{1,2},{2,3},{3,0},{4,5},{5,6},{6,7},{7,4},{8,9},{9,10},{10,1... | collective-permute-start | bytes 393224 | tf_op jit(solution)/shard_map/ppermute | solution.py:240
  23.2 12.8 %all_to_all.11 = f32[32,1,128]{2,1,0:T(1,128)S(1)} all-to-all(f32[32,1,128]{2,1,0:T(1,128)S(1)} %bitcast.10), channel_id=1, replica_groups=mesh['dp'=8,'seq'=4] {'dp','seq'}, dimensions={0} | all-to-all | bytes 32768 | tf_op jit(solution)/shard_map/all_to_all | solution.py:286
  36.0 0.0 collective-permute-done.5.refs_1_
  36.0 0.0 collective-permute-done.6.refs_2_
  36.0 0.0 collective-permute-done.7.refs_3_
  36.0 0.9 %unpack_heads.1 = (bf16[1,112,512]{2,1,0:T(8,128)(2,1)}, bf16[1,16,512]{2,1,0:T(8,128)(2,1)}, bf16[1,3,112,512]{3,2,1,0:T(8,128)(2,1)}, bf16[1,3,16,512]{3,2,1,0:T(8,128)(2,1)}, f32[1,64]{1,0:T(1,128)}) custom-call(bf16[4,128,128]{2,1,0:T(8,128)(2,1)S(1)} %get-tuple-element.57.refs_0_, bf16[4,128,128]{2,1,0:T(8,128)(2,1)S(1)} %collective-permute-done.5.refs_1_, ...), custom_call_target="tpu_custom_call" | custom-call | tf_op jit(solution)/shard_map/unpack_heads/pallas_call | solution.py:229
Async XLA Ops:
  0.6 11.3 %copy-start = (f32[512,128]{1,0:T(8,128)S(1)}, f32[512,128]{1,0:T(8,128)}, u32[]{:S(2)}) copy-start(f32[512,128]{1,0:T(8,128)} %constant.5.clone.sin_ref) | copy-start | bytes 786436
  0.6 11.3 %copy-start.1 = (f32[512,128]{1,0:T(8,128)S(1)}, f32[512,128]{1,0:T(8,128)}, u32[]{:S(2)}) copy-start(f32[512,128]{1,0:T(8,128)} %constant.4.clone.cos_ref) | copy-start | bytes 786436
  1.9 13.3 %collective-permute-start = (bf16[4,128,128]{2,1,0:T(8,128)(2,1)S(1)}, bf16[4,128,128]{2,1,0:T(8,128)(2,1)S(1)}, u32[]{:S(2)}, u32[]{:S(2)}) collective-permute-start(bf16[4,128,128]{2,1,0:T(8,128)(2,1)S(1)} %get-tuple-element.37), channel_id=1, source_target_pairs={{0,1},{1,2},{2,3},{3,0},{4,5},{5,6},{6,7},{7,4},{8,9},{9,10},{10,1... | collective-permute-start | bytes 393224 | tf_op jit(solution)/shard_map/ppermute | solution.py:240
  5.0 10.2 %collective-permute-start.1 = (bf16[3,128,128]{2,1,0:T(8,128)(2,1)S(1)}, bf16[3,128,128]{2,1,0:T(8,128)(2,1)S(1)}, u32[]{:S(2)}, u32[]{:S(2)}) collective-permute-start(bf16[3,128,128]{2,1,0:T(8,128)(2,1)S(1)} %get-tuple-element.38), channel_id=1, source_target_pairs={{0,2},{1,3},{2,0},{3,1},{4,6},{5,7},{6,4},{7,5},{8,10},{9,11},{10,... | collective-permute-start | bytes 294920 | tf_op jit(solution)/shard_map/ppermute | solution.py:240
  7.5 4.4 %copy-start.2 = (f32[4,128]{1,0:T(4,128)S(1)}, f32[4,128]{1,0:T(4,128)}, u32[]{:S(2)}) copy-start(f32[4,128]{1,0:T(4,128)} %refs_17_.1) | copy-start | bytes 6148
  7.5 7.6 %collective-permute-start.2 = (bf16[3,128,128]{2,1,0:T(8,128)(2,1)S(1)}, bf16[3,128,128]{2,1,0:T(8,128)(2,1)S(1)}, u32[]{:S(2)}, u32[]{:S(2)}) collective-permute-start(bf16[3,128,128]{2,1,0:T(8,128)(2,1)S(1)} %get-tuple-element.39), channel_id=1, source_target_pairs={{0,3},{1,0},{2,1},{3,2},{4,7},{5,4},{6,5},{7,6},{8,11},{9,8},{10,9... | collective-permute-start | bytes 294920 | tf_op jit(solution)/shard_map/ppermute | solution.py:240
  8.9 9.4 %collective-permute-start.3 = (bf16[128,128]{1,0:T(8,128)(2,1)S(1)}, bf16[128,128]{1,0:T(8,128)(2,1)S(1)}, u32[]{:S(2)}, u32[]{:S(2)}) collective-permute-start(bf16[128,128]{1,0:T(8,128)(2,1)S(1)} %get-tuple-element.40), channel_id=1, source_target_pairs={{0,2},{1,3},{2,0},{3,1},{4,6},{5,7},{6,4},{7,5},{8,10},{9,11},{10,... | collective-permute-start | bytes 98312 | tf_op jit(solution)/shard_map/ppermute | solution.py:240
  9.1 9.2 %collective-permute-start.4 = (bf16[128,128]{1,0:T(8,128)(2,1)S(1)}, bf16[128,128]{1,0:T(8,128)(2,1)S(1)}, u32[]{:S(2)}, u32[]{:S(2)}) collective-permute-start(bf16[128,128]{1,0:T(8,128)(2,1)S(1)} %get-tuple-element.41), channel_id=1, source_target_pairs={{0,3},{1,0},{2,1},{3,2},{4,7},{5,4},{6,5},{7,6},{8,11},{9,8},{10,9... | collective-permute-start | bytes 98312 | tf_op jit(solution)/shard_map/ppermute | solution.py:240
  19.3 16.6 %collective-permute-start.5 = (bf16[4,128,128]{2,1,0:T(8,128)(2,1)S(1)}, bf16[4,128,128]{2,1,0:T(8,128)(2,1)S(1)}, u32[]{:S(2)}, u32[]{:S(2)}) collective-permute-start(bf16[4,128,128]{2,1,0:T(8,128)(2,1)S(1)} %get-tuple-element.58), channel_id=1, source_target_pairs={{0,3},{1,0},{2,1},{3,2},{4,7},{5,4},{6,5},{7,6},{8,11},{9,8},{10,9... | collective-permute-start | bytes 393224 | tf_op jit(solution)/shard_map/ppermute | solution.py:240
  22.6 13.4 %collective-permute-start.6 = (bf16[4,128,128]{2,1,0:T(8,128)(2,1)S(1)}, bf16[4,128,128]{2,1,0:T(8,128)(2,1)S(1)}, u32[]{:S(2)}, u32[]{:S(2)}) collective-permute-start(bf16[4,128,128]{2,1,0:T(8,128)(2,1)S(1)} %get-tuple-element.59), channel_id=1, source_target_pairs={{0,2},{1,3},{2,0},{3,1},{4,6},{5,7},{6,4},{7,5},{8,10},{9,11},{10,... | collective-permute-start | bytes 393224 | tf_op jit(solution)/shard_map/ppermute | solution.py:240
  22.6 13.4 %collective-permute-start.7 = (bf16[4,128,128]{2,1,0:T(8,128)(2,1)S(1)}, bf16[4,128,128]{2,1,0:T(8,128)(2,1)S(1)}, u32[]{:S(2)}, u32[]{:S(2)}) collective-permute-start(bf16[4,128,128]{2,1,0:T(8,128)(2,1)S(1)} %get-tuple-element.60), channel_id=1, source_target_pairs={{0,1},{1,2},{2,3},{3,0},{4,5},{5,6},{6,7},{7,4},{8,9},{9,10},{10,1... | collective-permute-start | bytes 393224 | tf_op jit(solution)/shard_map/ppermute | solution.py:240

commit v4 on v3

--- a/solution.py
+++ b/solution.py
@@ -11,6 +11,7 @@
 
 HD = 128
 GRID_W = 64
+GAIN_ROWS = 16
 EPSILON = 1e-06
 LOG2_E = math.log2(math.e)
 SCALE = 1.0 / math.sqrt(HD)
@@ -19,6 +20,10 @@
 LAST = (((1,), (1,)), ((), ()))
 FIRST = (((0,), (0,)), ((), ()))
 bf16, f32 = jnp.bfloat16, jnp.float32
+
+
+def distances(n):
+    return sorted(range(n), key=lambda d: (min(d, n - d), d))
 
 
 def rope_tables(n, txt_rows, img_rows):
@@ -42,29 +47,19 @@
 
 
 def pair_swap():
-    row = lax.broadcasted_iota(jnp.int32, (HD, HD), 0)
-    col = lax.broadcasted_iota(jnp.int32, (HD, HD), 1)
+    row = lax.broadcasted_iota(jnp.int32, (2 * HD, 2 * HD), 0)
+    col = lax.broadcasted_iota(jnp.int32, (2 * HD, 2 * HD), 1)
     other = jnp.where(col % 2 == 0, col + 1, col - 1)
     return (row == other).astype(f32).astype(bf16)
 
 
 def lane_sum(x):
-    high = x.astype(bf16)
-    low = (x - high.astype(f32)).astype(bf16)
-    return jnp.dot(
-        jnp.concatenate([high, low], axis=1),
-        jnp.ones((2 * HD, HD), bf16),
-        preferred_element_type=f32,
-    )
-
-
-def wide(x, width):
-    return jnp.concatenate([x] * (width // HD), axis=1)
+    return jnp.sum(x, axis=1, keepdims=True)
 
 
 def pack_kernel(n, iq, tq, ic, tc, *refs):
-    outs, cots = refs[:n], refs[n : 2 * n - 2]
-    held, sems = refs[2 * n - 2 : -1], refs[-1]
+    outs, cots = refs[:n], refs[n : 2 * n - 1]
+    held, sems = refs[2 * n - 1 : -1], refs[-1]
     txt_rows = tc.shape[1]
     me = lax.axis_index("seq")
     copies = [
@@ -77,29 +72,33 @@
         copy.wait()
     iq, tq, ic, tc = held
     for step in range(n):
-        head = lax.rem(me + step, n)
+        head = lax.rem(me + distances(n)[step], n)
         cols = pl.ds(pl.multiple_of(head * HD, HD), HD)
         outs[step][:3, :txt_rows] = tq[0, :, :, cols]
         outs[step][:3, txt_rows:] = iq[0, :, :, cols]
-        cot = outs[step].at[3] if step < 2 else cots[step - 2]
+        cot = outs[step].at[3] if step < 1 else cots[step - 1]
         cot[:txt_rows] = tc[0, :, cols]
         cot[txt_rows:] = ic[0, :, cols]
 
 
 def unpack_kernel(n, *refs):
-    ins = refs[:n]
-    pieces, io, to, ig, tg, gain = refs[n:]
+    ins, parts = refs[:n], refs[n:-5]
+    io, to, ig, tg, gain = refs[-5:]
     txt_rows = to.shape[1]
+    rows = txt_rows + io.shape[1]
+    total = sum(part[...] for part in parts)
+    owner = lax.broadcasted_iota(jnp.int32, total.shape, 0) == lax.axis_index("dp")
+    total = jnp.sum(jnp.where(owner, total, 0.0), axis=0, keepdims=True)
+    gain[...] = total[:, : gain.shape[1]]
     me = lax.axis_index("seq")
-    gain[...] = jnp.sum(pieces[...], axis=0, keepdims=True)[:, : gain.shape[1]]
     for step in range(n):
-        head = lax.rem(me + step, n)
+        head = lax.rem(me + distances(n)[step], n)
         cols = pl.ds(pl.multiple_of(head * HD, HD), HD)
-        src = ins[step]
-        tg[0, :, :, cols] = src[0:3, :txt_rows]
-        ig[0, :, :, cols] = src[0:3, txt_rows:]
-        to[0, :, cols] = src[3, :txt_rows]
-        io[0, :, cols] = src[3, txt_rows:]
+        for slot in range(4):
+            txt, img = (to, io) if slot == 3 else (tg.at[:, slot], ig.at[:, slot])
+            at = slot * rows
+            txt[0, :, cols] = ins[step][at : at + txt_rows]
+            img[0, :, cols] = ins[step][at + txt_rows : at + rows]
 
 
 def table_kernel(n, txt_rows, cos_ref, sin_ref, gains_ref, cos_out, sin_out, *gain_tables):
@@ -110,7 +109,7 @@
     swapped = jnp.where(lane % 2 == 0, pltpu.roll(gains, HD - 1, 1), pltpu.roll(gains, 1, 1))
     is_txt = lax.broadcasted_iota(jnp.int32, (rows, HD), 0) < txt_rows
     for step in range(n):
-        owner = lax.rem(me + (n - step), n)
+        owner = lax.rem(me + (n - distances(n)[step]), n)
         src = pl.ds(pl.multiple_of(owner * rows, rows), rows)
         dst = slice(step * rows, (step + 1) * rows)
         cos, sin = cos_ref[src, :], sin_ref[src, :]
@@ -132,16 +131,21 @@
     rows = ins[0].shape[1]
     seq_len = n * rows
     swap = pair_swap()
+    raws = [jnp.concatenate([ins[step][slot] for step in range(n)], axis=0) for slot in range(2)]
+    others = jnp.dot(jnp.concatenate(raws, axis=1), swap, preferred_element_type=f32)
+    rots = []
     for slot, rot_ref, inv_ref in ((0, q_rot, q_inv), (1, k_rot, k_inv)):
-        raw = jnp.concatenate([ins[step][slot] for step in range(n)], axis=0)
-        wide_raw = raw.astype(f32)
-        inv = lax.rsqrt(lane_sum(wide_raw * wide_raw) * (1.0 / HD) + EPSILON)
-        other = jnp.dot(raw, swap, preferred_element_type=f32)
-        rot = wide_raw * tables[2 * slot][...] + other * tables[2 * slot + 1][...]
+        raw = raws[slot].astype(f32)
+        inv = lax.rsqrt(lane_sum(raw * raw) * (1.0 / HD) + EPSILON)
+        other = others[:, slot * HD : (slot + 1) * HD]
+        rot = raw * tables[2 * slot][...] + other * tables[2 * slot + 1][...]
         rot = (rot * inv).astype(bf16)
-        inv_ref[...] = inv
+        inv_ref[...] = jnp.broadcast_to(inv, inv_ref.shape)
         rot_ref[:, :HD] = rot
-        rot_ref[:, HD:] = jnp.dot(rot, swap, preferred_element_type=f32).astype(bf16)
+        rots.append(rot)
+    turned = jnp.dot(jnp.concatenate(rots, axis=1), swap, preferred_element_type=f32).astype(bf16)
+    q_rot[:, HD:] = turned[:, :HD]
+    k_rot[:, HD:] = turned[:, HD:]
     k = k_rot[:, :HD]
     v = jnp.concatenate([ins[step][2] for step in range(n)], axis=0)
     per_block = block_rows // rows
@@ -150,21 +154,24 @@
         s = lax.dot_general(q_rot[at, :HD], k, LAST, preferred_element_type=f32)
         e = jnp.exp2(s * (SCALE * LOG2_E))
         total = sum(e[:, j * HD : (j + 1) * HD] for j in range(seq_len // HD))
-        p = e * wide(1.0 / lane_sum(total), seq_len)
+        p = e * (1.0 / lane_sum(total))
         prob[at, :] = p
         o = jnp.dot(p.astype(bf16), v, preferred_element_type=f32).astype(bf16)
         for j in range(per_block):
             outs[i * per_block + j][...] = o[j * rows : (j + 1) * rows]
 
 
-def backward_kernel(n, txt_rows, per, grad_scale, block_rows, *refs):
-    ins, cots, refs = refs[:n], refs[n : 2 * n - 2], refs[2 * n - 2 :]
-    cots = [ins[j].at[3] for j in range(2)] + list(cots)
+def backward_kernel(n, txt_rows, grad_scale, block_rows, *refs):
+    rows = refs[0].shape[1]
+    ins, cots, refs = refs[:n], refs[n : 2 * n - 1], refs[2 * n - 1 :]
+    cots = [ins[j].at[3] for j in range(1)] + list(cots)
     outs, refs = refs[:n], refs[n:]
     q_rot, k_rot, q_inv, k_inv, prob, cos_ref, sin_ref, gains_ref = refs[:8]
-    grads, gain_out = refs[8 : n + 8], refs[n + 8]
+    blocks, gain_out = refs[8 : n + 8], refs[n + 8]
+    grads = [
+        [block.at[slot * rows : (slot + 1) * rows] for slot in range(4)] for block in blocks
+    ]
     q_acc, k_acc, v_acc = refs[n + 9 :]
-    rows = ins[0].shape[1]
     seq_len = n * rows
     v = jnp.concatenate([ins[step][2] for step in range(n)], axis=0)
     per_block = block_rows // rows
@@ -176,7 +183,7 @@
         delta = lane_sum(g.astype(f32) * o.astype(f32))
         p = prob[at, :]
         dp = lax.dot_general(g, v, LAST, preferred_element_type=f32)
-        ds = (p * (dp - wide(delta, seq_len)) * SCALE).astype(bf16)
+        ds = (p * (dp - delta) * SCALE).astype(bf16)
         dv = lax.dot_general(p.astype(bf16), g, FIRST, preferred_element_type=f32)
         q_acc[at, :] = jnp.dot(ds, k_rot[...], preferred_element_type=f32)
         dk = lax.dot_general(ds, q_rot[at, :], FIRST, preferred_element_type=f32)
@@ -201,17 +208,28 @@
             sums[slot] += jnp.sum(both[txt_rows:], axis=0, keepdims=True)
             sums[2 + slot] += jnp.sum(both[:txt_rows], axis=0, keepdims=True)
             middle = lane_sum(both * gain) * (1.0 / HD)
-            grads[step][slot] = ((grad * gain - hat * middle) * inv).astype(bf16)
+            grads[step][slot][...] = ((grad * gain - hat * middle) * inv).astype(bf16)
     for step in range(n):
-        grads[step][2] = v_acc[step * rows : (step + 1) * rows].astype(bf16)
-        grads[step][3] = outs[step][...]
-
+        grads[step][2][...] = v_acc[step * rows : (step + 1) * rows].astype(bf16)
+        grads[step][3][...] = outs[step][...]
+
+    total = jnp.concatenate(sums, axis=0) * grad_scale
+    high = total.astype(bf16).astype(f32)
+    terms = jnp.concatenate([high, total - high, jnp.zeros((GAIN_ROWS - 8, HD), f32)], axis=0)
+    blocks[1][4 * rows :] = terms.astype(bf16)
+    gain_out[...] = total
+
+
+def share_kernel(n, per, first, *refs):
+    tail = first[first.shape[0] - GAIN_ROWS :].astype(f32)
+    total = tail[:4] + tail[4:8]
+    for part in refs[:-1]:
+        total += part[...]
+    out = refs[-1]
     for i in range(4 * HD // per):
         row, off = (i * per) // HD, (i * per) % HD
-        piece = sums[row] * grad_scale
-        if off:
-            piece = pltpu.roll(piece, HD - off, 1)
-        gain_out[i * n : (i + 1) * n, :] = jnp.broadcast_to(piece, (n, HD))
+        piece = total[row : row + 1]
+        out[i : i + 1, :] = pltpu.roll(piece, HD - off, 1) if off else piece
 
 
 def per_device(img_qkv, txt_qkv, img_cot, txt_cot, norm_gains):
@@ -225,7 +243,8 @@
     block_rows = min(seq_len, 512)
     limit = 8 * MIB + 32 * block_rows * seq_len + 4 * seq_len * seq_len
 
-    def call(kernel, name, operands, out_shape, scratch=(), in_specs=None):
+    def call(kernel, name, operands, out_shape, scratch=(), in_specs=None, flops=None):
+        cost = flops and pl.CostEstimate(flops=flops, bytes_accessed=MIB, transcendentals=0)
         return pl.pallas_call(
             kernel,
             out_shape=out_shape,
@@ -233,11 +252,13 @@
             out_specs=[VMEM] * len(out_shape),
             scratch_shapes=list(scratch),
             compiler_params=pltpu.CompilerParams(vmem_limit_bytes=limit),
+            cost_estimate=cost,
             name=name,
         )(*operands)
 
     def send(block, d, sign):
-        return lax.ppermute(block, "seq", [(i, (i + sign * d) % n) for i in range(n)])
+        hop = sign * distances(n)[d]
+        return lax.ppermute(block, "seq", [(i, (i + hop) % n) for i in range(n)])
 
     def exchange(blocks, sign):
         return [blocks[0]] + [send(blocks[d], d, sign) for d in range(1, n)]
@@ -252,13 +273,13 @@
         functools.partial(pack_kernel, n),
         "pack_heads",
         [pltpu.with_memory_space_constraint(x, pltpu.HBM) for x in parts],
-        [block] * 2 + [three] * (n - 2) + [one] * (n - 2),
+        [block] * 1 + [three] * (n - 1) + [one] * (n - 1),
         [pltpu.VMEM(x.shape, bf16) for x in parts] + [pltpu.SemaphoreType.DMA((4,))],
         [pl.BlockSpec(memory_space=pltpu.HBM)] * 4,
     )
     cos, sin = rope_tables(n, txt_rows, img_rows)
     qkv = exchange(packed[:n], 1)
-    cot = [send(packed[n + i], 2 + i, 1) for i in range(n - 2)]
+    cot = [send(packed[n + i], 1 + i, 1) for i in range(n - 1)]
     tables = call(
         functools.partial(table_kernel, n, txt_rows),
         "rope_tables",
@@ -276,18 +297,31 @@
     )
     grad_scale = 1.0 / math.sqrt(dp * seq_len * (width // HD))
     backward = call(
-        functools.partial(backward_kernel, n, txt_rows, per, grad_scale, block_rows),
+        functools.partial(backward_kernel, n, txt_rows, grad_scale, block_rows),
         "backward",
         (*qkv, *cot, *forward, *tables[:2], norm_gains),
-        [block] * n + [shape((dp * n, HD))],
+        [shape((4 * rows + (GAIN_ROWS if step == 1 else 0), HD), bf16) for step in range(n)]
+        + [shape((4, HD))],
         [pltpu.VMEM((seq_len, 2 * HD), f32)] * 2 + [pltpu.VMEM((seq_len, HD), f32)],
     )
-    grads = exchange(backward[:n], -1)
-    pieces = lax.all_to_all(backward[n], ("dp", "seq"), 0, 0, tiled=True)
+    first = send(backward[1], 1, -1)
+    small = [backward[n]] + [send(backward[n], d, -1) for d in range(2, n)]
+    grads = [backward[0], first] + [send(backward[d], d, -1) for d in range(2, n)]
+    (part,) = call(
+        functools.partial(share_kernel, n, per),
+        "gain_share",
+        (first, *small),
+        [shape((dp, HD))],
+        flops=20 * 10**9,
+    )
+    part = part + lax.ppermute(part, "dp", [(i, i ^ 1) for i in range(dp)])
+    parts = [part] + [
+        lax.ppermute(part, "dp", [(i, i ^ d) for i in range(dp)]) for d in range(2, dp, 2)
+    ]
     io, to, ig, tg, gain = call(
         functools.partial(unpack_kernel, n),
         "unpack_heads",
-        (*grads, pieces),
+        (*grads, *parts),
         [
             shape((1, img_rows, width), bf16),
             shape((1, txt_rows, width), bf16),

time: 37.1 us -> 35.9 us (0.968)
  blocking collectives: 12.8 us -> 0 us
  starting transfers between devices: 13.9 us -> 21.7 us
  waiting for transfers between devices: 4.98 us -> 9.13 us
    all_to_all x1 -> x0, blocking collectives: 12.8 us -> none  [per_device(): pieces = lax.all_to_all(backward[n], ('dp', 'seq'), 0, 0, tiled=True)]
    ppermute x8 -> x15, starting transfers between devices: 13.9 us -> 21.7 us  [the longest x11 18.2 us: send(): return lax.ppermute(block, 'seq', [(i, (i + hop) % n) for i in range(n)])]
    ppermute x8 -> x15, waiting for transfers between devices: 4.98 us -> 9.13 us  [the longest x11 7.78 us: send(): return lax.ppermute(block, 'seq', [(i, (i + hop) % n) for i in range(n)])]
    pallas_call x5 -> x6, Pallas kernels: 4.51 us -> 4.21 us  [call(): pl.pallas_call(kernel, out_shape=out_shape, in_specs=in_specs or [VMEM] *...]
  transfers between devices with their start and end apart: 8 -> 15, of which waited for: 2 -> 7; matrix products, arithmetic and copies ran while one was open for 0% -> 0% of each run, Pallas kernels for 4% -> 3%
where the time goes in v4:
time: 35.9 us; the launch traced here: 35.7 us
  starting transfers between devices  21.7 us (60%)
  waiting for transfers between devices  9.13 us (25%)
  Pallas kernels  4.21 us (12%)
  between operations  0.72 us (2%)
    ppermute x11, starting transfers between devices, send(): return lax.ppermute(block, 'seq', [(i, (i + hop) % n) for i in range(n)])  18.2 us
    ppermute x11, waiting for transfers between devices, send(): return lax.ppermute(block, 'seq', [(i, (i + hop) % n) for i in range(n)])  7.78 us
    pallas_call x6, Pallas kernels, call(): pl.pallas_call(kernel, out_shape=out_shape, in_specs=in_specs or [VMEM] *...  4.21 us
    ppermute x3, starting transfers between devices, per_device(): lax.ppermute(part, 'dp', [(i, i ^ d) for i in range(dp)])  3.49 us
    ppermute x1, waiting for transfers between devices, per_device(): part = part + lax.ppermute(part, 'dp', [(i, i ^ 1) for i in range(dp)])  1.15 us
  transfers between devices with their start and end apart: 15, of which 7 were waited for; matrix products, arithmetic and copies ran while one was open for 0% of the time, Pallas kernels for 3%

profile of v4, /device:TPU:0, one launch (start us, length us, event | category | flops | bytes accessed | tf_op | source)
XLA Modules:
  0.0 35.7 jit_solution(14701997266077559328)
XLA Ops:
  0.6 0.0 copy-start
  0.6 0.0 copy-start.1
  0.7 1.2 %pack_heads.1 = (bf16[4,128,128]{2,1,0:T(8,128)(2,1)S(1)}, bf16[3,128,128]{2,1,0:T(8,128)(2,1)S(1)}, bf16[3,128,128]{2,1,0:T(8,128)(2,1)S(1)}, bf16[3,128,128]{2...) custom-call(bf16[1,3,112,512]{3,2,1,0:T(8,128)(2,1)} %bitcast.5, ...), custom_call_target="tpu_custom_call" | custom-call | tf_op jit(solution)/shard_map/pack_heads/pallas_call | solution.py:248
  1.9 3.1 %collective-permute-start = (bf16[3,128,128]{2,1,0:T(8,128)(2,1)S(1)}, bf16[3,128,128]{2,1,0:T(8,128)(2,1)S(1)}, u32[]{:S(2)}, u32[]{:S(2)}) collective-permute-start(bf16[3,128,128]{2,1,0:T(8,128)(2,1)S(1)} %get-tuple-element.38), channel_id=1, source_target_pairs={{0,1},{1,2},{2,3},{3,0},{4,5},{5,6},{6,7},{7,4},{8,9},{9,10},{10,1... | collective-permute-start | bytes 294920 | tf_op jit(solution)/shard_map/ppermute | solution.py:261
  5.0 2.1 %collective-permute-start.1 = (bf16[3,128,128]{2,1,0:T(8,128)(2,1)S(1)}, bf16[3,128,128]{2,1,0:T(8,128)(2,1)S(1)}, u32[]{:S(2)}, u32[]{:S(2)}) collective-permute-start(bf16[3,128,128]{2,1,0:T(8,128)(2,1)S(1)} %get-tuple-element.39), channel_id=1, source_target_pairs={{0,3},{1,0},{2,1},{3,2},{4,7},{5,4},{6,5},{7,6},{8,11},{9,8},{10,9... | collective-permute-start | bytes 294920 | tf_op jit(solution)/shard_map/ppermute | solution.py:261
  7.0 0.9 %collective-permute-start.2 = (bf16[3,128,128]{2,1,0:T(8,128)(2,1)S(1)}, bf16[3,128,128]{2,1,0:T(8,128)(2,1)S(1)}, u32[]{:S(2)}, u32[]{:S(2)}) collective-permute-start(bf16[3,128,128]{2,1,0:T(8,128)(2,1)S(1)} %get-tuple-element.40), channel_id=1, source_target_pairs={{0,2},{1,3},{2,0},{3,1},{4,6},{5,7},{6,4},{7,5},{8,10},{9,11},{10,... | collective-permute-start | bytes 294920 | tf_op jit(solution)/shard_map/ppermute | solution.py:261
  8.0 1.6 %collective-permute-start.3 = (bf16[128,128]{1,0:T(8,128)(2,1)S(1)}, bf16[128,128]{1,0:T(8,128)(2,1)S(1)}, u32[]{:S(2)}, u32[]{:S(2)}) collective-permute-start(bf16[128,128]{1,0:T(8,128)(2,1)S(1)} %get-tuple-element.41), channel_id=1, source_target_pairs={{0,1},{1,2},{2,3},{3,0},{4,5},{5,6},{6,7},{7,4},{8,9},{9,10},{10,1... | collective-permute-start | bytes 98312 | tf_op jit(solution)/shard_map/ppermute | solution.py:261
  9.6 2.2 %collective-permute-start.4 = (bf16[128,128]{1,0:T(8,128)(2,1)S(1)}, bf16[128,128]{1,0:T(8,128)(2,1)S(1)}, u32[]{:S(2)}, u32[]{:S(2)}) collective-permute-start(bf16[128,128]{1,0:T(8,128)(2,1)S(1)} %get-tuple-element.42), channel_id=1, source_target_pairs={{0,3},{1,0},{2,1},{3,2},{4,7},{5,4},{6,5},{7,6},{8,11},{9,8},{10,9... | collective-permute-start | bytes 98312 | tf_op jit(solution)/shard_map/ppermute | solution.py:261
  11.8 0.0 collective-permute-done.refs_1_
  11.8 2.1 %collective-permute-start.5 = (bf16[128,128]{1,0:T(8,128)(2,1)S(1)}, bf16[128,128]{1,0:T(8,128)(2,1)S(1)}, u32[]{:S(2)}, u32[]{:S(2)}) collective-permute-start(bf16[128,128]{1,0:T(8,128)(2,1)S(1)} %get-tuple-element.43), channel_id=1, source_target_pairs={{0,2},{1,3},{2,0},{3,1},{4,6},{5,7},{6,4},{7,5},{8,10},{9,11},{10,... | collective-permute-start | bytes 98312 | tf_op jit(solution)/shard_map/ppermute | solution.py:261
  13.9 0.1 rope_tables.1
  14.0 3.7 %collective-permute-done.2.refs_3_ = bf16[3,128,128]{2,1,0:T(8,128)(2,1)S(1)} collective-permute-done((bf16[3,128,128]{2,1,0:T(8,128)(2,1)S(1)}, bf16[3,128,128]{2,1,0:T(8,128)(2,1)S(1)}, u32[]{:S(2)}, u32[]{:S(2)}) %collective-permute-start.2) | collective-permute-done | bytes 98336 | tf_op jit(solution)/shard_map/ppermute | solution.py:261
  17.7 0.9 %forward.1 = (bf16[128,128]{1,0:T(8,128)(2,1)S(1)}, bf16[128,128]{1,0:T(8,128)(2,1)S(1)}, bf16[128,128]{1,0:T(8,128)(2,1)S(1)}, bf16[128,128]{1,0:T(8,128)(2,1)S...) custom-call(bf16[4,128,128]{2,1,0:T(8,128)(2,1)S(1)} %get-tuple-elem, ...), custom_call_target="tpu_custom_call" | custom-call | tf_op jit(solution)/shard_map/forward/pallas_call | solution.py:248
  18.7 0.0 collective-permute-done.3.refs_4_
  18.7 0.2 collective-permute-done.5.refs_6_
  18.9 1.0 %backward.1 = (bf16[512,128]{1,0:T(8,128)(2,1)S(1)}, bf16[528,128]{1,0:T(8,128)(2,1)S(1)}, bf16[512,128]{1,0:T(8,128)(2,1)S(1)}, bf16[512,128]{1,0:T(8,128)(2,1)S(1)}, f32[4,128]{1,0:T(4,128)S(1)}) custom-call(bf16[4,128,128]{2,1,0:T(8,128)(2,1)S(1)} %get-tuple-element.37.refs_0_, bf16[3,128,128]{2,1,0:T(8,128)(2,1)S(1)} %collective-permute-done.refs_1_, ...), custom_call_target="tpu_custom_call" | custom-call | tf_op jit(solution)/shard_map/backward/pallas_call | solution.py:248
  19.9 1.8 %collective-permute-start.6 = (bf16[528,128]{1,0:T(8,128)(2,1)S(1)}, bf16[528,128]{1,0:T(8,128)(2,1)S(1)}, u32[]{:S(2)}, u32[]{:S(2)}) collective-permute-start(bf16[528,128]{1,0:T(8,128)(2,1)S(1)} %get-tuple-element.60), channel_id=1, source_target_pairs={{0,3},{1,0},{2,1},{3,2},{4,7},{5,4},{6,5},{7,6},{8,11},{9,8},{10,9... | collective-permute-start | bytes 405512 | tf_op jit(solution)/shard_map/ppermute | solution.py:261
  21.6 0.6 %collective-permute-start.9 = (f32[4,128]{1,0:T(4,128)S(1)}, f32[4,128]{1,0:T(4,128)S(1)}, u32[]{:S(2)}, u32[]{:S(2)}) collective-permute-start(f32[4,128]{1,0:T(4,128)S(1)} %get-tuple-element.63.refs_0_), channel_id=1, source_target_pairs={{0,1},{1,2},{2,3},{3,0},{4,5},{5,6},{6,7},{7,4},{8,9},{9,10},{10,1... | collective-permute-start | bytes 6152 | tf_op jit(solution)/shard_map/ppermute | solution.py:261
  22.3 2.8 %collective-permute-start.7 = (bf16[512,128]{1,0:T(8,128)(2,1)S(1)}, bf16[512,128]{1,0:T(8,128)(2,1)S(1)}, u32[]{:S(2)}, u32[]{:S(2)}) collective-permute-start(bf16[512,128]{1,0:T(8,128)(2,1)S(1)} %get-tuple-element.61), channel_id=1, source_target_pairs={{0,1},{1,2},{2,3},{3,0},{4,5},{5,6},{6,7},{7,4},{8,9},{9,10},{10,1... | collective-permute-start | bytes 393224 | tf_op jit(solution)/shard_map/ppermute | solution.py:261
  25.1 0.9 %collective-permute-start.8 = (bf16[512,128]{1,0:T(8,128)(2,1)S(1)}, bf16[512,128]{1,0:T(8,128)(2,1)S(1)}, u32[]{:S(2)}, u32[]{:S(2)}) collective-permute-start(bf16[512,128]{1,0:T(8,128)(2,1)S(1)} %get-tuple-element.62), channel_id=1, source_target_pairs={{0,2},{1,3},{2,0},{3,1},{4,6},{5,7},{6,4},{7,5},{8,10},{9,11},{10,... | collective-permute-start | bytes 393224 | tf_op jit(solution)/shard_map/ppermute | solution.py:261
  26.0 0.1 collective-permute-done.10.refs_2_
  26.1 0.9 %collective-permute-done.9.refs_1_ = f32[4,128]{1,0:T(4,128)S(1)} collective-permute-done((f32[4,128]{1,0:T(4,128)S(1)}, f32[4,128]{1,0:T(4,128)S(1)}, u32[]{:S(2)}, u32[]{:S(2)}) %collective-permute-start.9) | collective-permute-done | bytes 2080 | tf_op jit(solution)/shard_map/ppermute | solution.py:261
  27.0 0.0 collective-permute-done.6.first.refs_1_
  27.0 0.1 gain_share.1
  27.1 0.0 collective-permute-start.11
  27.1 1.2 %collective-permute-done.11 = f32[8,128]{1,0:T(8,128)S(1)} collective-permute-done((f32[8,128]{1,0:T(8,128)S(1)}, f32[8,128]{1,0:T(8,128)S(1)}, u32[]{:S(2)}, u32[]{:S(2)}) %collective-permute-start.11) | collective-permute-done | bytes 4128 | tf_op jit(solution)/shard_map/ppermute | solution.py:317
  28.3 2.4 %collective-permute-start.14 = (f32[8,128]{1,0:T(8,128)S(1)}, f32[8,128]{1,0:T(8,128)S(1)}, u32[]{:S(2)}, u32[]{:S(2)}) collective-permute-start(f32[8,128]{1,0:T(8,128)S(1)} %add.3.refs_4_), channel_id=1, source_target_pairs={{0,24},{4,28},{8,16},{12,20},{16,8},{20,12},{24,0},{28,4},{1,25},{... | collective-permute-start | bytes 12296 | tf_op jit(solution)/shard_map/ppermute | solution.py:319
  30.7 0.5 %collective-permute-start.13 = (f32[8,128]{1,0:T(8,128)S(1)}, f32[8,128]{1,0:T(8,128)S(1)}, u32[]{:S(2)}, u32[]{:S(2)}) collective-permute-start(f32[8,128]{1,0:T(8,128)S(1)} %add.3.refs_4_), channel_id=1, source_target_pairs={{0,16},{4,20},{8,24},{12,28},{16,0},{20,4},{24,8},{28,12},{1,17},{... | collective-permute-start | bytes 12296 | tf_op jit(solution)/shard_map/ppermute | solution.py:319
  31.2 0.5 %collective-permute-start.12 = (f32[8,128]{1,0:T(8,128)S(1)}, f32[8,128]{1,0:T(8,128)S(1)}, u32[]{:S(2)}, u32[]{:S(2)}) collective-permute-start(f32[8,128]{1,0:T(8,128)S(1)} %add.3.refs_4_), channel_id=1, source_target_pairs={{0,8},{4,12},{8,0},{12,4},{16,24},{20,28},{24,16},{28,20},{1,9},{5... | collective-permute-start | bytes 12296 | tf_op jit(solution)/shard_map/ppermute | solution.py:319
  31.8 2.9 %collective-permute-done.8.refs_3_ = bf16[512,128]{1,0:T(8,128)(2,1)S(1)} collective-permute-done((bf16[512,128]{1,0:T(8,128)(2,1)S(1)}, bf16[512,128]{1,0:T(8,128)(2,1)S(1)}, u32[]{:S(2)}, u32[]{:S(2)}) %collective-permute-start.8) | collective-permute-done | bytes 131104 | tf_op jit(solution)/shard_map/ppermute | solution.py:261
  34.7 0.2 collective-permute-done.12.refs_5_
  34.8 0.9 %unpack_heads.1 = (bf16[1,112,512]{2,1,0:T(8,128)(2,1)}, bf16[1,16,512]{2,1,0:T(8,128)(2,1)}, bf16[1,3,112,512]{3,2,1,0:T(8,128)(2,1)}, bf16[1,3,16,512]{3,2,1,0:T(8,128)(2,1)}, f32[1,64]{1,0:T(1,128)}) custom-call(bf16[512,128]{1,0:T(8,128)(2,1)S(1)} %get-tuple-element.59.refs_0_, bf16[528,128]{1,0:T(8,128)(2,1)S(1)} %collective-permute-done.6.first.refs_1_, ...), custom_call_target="tpu_custom_call" | custom-call | tf_op jit(solution)/shard_map/unpack_heads/pallas_call | solution.py:248
  (11 shorter events, 0.0 us)
Async XLA Ops:
  0.6 13.3 %copy-start = (f32[512,128]{1,0:T(8,128)S(1)}, f32[512,128]{1,0:T(8,128)}, u32[]{:S(2)}) copy-start(f32[512,128]{1,0:T(8,128)} %constant.5.clone.sin_ref) | copy-start | bytes 786436
  0.6 13.3 %copy-start.1 = (f32[512,128]{1,0:T(8,128)S(1)}, f32[512,128]{1,0:T(8,128)}, u32[]{:S(2)}) copy-start(f32[512,128]{1,0:T(8,128)} %constant.4.clone.cos_ref) | copy-start | bytes 786436
  1.9 9.9 %collective-permute-start = (bf16[3,128,128]{2,1,0:T(8,128)(2,1)S(1)}, bf16[3,128,128]{2,1,0:T(8,128)(2,1)S(1)}, u32[]{:S(2)}, u32[]{:S(2)}) collective-permute-start(bf16[3,128,128]{2,1,0:T(8,128)(2,1)S(1)} %get-tuple-element.38), channel_id=1, source_target_pairs={{0,1},{1,2},{2,3},{3,0},{4,5},{5,6},{6,7},{7,4},{8,9},{9,10},{10,1... | collective-permute-start | bytes 294920 | tf_op jit(solution)/shard_map/ppermute | solution.py:261
  5.0 9.1 %collective-permute-start.1 = (bf16[3,128,128]{2,1,0:T(8,128)(2,1)S(1)}, bf16[3,128,128]{2,1,0:T(8,128)(2,1)S(1)}, u32[]{:S(2)}, u32[]{:S(2)}) collective-permute-start(bf16[3,128,128]{2,1,0:T(8,128)(2,1)S(1)} %get-tuple-element.39), channel_id=1, source_target_pairs={{0,3},{1,0},{2,1},{3,2},{4,7},{5,4},{6,5},{7,6},{8,11},{9,8},{10,9... | collective-permute-start | bytes 294920 | tf_op jit(solution)/shard_map/ppermute | solution.py:261
  7.0 10.7 %collective-permute-start.2 = (bf16[3,128,128]{2,1,0:T(8,128)(2,1)S(1)}, bf16[3,128,128]{2,1,0:T(8,128)(2,1)S(1)}, u32[]{:S(2)}, u32[]{:S(2)}) collective-permute-start(bf16[3,128,128]{2,1,0:T(8,128)(2,1)S(1)} %get-tuple-element.40), channel_id=1, source_target_pairs={{0,2},{1,3},{2,0},{3,1},{4,6},{5,7},{6,4},{7,5},{8,10},{9,11},{10,... | collective-permute-start | bytes 294920 | tf_op jit(solution)/shard_map/ppermute | solution.py:261
  8.0 5.9 %copy-start.2 = (f32[4,128]{1,0:T(4,128)S(1)}, f32[4,128]{1,0:T(4,128)}, u32[]{:S(2)}) copy-start(f32[4,128]{1,0:T(4,128)} %refs_18_.1) | copy-start | bytes 6148
  8.0 10.7 %collective-permute-start.3 = (bf16[128,128]{1,0:T(8,128)(2,1)S(1)}, bf16[128,128]{1,0:T(8,128)(2,1)S(1)}, u32[]{:S(2)}, u32[]{:S(2)}) collective-permute-start(bf16[128,128]{1,0:T(8,128)(2,1)S(1)} %get-tuple-element.41), channel_id=1, source_target_pairs={{0,1},{1,2},{2,3},{3,0},{4,5},{5,6},{6,7},{7,4},{8,9},{9,10},{10,1... | collective-permute-start | bytes 98312 | tf_op jit(solution)/shard_map/ppermute | solution.py:261
  9.6 9.1 %collective-permute-start.4 = (bf16[128,128]{1,0:T(8,128)(2,1)S(1)}, bf16[128,128]{1,0:T(8,128)(2,1)S(1)}, u32[]{:S(2)}, u32[]{:S(2)}) collective-permute-start(bf16[128,128]{1,0:T(8,128)(2,1)S(1)} %get-tuple-element.42), channel_id=1, source_target_pairs={{0,3},{1,0},{2,1},{3,2},{4,7},{5,4},{6,5},{7,6},{8,11},{9,8},{10,9... | collective-permute-start | bytes 98312 | tf_op jit(solution)/shard_map/ppermute | solution.py:261
  11.8 7.1 %collective-permute-start.5 = (bf16[128,128]{1,0:T(8,128)(2,1)S(1)}, bf16[128,128]{1,0:T(8,128)(2,1)S(1)}, u32[]{:S(2)}, u32[]{:S(2)}) collective-permute-start(bf16[128,128]{1,0:T(8,128)(2,1)S(1)} %get-tuple-element.43), channel_id=1, source_target_pairs={{0,2},{1,3},{2,0},{3,1},{4,6},{5,7},{6,4},{7,5},{8,10},{9,11},{10,... | collective-permute-start | bytes 98312 | tf_op jit(solution)/shard_map/ppermute | solution.py:261
  19.9 7.2 %collective-permute-start.6 = (bf16[528,128]{1,0:T(8,128)(2,1)S(1)}, bf16[528,128]{1,0:T(8,128)(2,1)S(1)}, u32[]{:S(2)}, u32[]{:S(2)}) collective-permute-start(bf16[528,128]{1,0:T(8,128)(2,1)S(1)} %get-tuple-element.60), channel_id=1, source_target_pairs={{0,3},{1,0},{2,1},{3,2},{4,7},{5,4},{6,5},{7,6},{8,11},{9,8},{10,9... | collective-permute-start | bytes 405512 | tf_op jit(solution)/shard_map/ppermute | solution.py:261
  21.6 4.5 %collective-permute-start.10 = (f32[4,128]{1,0:T(4,128)S(1)}, f32[4,128]{1,0:T(4,128)S(1)}, u32[]{:S(2)}, u32[]{:S(2)}) collective-permute-start(f32[4,128]{1,0:T(4,128)S(1)} %get-tuple-element.63.refs_0_), channel_id=1, source_target_pairs={{0,2},{1,3},{2,0},{3,1},{4,6},{5,7},{6,4},{7,5},{8,10},{9,11},{10,... | collective-permute-start | bytes 6152 | tf_op jit(solution)/shard_map/ppermute | solution.py:261
  21.6 5.4 %collective-permute-start.9 = (f32[4,128]{1,0:T(4,128)S(1)}, f32[4,128]{1,0:T(4,128)S(1)}, u32[]{:S(2)}, u32[]{:S(2)}) collective-permute-start(f32[4,128]{1,0:T(4,128)S(1)} %get-tuple-element.63.refs_0_), channel_id=1, source_target_pairs={{0,1},{1,2},{2,3},{3,0},{4,5},{5,6},{6,7},{7,4},{8,9},{9,10},{10,1... | collective-permute-start | bytes 6152 | tf_op jit(solution)/shard_map/ppermute | solution.py:261
  22.3 9.5 %collective-permute-start.7 = (bf16[512,128]{1,0:T(8,128)(2,1)S(1)}, bf16[512,128]{1,0:T(8,128)(2,1)S(1)}, u32[]{:S(2)}, u32[]{:S(2)}) collective-permute-start(bf16[512,128]{1,0:T(8,128)(2,1)S(1)} %get-tuple-element.61), channel_id=1, source_target_pairs={{0,1},{1,2},{2,3},{3,0},{4,5},{5,6},{6,7},{7,4},{8,9},{9,10},{10,1... | collective-permute-start | bytes 393224 | tf_op jit(solution)/shard_map/ppermute | solution.py:261
  25.1 9.5 %collective-permute-start.8 = (bf16[512,128]{1,0:T(8,128)(2,1)S(1)}, bf16[512,128]{1,0:T(8,128)(2,1)S(1)}, u32[]{:S(2)}, u32[]{:S(2)}) collective-permute-start(bf16[512,128]{1,0:T(8,128)(2,1)S(1)} %get-tuple-element.62), channel_id=1, source_target_pairs={{0,2},{1,3},{2,0},{3,1},{4,6},{5,7},{6,4},{7,5},{8,10},{9,11},{10,... | collective-permute-start | bytes 393224 | tf_op jit(solution)/shard_map/ppermute | solution.py:261
  27.1 1.2 %collective-permute-start.11 = (f32[8,128]{1,0:T(8,128)S(1)}, f32[8,128]{1,0:T(8,128)S(1)}, u32[]{:S(2)}, u32[]{:S(2)}) collective-permute-start(f32[8,128]{1,0:T(8,128)S(1)} %gain_share.1), channel_id=1, source_target_pairs={{0,4},{4,0},{8,12},{12,8},{16,20},{20,16},{24,28},{28,24},{1,5},{5... | collective-permute-start | bytes 12296 | tf_op jit(solution)/shard_map/ppermute | solution.py:317
  28.3 6.4 %collective-permute-start.14 = (f32[8,128]{1,0:T(8,128)S(1)}, f32[8,128]{1,0:T(8,128)S(1)}, u32[]{:S(2)}, u32[]{:S(2)}) collective-permute-start(f32[8,128]{1,0:T(8,128)S(1)} %add.3.refs_4_), channel_id=1, source_target_pairs={{0,24},{4,28},{8,16},{12,20},{16,8},{20,12},{24,0},{28,4},{1,25},{... | collective-permute-start | bytes 12296 | tf_op jit(solution)/shard_map/ppermute | solution.py:319
  30.7 3.9 %collective-permute-start.13 = (f32[8,128]{1,0:T(8,128)S(1)}, f32[8,128]{1,0:T(8,128)S(1)}, u32[]{:S(2)}, u32[]{:S(2)}) collective-permute-start(f32[8,128]{1,0:T(8,128)S(1)} %add.3.refs_4_), channel_id=1, source_target_pairs={{0,16},{4,20},{8,24},{12,28},{16,0},{20,4},{24,8},{28,12},{1,17},{... | collective-permute-start | bytes 12296 | tf_op jit(solution)/shard_map/ppermute | solution.py:319
  31.2 3.6 %collective-permute-start.12 = (f32[8,128]{1,0:T(8,128)S(1)}, f32[8,128]{1,0:T(8,128)S(1)}, u32[]{:S(2)}, u32[]{:S(2)}) collective-permute-start(f32[8,128]{1,0:T(8,128)S(1)} %add.3.refs_4_), channel_id=1, source_target_pairs={{0,8},{4,12},{8,0},{12,4},{16,24},{20,28},{24,16},{28,20},{1,9},{5... | collective-permute-start | bytes 12296 | tf_op jit(solution)/shard_map/ppermute | solution.py:319

commit v5 on v4

--- a/solution.py
+++ b/solution.py
@@ -23,7 +23,7 @@
 
 
 def distances(n):
-    return sorted(range(n), key=lambda d: (min(d, n - d), d))
+    return [0, n - 1, *range(1, n - 1)]
 
 
 def rope_tables(n, txt_rows, img_rows):
@@ -72,7 +72,7 @@
         copy.wait()
     iq, tq, ic, tc = held
     for step in range(n):
-        head = lax.rem(me + distances(n)[step], n)
+        head = me ^ distances(n)[step]
         cols = pl.ds(pl.multiple_of(head * HD, HD), HD)
         outs[step][:3, :txt_rows] = tq[0, :, :, cols]
         outs[step][:3, txt_rows:] = iq[0, :, :, cols]
@@ -82,23 +82,27 @@
 
 
 def unpack_kernel(n, *refs):
-    ins, parts = refs[:n], refs[n:-5]
-    io, to, ig, tg, gain = refs[-5:]
+    ins = refs[:n]
+    io, to, ig, tg = refs[n:]
     txt_rows = to.shape[1]
     rows = txt_rows + io.shape[1]
-    total = sum(part[...] for part in parts)
-    owner = lax.broadcasted_iota(jnp.int32, total.shape, 0) == lax.axis_index("dp")
-    total = jnp.sum(jnp.where(owner, total, 0.0), axis=0, keepdims=True)
-    gain[...] = total[:, : gain.shape[1]]
     me = lax.axis_index("seq")
     for step in range(n):
-        head = lax.rem(me + distances(n)[step], n)
+        head = me ^ distances(n)[step]
         cols = pl.ds(pl.multiple_of(head * HD, HD), HD)
         for slot in range(4):
             txt, img = (to, io) if slot == 3 else (tg.at[:, slot], ig.at[:, slot])
             at = slot * rows
             txt[0, :, cols] = ins[step][at : at + txt_rows]
             img[0, :, cols] = ins[step][at + txt_rows : at + rows]
+
+
+def gain_kernel(*refs):
+    parts, gain = refs[:-1], refs[-1]
+    total = sum(part[...] for part in parts)
+    owner = lax.broadcasted_iota(jnp.int32, total.shape, 0) == lax.axis_index("dp")
+    total = jnp.sum(jnp.where(owner, total, 0.0), axis=0, keepdims=True)
+    gain[...] = total[:, : gain.shape[1]]
 
 
 def table_kernel(n, txt_rows, cos_ref, sin_ref, gains_ref, cos_out, sin_out, *gain_tables):
@@ -109,7 +113,7 @@
     swapped = jnp.where(lane % 2 == 0, pltpu.roll(gains, HD - 1, 1), pltpu.roll(gains, 1, 1))
     is_txt = lax.broadcasted_iota(jnp.int32, (rows, HD), 0) < txt_rows
     for step in range(n):
-        owner = lax.rem(me + (n - distances(n)[step]), n)
+        owner = me ^ distances(n)[step]
         src = pl.ds(pl.multiple_of(owner * rows, rows), rows)
         dst = slice(step * rows, (step + 1) * rows)
         cos, sin = cos_ref[src, :], sin_ref[src, :]
@@ -127,7 +131,7 @@
 def forward_kernel(n, block_rows, *refs):
     ins, tables = refs[:n], refs[n : n + 4]
     outs = refs[n + 4 : 2 * n + 4]
-    q_rot, k_rot, q_inv, k_inv, prob = refs[2 * n + 4 :]
+    q_rot, k_rot, q_inv, k_inv, prob, scaled = refs[2 * n + 4 :]
     rows = ins[0].shape[1]
     seq_len = n * rows
     swap = pair_swap()
@@ -154,9 +158,11 @@
         s = lax.dot_general(q_rot[at, :HD], k, LAST, preferred_element_type=f32)
         e = jnp.exp2(s * (SCALE * LOG2_E))
         total = sum(e[:, j * HD : (j + 1) * HD] for j in range(seq_len // HD))
-        p = e * (1.0 / lane_sum(total))
-        prob[at, :] = p
-        o = jnp.dot(p.astype(bf16), v, preferred_element_type=f32).astype(bf16)
+        inv = 1.0 / lane_sum(total)
+        scaled[at, :] = e * (inv * SCALE)
+        pb = (e * inv).astype(bf16)
+        prob[at, :] = pb
+        o = jnp.dot(pb, v, preferred_element_type=f32).astype(bf16)
         for j in range(per_block):
             outs[i * per_block + j][...] = o[j * rows : (j + 1) * rows]
 
@@ -166,12 +172,12 @@
     ins, cots, refs = refs[:n], refs[n : 2 * n - 1], refs[2 * n - 1 :]
     cots = [ins[j].at[3] for j in range(1)] + list(cots)
     outs, refs = refs[:n], refs[n:]
-    q_rot, k_rot, q_inv, k_inv, prob, cos_ref, sin_ref, gains_ref = refs[:8]
-    blocks, gain_out = refs[8 : n + 8], refs[n + 8]
+    q_rot, k_rot, q_inv, k_inv, prob, scaled, cos_ref, sin_ref, gains_ref = refs[:9]
+    blocks, gain_out = refs[9 : n + 9], refs[n + 9]
     grads = [
         [block.at[slot * rows : (slot + 1) * rows] for slot in range(4)] for block in blocks
     ]
-    q_acc, k_acc, v_acc = refs[n + 9 :]
+    q_acc, k_acc, v_acc = refs[n + 10 :]
     seq_len = n * rows
     v = jnp.concatenate([ins[step][2] for step in range(n)], axis=0)
     per_block = block_rows // rows
@@ -181,10 +187,9 @@
         g = jnp.concatenate([cots[j][...] for j in mine], axis=0)
         o = jnp.concatenate([outs[j][...] for j in mine], axis=0)
         delta = lane_sum(g.astype(f32) * o.astype(f32))
-        p = prob[at, :]
         dp = lax.dot_general(g, v, LAST, preferred_element_type=f32)
-        ds = (p * (dp - delta) * SCALE).astype(bf16)
-        dv = lax.dot_general(p.astype(bf16), g, FIRST, preferred_element_type=f32)
+        ds = (scaled[at, :] * (dp - delta)).astype(bf16)
+        dv = lax.dot_general(prob[at, :], g, FIRST, preferred_element_type=f32)
         q_acc[at, :] = jnp.dot(ds, k_rot[...], preferred_element_type=f32)
         dk = lax.dot_general(ds, q_rot[at, :], FIRST, preferred_element_type=f32)
         if i == 0:
@@ -241,7 +246,7 @@
     seq_len = n * rows
     per = 4 * HD // dp
     block_rows = min(seq_len, 512)
-    limit = 8 * MIB + 32 * block_rows * seq_len + 4 * seq_len * seq_len
+    limit = 8 * MIB + 32 * block_rows * seq_len + 6 * seq_len * seq_len
 
     def call(kernel, name, operands, out_shape, scratch=(), in_specs=None, flops=None):
         cost = flops and pl.CostEstimate(flops=flops, bytes_accessed=MIB, transcendentals=0)
@@ -256,12 +261,11 @@
             name=name,
         )(*operands)
 
-    def send(block, d, sign):
-        hop = sign * distances(n)[d]
-        return lax.ppermute(block, "seq", [(i, (i + hop) % n) for i in range(n)])
-
-    def exchange(blocks, sign):
-        return [blocks[0]] + [send(blocks[d], d, sign) for d in range(1, n)]
+    def send(block, d):
+        return lax.ppermute(block, "seq", [(i, i ^ distances(n)[d]) for i in range(n)])
+
+    def exchange(blocks):
+        return [blocks[0]] + [send(blocks[d], d) for d in range(1, n)]
 
     def shape(dims, dtype=f32):
         return jax.ShapeDtypeStruct(dims, dtype)
@@ -278,8 +282,8 @@
         [pl.BlockSpec(memory_space=pltpu.HBM)] * 4,
     )
     cos, sin = rope_tables(n, txt_rows, img_rows)
-    qkv = exchange(packed[:n], 1)
-    cot = [send(packed[n + i], 1 + i, 1) for i in range(n - 1)]
+    qkv = exchange(packed[:n])
+    cot = [send(packed[n + i], 1 + i) for i in range(n - 1)]
     tables = call(
         functools.partial(table_kernel, n, txt_rows),
         "rope_tables",
@@ -293,7 +297,7 @@
         [one] * n
         + [shape((seq_len, 2 * HD), bf16)] * 2
         + [shape((seq_len, HD))] * 2
-        + [shape((seq_len, seq_len))],
+        + [shape((seq_len, seq_len), bf16), shape((seq_len, seq_len))],
     )
     grad_scale = 1.0 / math.sqrt(dp * seq_len * (width // HD))
     backward = call(
@@ -304,9 +308,11 @@
         + [shape((4, HD))],
         [pltpu.VMEM((seq_len, 2 * HD), f32)] * 2 + [pltpu.VMEM((seq_len, HD), f32)],
     )
-    first = send(backward[1], 1, -1)
-    small = [backward[n]] + [send(backward[n], d, -1) for d in range(2, n)]
-    grads = [backward[0], first] + [send(backward[d], d, -1) for d in range(2, n)]
+    order = [1, *range(n - 1, 1, -1)]
+    back = {d: send(backward[d], d) for d in order}
+    first = back[1]
+    small = [backward[n]] + [send(backward[n], d) for d in order[1:]]
+    grads = [backward[0]] + [back[d] for d in range(1, n)]
     (part,) = call(
         functools.partial(share_kernel, n, per),
         "gain_share",
@@ -318,18 +324,19 @@
     parts = [part] + [
         lax.ppermute(part, "dp", [(i, i ^ d) for i in range(dp)]) for d in range(2, dp, 2)
     ]
-    io, to, ig, tg, gain = call(
+    io, to, ig, tg = call(
         functools.partial(unpack_kernel, n),
         "unpack_heads",
-        (*grads, *parts),
+        grads,
         [
             shape((1, img_rows, width), bf16),
             shape((1, txt_rows, width), bf16),
             shape((1, 3, img_rows, width), bf16),
             shape((1, 3, txt_rows, width), bf16),
-            shape((1, per)),
         ],
     )
+    *parts, to = lax.optimization_barrier((*parts, to))
+    (gain,) = call(gain_kernel, "gain_sum", parts, [shape((1, per))])
     return io, to, jnp.swapaxes(ig, 1, 2), jnp.swapaxes(tg, 1, 2), gain.reshape(per)
 
 

time: 35.9 us -> 35.7 us (level)
  Pallas kernels: 4.21 us -> 4.69 us
  waiting for transfers between devices: 9.13 us -> 8.73 us
    ppermute x11, waiting for transfers between devices: 7.78 us -> 5.85 us  [send(): lax.ppermute(block, 'seq', [(i, i ^ distances(n)[d]) for i in range(n)])]
    ppermute x3, waiting for transfers between devices: 0.2 us -> 1.73 us  [per_device(): lax.ppermute(part, 'dp', [(i, i ^ d) for i in range(dp)])]
    pallas_call x6 -> x7, Pallas kernels: 4.21 us -> 4.69 us  [call(): pl.pallas_call(kernel, out_shape=out_shape, in_specs=in_specs or [VMEM] *...]
  transfers between devices with their start and end apart: 15 -> 15, of which waited for: 7 -> 8; matrix products, arithmetic and copies ran while one was open for 0% -> 0% of each run, Pallas kernels for 3% -> 6%
where the time goes in v5:
time: 35.7 us; the launch traced here: 35.5 us
  starting transfers between devices  21.4 us (60%)
  waiting for transfers between devices  8.73 us (24%)
  Pallas kernels  4.69 us (13%)
  between operations  0.72 us (2%)
    ppermute x11, starting transfers between devices, send(): lax.ppermute(block, 'seq', [(i, i ^ distances(n)[d]) for i in range(n)])  17.9 us
    ppermute x11, waiting for transfers between devices, send(): lax.ppermute(block, 'seq', [(i, i ^ distances(n)[d]) for i in range(n)])  5.85 us
    pallas_call x7, Pallas kernels, call(): pl.pallas_call(kernel, out_shape=out_shape, in_specs=in_specs or [VMEM] *...  4.69 us
    ppermute x3, starting transfers between devices, per_device(): lax.ppermute(part, 'dp', [(i, i ^ d) for i in range(dp)])  3.49 us
    ppermute x3, waiting for transfers between devices, per_device(): lax.ppermute(part, 'dp', [(i, i ^ d) for i in range(dp)])  1.73 us
    ppermute x1, waiting for transfers between devices, per_device(): part = part + lax.ppermute(part, 'dp', [(i, i ^ 1) for i in range(dp)])  1.15 us
  transfers between devices with their start and end apart: 15, of which 8 were waited for; matrix products, arithmetic and copies ran while one was open for 0% of the time, Pallas kernels for 6%

profile of v5, /device:TPU:0, one launch (start us, length us, event | category | flops | bytes accessed | tf_op | source)
XLA Modules:
  0.0 35.5 jit_solution(2176390221978208107)
XLA Ops:
  0.6 0.0 copy-start
  0.6 0.0 copy-start.1
  0.7 1.2 %pack_heads.1 = (bf16[4,128,128]{2,1,0:T(8,128)(2,1)S(1)}, bf16[3,128,128]{2,1,0:T(8,128)(2,1)S(1)}, bf16[3,128,128]{2,1,0:T(8,128)(2,1)S(1)}, bf16[3,128,128]{2...) custom-call(bf16[1,3,112,512]{3,2,1,0:T(8,128)(2,1)} %bitcast.5, ...), custom_call_target="tpu_custom_call" | custom-call | tf_op jit(solution)/shard_map/pack_heads/pallas_call | solution.py:253
  1.9 5.1 %collective-permute-start = (bf16[3,128,128]{2,1,0:T(8,128)(2,1)S(1)}, bf16[3,128,128]{2,1,0:T(8,128)(2,1)S(1)}, u32[]{:S(2)}, u32[]{:S(2)}) collective-permute-start(bf16[3,128,128]{2,1,0:T(8,128)(2,1)S(1)} %get-tuple-element.43), channel_id=1, source_target_pairs={{0,3},{1,2},{2,1},{3,0},{4,7},{5,6},{6,5},{7,4},{8,11},{9,10},{10,... | collective-permute-start | bytes 294920 | tf_op jit(solution)/shard_map/ppermute | solution.py:265
  7.0 0.6 %collective-permute-start.2 = (bf16[3,128,128]{2,1,0:T(8,128)(2,1)S(1)}, bf16[3,128,128]{2,1,0:T(8,128)(2,1)S(1)}, u32[]{:S(2)}, u32[]{:S(2)}) collective-permute-start(bf16[3,128,128]{2,1,0:T(8,128)(2,1)S(1)} %get-tuple-element.45), channel_id=1, source_target_pairs={{0,2},{1,3},{2,0},{3,1},{4,6},{5,7},{6,4},{7,5},{8,10},{9,11},{10,... | collective-permute-start | bytes 294920 | tf_op jit(solution)/shard_map/ppermute | solution.py:265
  7.6 3.7 %collective-permute-start.3 = (bf16[128,128]{1,0:T(8,128)(2,1)S(1)}, bf16[128,128]{1,0:T(8,128)(2,1)S(1)}, u32[]{:S(2)}, u32[]{:S(2)}) collective-permute-start(bf16[128,128]{1,0:T(8,128)(2,1)S(1)} %get-tuple-element.46), channel_id=1, source_target_pairs={{0,3},{1,2},{2,1},{3,0},{4,7},{5,6},{6,5},{7,4},{8,11},{9,10},{10,... | collective-permute-start | bytes 98312 | tf_op jit(solution)/shard_map/ppermute | solution.py:265
  11.4 0.8 %collective-permute-start.5 = (bf16[128,128]{1,0:T(8,128)(2,1)S(1)}, bf16[128,128]{1,0:T(8,128)(2,1)S(1)}, u32[]{:S(2)}, u32[]{:S(2)}) collective-permute-start(bf16[128,128]{1,0:T(8,128)(2,1)S(1)} %get-tuple-element.48), channel_id=1, source_target_pairs={{0,2},{1,3},{2,0},{3,1},{4,6},{5,7},{6,4},{7,5},{8,10},{9,11},{10,... | collective-permute-start | bytes 98312 | tf_op jit(solution)/shard_map/ppermute | solution.py:265
  12.2 0.1 rope_tables.1
  12.3 1.1 %collective-permute-done.1.refs_2_ = bf16[3,128,128]{2,1,0:T(8,128)(2,1)S(1)} collective-permute-done((bf16[3,128,128]{2,1,0:T(8,128)(2,1)S(1)}, bf16[3,128,128]{2,1,0:T(8,128)(2,1)S(1)}, u32[]{:S(2)}, u32[]{:S(2)}) %collective-permute-start.1) | collective-permute-done | bytes 98336 | tf_op jit(solution)/shard_map/ppermute | solution.py:265
  13.4 3.6 %collective-permute-done.2.refs_3_ = bf16[3,128,128]{2,1,0:T(8,128)(2,1)S(1)} collective-permute-done((bf16[3,128,128]{2,1,0:T(8,128)(2,1)S(1)}, bf16[3,128,128]{2,1,0:T(8,128)(2,1)S(1)}, u32[]{:S(2)}, u32[]{:S(2)}) %collective-permute-start.2) | collective-permute-done | bytes 98336 | tf_op jit(solution)/shard_map/ppermute | solution.py:265
  16.9 1.0 %forward.1 = (bf16[128,128]{1,0:T(8,128)(2,1)S(1)}, bf16[128,128]{1,0:T(8,128)(2,1)S(1)}, bf16[128,128]{1,0:T(8,128)(2,1)S(1)}, bf16[128,128]{1,0:T(8,128)(2,1)S...) custom-call(bf16[4,128,128]{2,1,0:T(8,128)(2,1)S(1)} %get-tuple-elem, ...), custom_call_target="tpu_custom_call" | custom-call | tf_op jit(solution)/shard_map/forward/pallas_call | solution.py:253
  17.9 0.0 collective-permute-done.4.refs_5_
  17.9 0.1 collective-permute-done.5.refs_6_
  18.1 0.9 %backward.1 = (bf16[512,128]{1,0:T(8,128)(2,1)S(1)}, bf16[528,128]{1,0:T(8,128)(2,1)S(1)}, bf16[512,128]{1,0:T(8,128)(2,1)S(1)}, bf16[512,128]{1,0:T(8,128)(2,1)S(1)}, f32[4,128]{1,0:T(4,128)S(1)}) custom-call(bf16[4,128,128]{2,1,0:T(8,128)(2,1)S(1)} %get-tuple-element.42.refs_0_, bf16[3,128,128]{2,1,0:T(8,128)(2,1)S(1)} %collective-permute-done.refs_1_, ...), custom_call_target="tpu_custom_call" | custom-call | tf_op jit(solution)/shard_map/backward/pallas_call | solution.py:253
  19.0 2.6 %collective-permute-start.6 = (bf16[528,128]{1,0:T(8,128)(2,1)S(1)}, bf16[528,128]{1,0:T(8,128)(2,1)S(1)}, u32[]{:S(2)}, u32[]{:S(2)}) collective-permute-start(bf16[528,128]{1,0:T(8,128)(2,1)S(1)} %get-tuple-element.66), channel_id=1, source_target_pairs={{0,3},{1,2},{2,1},{3,0},{4,7},{5,6},{6,5},{7,4},{8,11},{9,10},{10,... | collective-permute-start | bytes 405512 | tf_op jit(solution)/shard_map/ppermute | solution.py:265
  21.6 1.8 %collective-permute-start.9 = (f32[4,128]{1,0:T(4,128)S(1)}, f32[4,128]{1,0:T(4,128)S(1)}, u32[]{:S(2)}, u32[]{:S(2)}) collective-permute-start(f32[4,128]{1,0:T(4,128)S(1)} %get-tuple-element.70.refs_0_), channel_id=1, source_target_pairs={{0,2},{1,3},{2,0},{3,1},{4,6},{5,7},{6,4},{7,5},{8,10},{9,11},{10,... | collective-permute-start | bytes 6152 | tf_op jit(solution)/shard_map/ppermute | solution.py:265
  23.5 0.2 collective-permute-start.7
  23.7 2.9 %collective-permute-start.8 = (bf16[512,128]{1,0:T(8,128)(2,1)S(1)}, bf16[512,128]{1,0:T(8,128)(2,1)S(1)}, u32[]{:S(2)}, u32[]{:S(2)}) collective-permute-start(bf16[512,128]{1,0:T(8,128)(2,1)S(1)} %get-tuple-element.68), channel_id=1, source_target_pairs={{0,2},{1,3},{2,0},{3,1},{4,6},{5,7},{6,4},{7,5},{8,10},{9,11},{10,... | collective-permute-start | bytes 393224 | tf_op jit(solution)/shard_map/ppermute | solution.py:265
  26.6 0.0 collective-permute-done.10.refs_2_
  26.6 0.6 %collective-permute-done.9.refs_1_ = f32[4,128]{1,0:T(4,128)S(1)} collective-permute-done((f32[4,128]{1,0:T(4,128)S(1)}, f32[4,128]{1,0:T(4,128)S(1)}, u32[]{:S(2)}, u32[]{:S(2)}) %collective-permute-start.9) | collective-permute-done | bytes 2080 | tf_op jit(solution)/shard_map/ppermute | solution.py:265
  27.2 0.0 collective-permute-done.6.refs_1_.first
  27.2 0.1 gain_share.1
  27.3 0.0 collective-permute-start.11
  27.3 1.2 %collective-permute-done.11 = f32[8,128]{1,0:T(8,128)S(1)} collective-permute-done((f32[8,128]{1,0:T(8,128)S(1)}, f32[8,128]{1,0:T(8,128)S(1)}, u32[]{:S(2)}, u32[]{:S(2)}) %collective-permute-start.11) | collective-permute-done | bytes 4128 | tf_op jit(solution)/shard_map/ppermute | solution.py:323
  28.4 2.4 %collective-permute-start.14 = (f32[8,128]{1,0:T(8,128)S(1)}, f32[8,128]{1,0:T(8,128)S(1)}, u32[]{:S(2)}, u32[]{:S(2)}) collective-permute-start(f32[8,128]{1,0:T(8,128)S(1)} %add.3.refs_0_), channel_id=1, source_target_pairs={{0,24},{4,28},{8,16},{12,20},{16,8},{20,12},{24,0},{28,4},{1,25},{... | collective-permute-start | bytes 12296 | tf_op jit(solution)/shard_map/ppermute | solution.py:325
  30.9 0.5 %collective-permute-start.13 = (f32[8,128]{1,0:T(8,128)S(1)}, f32[8,128]{1,0:T(8,128)S(1)}, u32[]{:S(2)}, u32[]{:S(2)}) collective-permute-start(f32[8,128]{1,0:T(8,128)S(1)} %add.3.refs_0_), channel_id=1, source_target_pairs={{0,16},{4,20},{8,24},{12,28},{16,0},{20,4},{24,8},{28,12},{1,17},{... | collective-permute-start | bytes 12296 | tf_op jit(solution)/shard_map/ppermute | solution.py:325
  31.4 0.5 %collective-permute-start.12 = (f32[8,128]{1,0:T(8,128)S(1)}, f32[8,128]{1,0:T(8,128)S(1)}, u32[]{:S(2)}, u32[]{:S(2)}) collective-permute-start(f32[8,128]{1,0:T(8,128)S(1)} %add.3.refs_0_), channel_id=1, source_target_pairs={{0,8},{4,12},{8,0},{12,4},{16,24},{20,28},{24,16},{28,20},{1,9},{5... | collective-permute-start | bytes 12296 | tf_op jit(solution)/shard_map/ppermute | solution.py:325
  31.9 0.5 %collective-permute-done.8.refs_3_ = bf16[512,128]{1,0:T(8,128)(2,1)S(1)} collective-permute-done((bf16[512,128]{1,0:T(8,128)(2,1)S(1)}, bf16[512,128]{1,0:T(8,128)(2,1)S(1)}, u32[]{:S(2)}, u32[]{:S(2)}) %collective-permute-start.8) | collective-permute-done | bytes 131104 | tf_op jit(solution)/shard_map/ppermute | solution.py:265
  32.4 0.9 %unpack_heads.1 = (bf16[1,112,512]{2,1,0:T(8,128)(2,1)}, bf16[1,16,512]{2,1,0:T(8,128)(2,1)}, bf16[1,3,112,512]{3,2,1,0:T(8,128)(2,1)}, bf16[1,3,16,512]{3,2,1,0:T(8,128)(2,1)}) custom-call(bf16[512,128]{1,0:T(8,128)(2,1)S(1)} %get-tuple-element.65.refs_0_, bf16[528,128]{1,0:T(8,128)(2,1)S(1)} %collective-permute-done.6.refs_1_.first, ...), custom_call_target="tpu_custom_call" | custom-call | tf_op jit(solution)/shard_map/unpack_heads/pallas_call | solution.py:253
  33.3 1.2 %collective-permute-done.13.refs_2_ = f32[8,128]{1,0:T(8,128)S(1)} collective-permute-done((f32[8,128]{1,0:T(8,128)S(1)}, f32[8,128]{1,0:T(8,128)S(1)}, u32[]{:S(2)}, u32[]{:S(2)}) %collective-permute-start.13) | collective-permute-done | bytes 4128 | tf_op jit(solution)/shard_map/ppermute | solution.py:325
  34.5 0.5 %collective-permute-done.12.refs_1_ = f32[8,128]{1,0:T(8,128)S(1)} collective-permute-done((f32[8,128]{1,0:T(8,128)S(1)}, f32[8,128]{1,0:T(8,128)S(1)}, u32[]{:S(2)}, u32[]{:S(2)}) %collective-permute-start.12) | collective-permute-done | bytes 4128 | tf_op jit(solution)/shard_map/ppermute | solution.py:325
  35.0 0.5 %gain_sum.1 = f32[1,64]{1,0:T(1,128)} custom-call(f32[8,128]{1,0:T(8,128)S(1)} %add.3.refs_0_, f32[8,128]{1,0:T(8,128)S(1)} %collective-permute-done.12.refs_1_, f32[8,128]{1,0:T(8,128)S(1)} %collective-permute-done.13.refs_2_, f32[8,128]{1,0:T(8,128)S(1)} %collective-permute-done.14.refs_3_), custom_call_target="tpu_custom_call" | custom-call | tf_op jit(solution)/shard_map/gain_sum/pallas_call | solution.py:253
  (12 shorter events, 0.0 us)
Async XLA Ops:
  0.6 11.5 %copy-start = (f32[512,128]{1,0:T(8,128)S(1)}, f32[512,128]{1,0:T(8,128)}, u32[]{:S(2)}) copy-start(f32[512,128]{1,0:T(8,128)} %constant.5.clone.sin_ref) | copy-start | bytes 786436
  0.6 11.5 %copy-start.1 = (f32[512,128]{1,0:T(8,128)S(1)}, f32[512,128]{1,0:T(8,128)}, u32[]{:S(2)}) copy-start(f32[512,128]{1,0:T(8,128)} %constant.4.clone.cos_ref) | copy-start | bytes 786436
  1.9 9.5 %collective-permute-start = (bf16[3,128,128]{2,1,0:T(8,128)(2,1)S(1)}, bf16[3,128,128]{2,1,0:T(8,128)(2,1)S(1)}, u32[]{:S(2)}, u32[]{:S(2)}) collective-permute-start(bf16[3,128,128]{2,1,0:T(8,128)(2,1)S(1)} %get-tuple-element.43), channel_id=1, source_target_pairs={{0,3},{1,2},{2,1},{3,0},{4,7},{5,6},{6,5},{7,4},{8,11},{9,10},{10,... | collective-permute-start | bytes 294920 | tf_op jit(solution)/shard_map/ppermute | solution.py:265
  7.0 6.4 %collective-permute-start.1 = (bf16[3,128,128]{2,1,0:T(8,128)(2,1)S(1)}, bf16[3,128,128]{2,1,0:T(8,128)(2,1)S(1)}, u32[]{:S(2)}, u32[]{:S(2)}) collective-permute-start(bf16[3,128,128]{2,1,0:T(8,128)(2,1)S(1)} %get-tuple-element.44), channel_id=1, source_target_pairs={{0,1},{1,0},{2,3},{3,2},{4,5},{5,4},{6,7},{7,6},{8,9},{9,8},{10,11... | collective-permute-start | bytes 294920 | tf_op jit(solution)/shard_map/ppermute | solution.py:265
  7.0 9.9 %collective-permute-start.2 = (bf16[3,128,128]{2,1,0:T(8,128)(2,1)S(1)}, bf16[3,128,128]{2,1,0:T(8,128)(2,1)S(1)}, u32[]{:S(2)}, u32[]{:S(2)}) collective-permute-start(bf16[3,128,128]{2,1,0:T(8,128)(2,1)S(1)} %get-tuple-element.45), channel_id=1, source_target_pairs={{0,2},{1,3},{2,0},{3,1},{4,6},{5,7},{6,4},{7,5},{8,10},{9,11},{10,... | collective-permute-start | bytes 294920 | tf_op jit(solution)/shard_map/ppermute | solution.py:265
  7.6 4.5 %copy-start.2 = (f32[4,128]{1,0:T(4,128)S(1)}, f32[4,128]{1,0:T(4,128)}, u32[]{:S(2)}) copy-start(f32[4,128]{1,0:T(4,128)} %refs_19_.1) | copy-start | bytes 6148
  7.6 10.3 %collective-permute-start.3 = (bf16[128,128]{1,0:T(8,128)(2,1)S(1)}, bf16[128,128]{1,0:T(8,128)(2,1)S(1)}, u32[]{:S(2)}, u32[]{:S(2)}) collective-permute-start(bf16[128,128]{1,0:T(8,128)(2,1)S(1)} %get-tuple-element.46), channel_id=1, source_target_pairs={{0,3},{1,2},{2,1},{3,0},{4,7},{5,6},{6,5},{7,4},{8,11},{9,10},{10,... | collective-permute-start | bytes 98312 | tf_op jit(solution)/shard_map/ppermute | solution.py:265
  11.4 6.5 %collective-permute-start.4 = (bf16[128,128]{1,0:T(8,128)(2,1)S(1)}, bf16[128,128]{1,0:T(8,128)(2,1)S(1)}, u32[]{:S(2)}, u32[]{:S(2)}) collective-permute-start(bf16[128,128]{1,0:T(8,128)(2,1)S(1)} %get-tuple-element.47), channel_id=1, source_target_pairs={{0,1},{1,0},{2,3},{3,2},{4,5},{5,4},{6,7},{7,6},{8,9},{9,8},{10,11... | collective-permute-start | bytes 98312 | tf_op jit(solution)/shard_map/ppermute | solution.py:265
  11.4 6.7 %collective-permute-start.5 = (bf16[128,128]{1,0:T(8,128)(2,1)S(1)}, bf16[128,128]{1,0:T(8,128)(2,1)S(1)}, u32[]{:S(2)}, u32[]{:S(2)}) collective-permute-start(bf16[128,128]{1,0:T(8,128)(2,1)S(1)} %get-tuple-element.48), channel_id=1, source_target_pairs={{0,2},{1,3},{2,0},{3,1},{4,6},{5,7},{6,4},{7,5},{8,10},{9,11},{10,... | collective-permute-start | bytes 98312 | tf_op jit(solution)/shard_map/ppermute | solution.py:265
  19.0 8.2 %collective-permute-start.6 = (bf16[528,128]{1,0:T(8,128)(2,1)S(1)}, bf16[528,128]{1,0:T(8,128)(2,1)S(1)}, u32[]{:S(2)}, u32[]{:S(2)}) collective-permute-start(bf16[528,128]{1,0:T(8,128)(2,1)S(1)} %get-tuple-element.66), channel_id=1, source_target_pairs={{0,3},{1,2},{2,1},{3,0},{4,7},{5,6},{6,5},{7,4},{8,11},{9,10},{10,... | collective-permute-start | bytes 405512 | tf_op jit(solution)/shard_map/ppermute | solution.py:265
  21.6 5.0 %collective-permute-start.10 = (f32[4,128]{1,0:T(4,128)S(1)}, f32[4,128]{1,0:T(4,128)S(1)}, u32[]{:S(2)}, u32[]{:S(2)}) collective-permute-start(f32[4,128]{1,0:T(4,128)S(1)} %get-tuple-element.70.refs_0_), channel_id=1, source_target_pairs={{0,1},{1,0},{2,3},{3,2},{4,5},{5,4},{6,7},{7,6},{8,9},{9,8},{10,11... | collective-permute-start | bytes 6152 | tf_op jit(solution)/shard_map/ppermute | solution.py:265
  21.6 5.5 %collective-permute-start.9 = (f32[4,128]{1,0:T(4,128)S(1)}, f32[4,128]{1,0:T(4,128)S(1)}, u32[]{:S(2)}, u32[]{:S(2)}) collective-permute-start(f32[4,128]{1,0:T(4,128)S(1)} %get-tuple-element.70.refs_0_), channel_id=1, source_target_pairs={{0,2},{1,3},{2,0},{3,1},{4,6},{5,7},{6,4},{7,5},{8,10},{9,11},{10,... | collective-permute-start | bytes 6152 | tf_op jit(solution)/shard_map/ppermute | solution.py:265
  23.5 8.5 %collective-permute-start.7 = (bf16[512,128]{1,0:T(8,128)(2,1)S(1)}, bf16[512,128]{1,0:T(8,128)(2,1)S(1)}, u32[]{:S(2)}, u32[]{:S(2)}) collective-permute-start(bf16[512,128]{1,0:T(8,128)(2,1)S(1)} %get-tuple-element.67), channel_id=1, source_target_pairs={{0,1},{1,0},{2,3},{3,2},{4,5},{5,4},{6,7},{7,6},{8,9},{9,8},{10,11... | collective-permute-start | bytes 393224 | tf_op jit(solution)/shard_map/ppermute | solution.py:265
  23.7 8.7 %collective-permute-start.8 = (bf16[512,128]{1,0:T(8,128)(2,1)S(1)}, bf16[512,128]{1,0:T(8,128)(2,1)S(1)}, u32[]{:S(2)}, u32[]{:S(2)}) collective-permute-start(bf16[512,128]{1,0:T(8,128)(2,1)S(1)} %get-tuple-element.68), channel_id=1, source_target_pairs={{0,2},{1,3},{2,0},{3,1},{4,6},{5,7},{6,4},{7,5},{8,10},{9,11},{10,... | collective-permute-start | bytes 393224 | tf_op jit(solution)/shard_map/ppermute | solution.py:265
  27.3 1.2 %collective-permute-start.11 = (f32[8,128]{1,0:T(8,128)S(1)}, f32[8,128]{1,0:T(8,128)S(1)}, u32[]{:S(2)}, u32[]{:S(2)}) collective-permute-start(f32[8,128]{1,0:T(8,128)S(1)} %gain_share.1), channel_id=1, source_target_pairs={{0,4},{4,0},{8,12},{12,8},{16,20},{20,16},{24,28},{28,24},{1,5},{5... | collective-permute-start | bytes 12296 | tf_op jit(solution)/shard_map/ppermute | solution.py:323
  28.4 4.8 %collective-permute-start.14 = (f32[8,128]{1,0:T(8,128)S(1)}, f32[8,128]{1,0:T(8,128)S(1)}, u32[]{:S(2)}, u32[]{:S(2)}) collective-permute-start(f32[8,128]{1,0:T(8,128)S(1)} %add.3.refs_0_), channel_id=1, source_target_pairs={{0,24},{4,28},{8,16},{12,20},{16,8},{20,12},{24,0},{28,4},{1,25},{... | collective-permute-start | bytes 12296 | tf_op jit(solution)/shard_map/ppermute | solution.py:325
  30.9 3.6 %collective-permute-start.13 = (f32[8,128]{1,0:T(8,128)S(1)}, f32[8,128]{1,0:T(8,128)S(1)}, u32[]{:S(2)}, u32[]{:S(2)}) collective-permute-start(f32[8,128]{1,0:T(8,128)S(1)} %add.3.refs_0_), channel_id=1, source_target_pairs={{0,16},{4,20},{8,24},{12,28},{16,0},{20,4},{24,8},{28,12},{1,17},{... | collective-permute-start | bytes 12296 | tf_op jit(solution)/shard_map/ppermute | solution.py:325
  31.4 3.6 %collective-permute-start.12 = (f32[8,128]{1,0:T(8,128)S(1)}, f32[8,128]{1,0:T(8,128)S(1)}, u32[]{:S(2)}, u32[]{:S(2)}) collective-permute-start(f32[8,128]{1,0:T(8,128)S(1)} %add.3.refs_0_), channel_id=1, source_target_pairs={{0,8},{4,12},{8,0},{12,4},{16,24},{20,28},{24,16},{28,20},{1,9},{5... | collective-permute-start | bytes 12296 | tf_op jit(solution)/shard_map/ppermute | solution.py:325

commit v6 on v5

--- a/solution.py
+++ b/solution.py
@@ -321,8 +321,9 @@
         flops=20 * 10**9,
     )
     part = part + lax.ppermute(part, "dp", [(i, i ^ 1) for i in range(dp)])
+    across = sorted(range(2, dp, 2), key=lambda d: (d & (d - 1) != 0, -d))
     parts = [part] + [
-        lax.ppermute(part, "dp", [(i, i ^ d) for i in range(dp)]) for d in range(2, dp, 2)
+        lax.ppermute(part, "dp", [(i, i ^ d) for i in range(dp)]) for d in across
     ]
     io, to, ig, tg = call(
         functools.partial(unpack_kernel, n),

time: 35.7 us -> 35.7 us (level)
  no operation moved by 1% of the time
where the time goes in v6:
time: 35.7 us; the launch traced here: 35.5 us
  starting transfers between devices  21.4 us (60%)
  waiting for transfers between devices  8.76 us (25%)
  Pallas kernels  4.69 us (13%)
  between operations  0.72 us (2%)
    ppermute x11, starting transfers between devices, send(): lax.ppermute(block, 'seq', [(i, i ^ distances(n)[d]) for i in range(n)])  17.9 us
    ppermute x11, waiting for transfers between devices, send(): lax.ppermute(block, 'seq', [(i, i ^ distances(n)[d]) for i in range(n)])  5.85 us
    pallas_call x7, Pallas kernels, call(): pl.pallas_call(kernel, out_shape=out_shape, in_specs=in_specs or [VMEM] *...  4.69 us
    ppermute x3, starting transfers between devices, per_device(): lax.ppermute(part, 'dp', [(i, i ^ d) for i in range(dp)])  3.49 us
    ppermute x3, waiting for transfers between devices, per_device(): lax.ppermute(part, 'dp', [(i, i ^ d) for i in range(dp)])  1.76 us
    ppermute x1, waiting for transfers between devices, per_device(): part = part + lax.ppermute(part, 'dp', [(i, i ^ 1) for i in range(dp)])  1.15 us
  transfers between devices with their start and end apart: 15, of which 8 were waited for; matrix products, arithmetic and copies ran while one was open for 0% of the time, Pallas kernels for 6%

profile of v6, /device:TPU:0, one launch (start us, length us, event | category | flops | bytes accessed | tf_op | source)
XLA Modules:
  0.0 35.5 jit_solution(6241029473541088430)
XLA Ops:
  0.6 0.0 copy-start
  0.6 0.0 copy-start.1
  0.7 1.2 %pack_heads.1 = (bf16[4,128,128]{2,1,0:T(8,128)(2,1)S(1)}, bf16[3,128,128]{2,1,0:T(8,128)(2,1)S(1)}, bf16[3,128,128]{2,1,0:T(8,128)(2,1)S(1)}, bf16[3,128,128]{2...) custom-call(bf16[1,3,112,512]{3,2,1,0:T(8,128)(2,1)} %bitcast.5, ...), custom_call_target="tpu_custom_call" | custom-call | tf_op jit(solution)/shard_map/pack_heads/pallas_call | solution.py:253
  1.9 5.1 %collective-permute-start = (bf16[3,128,128]{2,1,0:T(8,128)(2,1)S(1)}, bf16[3,128,128]{2,1,0:T(8,128)(2,1)S(1)}, u32[]{:S(2)}, u32[]{:S(2)}) collective-permute-start(bf16[3,128,128]{2,1,0:T(8,128)(2,1)S(1)} %get-tuple-element.43), channel_id=1, source_target_pairs={{0,3},{1,2},{2,1},{3,0},{4,7},{5,6},{6,5},{7,4},{8,11},{9,10},{10,... | collective-permute-start | bytes 294920 | tf_op jit(solution)/shard_map/ppermute | solution.py:265
  7.0 0.6 %collective-permute-start.2 = (bf16[3,128,128]{2,1,0:T(8,128)(2,1)S(1)}, bf16[3,128,128]{2,1,0:T(8,128)(2,1)S(1)}, u32[]{:S(2)}, u32[]{:S(2)}) collective-permute-start(bf16[3,128,128]{2,1,0:T(8,128)(2,1)S(1)} %get-tuple-element.45), channel_id=1, source_target_pairs={{0,2},{1,3},{2,0},{3,1},{4,6},{5,7},{6,4},{7,5},{8,10},{9,11},{10,... | collective-permute-start | bytes 294920 | tf_op jit(solution)/shard_map/ppermute | solution.py:265
  7.6 3.7 %collective-permute-start.3 = (bf16[128,128]{1,0:T(8,128)(2,1)S(1)}, bf16[128,128]{1,0:T(8,128)(2,1)S(1)}, u32[]{:S(2)}, u32[]{:S(2)}) collective-permute-start(bf16[128,128]{1,0:T(8,128)(2,1)S(1)} %get-tuple-element.46), channel_id=1, source_target_pairs={{0,3},{1,2},{2,1},{3,0},{4,7},{5,6},{6,5},{7,4},{8,11},{9,10},{10,... | collective-permute-start | bytes 98312 | tf_op jit(solution)/shard_map/ppermute | solution.py:265
  11.4 0.8 %collective-permute-start.5 = (bf16[128,128]{1,0:T(8,128)(2,1)S(1)}, bf16[128,128]{1,0:T(8,128)(2,1)S(1)}, u32[]{:S(2)}, u32[]{:S(2)}) collective-permute-start(bf16[128,128]{1,0:T(8,128)(2,1)S(1)} %get-tuple-element.48), channel_id=1, source_target_pairs={{0,2},{1,3},{2,0},{3,1},{4,6},{5,7},{6,4},{7,5},{8,10},{9,11},{10,... | collective-permute-start | bytes 98312 | tf_op jit(solution)/shard_map/ppermute | solution.py:265
  12.2 0.1 rope_tables.1
  12.3 1.1 %collective-permute-done.1.refs_2_ = bf16[3,128,128]{2,1,0:T(8,128)(2,1)S(1)} collective-permute-done((bf16[3,128,128]{2,1,0:T(8,128)(2,1)S(1)}, bf16[3,128,128]{2,1,0:T(8,128)(2,1)S(1)}, u32[]{:S(2)}, u32[]{:S(2)}) %collective-permute-start.1) | collective-permute-done | bytes 98336 | tf_op jit(solution)/shard_map/ppermute | solution.py:265
  13.4 3.6 %collective-permute-done.2.refs_3_ = bf16[3,128,128]{2,1,0:T(8,128)(2,1)S(1)} collective-permute-done((bf16[3,128,128]{2,1,0:T(8,128)(2,1)S(1)}, bf16[3,128,128]{2,1,0:T(8,128)(2,1)S(1)}, u32[]{:S(2)}, u32[]{:S(2)}) %collective-permute-start.2) | collective-permute-done | bytes 98336 | tf_op jit(solution)/shard_map/ppermute | solution.py:265
  16.9 1.0 %forward.1 = (bf16[128,128]{1,0:T(8,128)(2,1)S(1)}, bf16[128,128]{1,0:T(8,128)(2,1)S(1)}, bf16[128,128]{1,0:T(8,128)(2,1)S(1)}, bf16[128,128]{1,0:T(8,128)(2,1)S...) custom-call(bf16[4,128,128]{2,1,0:T(8,128)(2,1)S(1)} %get-tuple-elem, ...), custom_call_target="tpu_custom_call" | custom-call | tf_op jit(solution)/shard_map/forward/pallas_call | solution.py:253
  17.9 0.0 collective-permute-done.4.refs_5_
  17.9 0.1 collective-permute-done.5.refs_6_
  18.1 0.9 %backward.1 = (bf16[512,128]{1,0:T(8,128)(2,1)S(1)}, bf16[528,128]{1,0:T(8,128)(2,1)S(1)}, bf16[512,128]{1,0:T(8,128)(2,1)S(1)}, bf16[512,128]{1,0:T(8,128)(2,1)S(1)}, f32[4,128]{1,0:T(4,128)S(1)}) custom-call(bf16[4,128,128]{2,1,0:T(8,128)(2,1)S(1)} %get-tuple-element.42.refs_0_, bf16[3,128,128]{2,1,0:T(8,128)(2,1)S(1)} %collective-permute-done.refs_1_, ...), custom_call_target="tpu_custom_call" | custom-call | tf_op jit(solution)/shard_map/backward/pallas_call | solution.py:253
  19.0 2.6 %collective-permute-start.6 = (bf16[528,128]{1,0:T(8,128)(2,1)S(1)}, bf16[528,128]{1,0:T(8,128)(2,1)S(1)}, u32[]{:S(2)}, u32[]{:S(2)}) collective-permute-start(bf16[528,128]{1,0:T(8,128)(2,1)S(1)} %get-tuple-element.66), channel_id=1, source_target_pairs={{0,3},{1,2},{2,1},{3,0},{4,7},{5,6},{6,5},{7,4},{8,11},{9,10},{10,... | collective-permute-start | bytes 405512 | tf_op jit(solution)/shard_map/ppermute | solution.py:265
  21.6 1.8 %collective-permute-start.9 = (f32[4,128]{1,0:T(4,128)S(1)}, f32[4,128]{1,0:T(4,128)S(1)}, u32[]{:S(2)}, u32[]{:S(2)}) collective-permute-start(f32[4,128]{1,0:T(4,128)S(1)} %get-tuple-element.70.refs_0_), channel_id=1, source_target_pairs={{0,2},{1,3},{2,0},{3,1},{4,6},{5,7},{6,4},{7,5},{8,10},{9,11},{10,... | collective-permute-start | bytes 6152 | tf_op jit(solution)/shard_map/ppermute | solution.py:265
  23.5 0.2 collective-permute-start.7
  23.7 2.9 %collective-permute-start.8 = (bf16[512,128]{1,0:T(8,128)(2,1)S(1)}, bf16[512,128]{1,0:T(8,128)(2,1)S(1)}, u32[]{:S(2)}, u32[]{:S(2)}) collective-permute-start(bf16[512,128]{1,0:T(8,128)(2,1)S(1)} %get-tuple-element.68), channel_id=1, source_target_pairs={{0,2},{1,3},{2,0},{3,1},{4,6},{5,7},{6,4},{7,5},{8,10},{9,11},{10,... | collective-permute-start | bytes 393224 | tf_op jit(solution)/shard_map/ppermute | solution.py:265
  26.6 0.0 collective-permute-done.10.refs_2_
  26.6 0.6 %collective-permute-done.9.refs_1_ = f32[4,128]{1,0:T(4,128)S(1)} collective-permute-done((f32[4,128]{1,0:T(4,128)S(1)}, f32[4,128]{1,0:T(4,128)S(1)}, u32[]{:S(2)}, u32[]{:S(2)}) %collective-permute-start.9) | collective-permute-done | bytes 2080 | tf_op jit(solution)/shard_map/ppermute | solution.py:265
  27.2 0.0 collective-permute-done.6.refs_1_.first
  27.2 0.1 gain_share.1
  27.3 0.0 collective-permute-start.11
  27.3 1.2 %collective-permute-done.11 = f32[8,128]{1,0:T(8,128)S(1)} collective-permute-done((f32[8,128]{1,0:T(8,128)S(1)}, f32[8,128]{1,0:T(8,128)S(1)}, u32[]{:S(2)}, u32[]{:S(2)}) %collective-permute-start.11) | collective-permute-done | bytes 4128 | tf_op jit(solution)/shard_map/ppermute | solution.py:323
  28.4 2.4 %collective-permute-start.14 = (f32[8,128]{1,0:T(8,128)S(1)}, f32[8,128]{1,0:T(8,128)S(1)}, u32[]{:S(2)}, u32[]{:S(2)}) collective-permute-start(f32[8,128]{1,0:T(8,128)S(1)} %add.3.refs_0_), channel_id=1, source_target_pairs={{0,24},{4,28},{8,16},{12,20},{16,8},{20,12},{24,0},{28,4},{1,25},{... | collective-permute-start | bytes 12296 | tf_op jit(solution)/shard_map/ppermute | solution.py:326
  30.9 0.5 %collective-permute-start.13 = (f32[8,128]{1,0:T(8,128)S(1)}, f32[8,128]{1,0:T(8,128)S(1)}, u32[]{:S(2)}, u32[]{:S(2)}) collective-permute-start(f32[8,128]{1,0:T(8,128)S(1)} %add.3.refs_0_), channel_id=1, source_target_pairs={{0,8},{4,12},{8,0},{12,4},{16,24},{20,28},{24,16},{28,20},{1,9},{5... | collective-permute-start | bytes 12296 | tf_op jit(solution)/shard_map/ppermute | solution.py:326
  31.4 0.5 %collective-permute-start.12 = (f32[8,128]{1,0:T(8,128)S(1)}, f32[8,128]{1,0:T(8,128)S(1)}, u32[]{:S(2)}, u32[]{:S(2)}) collective-permute-start(f32[8,128]{1,0:T(8,128)S(1)} %add.3.refs_0_), channel_id=1, source_target_pairs={{0,16},{4,20},{8,24},{12,28},{16,0},{20,4},{24,8},{28,12},{1,17},{... | collective-permute-start | bytes 12296 | tf_op jit(solution)/shard_map/ppermute | solution.py:326
  31.9 0.5 %collective-permute-done.8.refs_3_ = bf16[512,128]{1,0:T(8,128)(2,1)S(1)} collective-permute-done((bf16[512,128]{1,0:T(8,128)(2,1)S(1)}, bf16[512,128]{1,0:T(8,128)(2,1)S(1)}, u32[]{:S(2)}, u32[]{:S(2)}) %collective-permute-start.8) | collective-permute-done | bytes 131104 | tf_op jit(solution)/shard_map/ppermute | solution.py:265
  32.4 0.9 %unpack_heads.1 = (bf16[1,112,512]{2,1,0:T(8,128)(2,1)}, bf16[1,16,512]{2,1,0:T(8,128)(2,1)}, bf16[1,3,112,512]{3,2,1,0:T(8,128)(2,1)}, bf16[1,3,16,512]{3,2,1,0:T(8,128)(2,1)}) custom-call(bf16[512,128]{1,0:T(8,128)(2,1)S(1)} %get-tuple-element.65.refs_0_, bf16[528,128]{1,0:T(8,128)(2,1)S(1)} %collective-permute-done.6.refs_1_.first, ...), custom_call_target="tpu_custom_call" | custom-call | tf_op jit(solution)/shard_map/unpack_heads/pallas_call | solution.py:253
  33.3 1.2 %collective-permute-done.13.refs_2_ = f32[8,128]{1,0:T(8,128)S(1)} collective-permute-done((f32[8,128]{1,0:T(8,128)S(1)}, f32[8,128]{1,0:T(8,128)S(1)}, u32[]{:S(2)}, u32[]{:S(2)}) %collective-permute-start.13) | collective-permute-done | bytes 4128 | tf_op jit(solution)/shard_map/ppermute | solution.py:326
  34.5 0.5 %collective-permute-done.12.refs_1_ = f32[8,128]{1,0:T(8,128)S(1)} collective-permute-done((f32[8,128]{1,0:T(8,128)S(1)}, f32[8,128]{1,0:T(8,128)S(1)}, u32[]{:S(2)}, u32[]{:S(2)}) %collective-permute-start.12) | collective-permute-done | bytes 4128 | tf_op jit(solution)/shard_map/ppermute | solution.py:326
  35.0 0.5 %gain_sum.1 = f32[1,64]{1,0:T(1,128)} custom-call(f32[8,128]{1,0:T(8,128)S(1)} %add.3.refs_0_, f32[8,128]{1,0:T(8,128)S(1)} %collective-permute-done.12.refs_1_, f32[8,128]{1,0:T(8,128)S(1)} %collective-permute-done.13.refs_2_, f32[8,128]{1,0:T(8,128)S(1)} %collective-permute-done.14.refs_3_), custom_call_target="tpu_custom_call" | custom-call | tf_op jit(solution)/shard_map/gain_sum/pallas_call | solution.py:253
  (12 shorter events, 0.0 us)
Async XLA Ops:
  0.6 11.5 %copy-start = (f32[512,128]{1,0:T(8,128)S(1)}, f32[512,128]{1,0:T(8,128)}, u32[]{:S(2)}) copy-start(f32[512,128]{1,0:T(8,128)} %constant.5.clone.sin_ref) | copy-start | bytes 786436
  0.6 11.5 %copy-start.1 = (f32[512,128]{1,0:T(8,128)S(1)}, f32[512,128]{1,0:T(8,128)}, u32[]{:S(2)}) copy-start(f32[512,128]{1,0:T(8,128)} %constant.4.clone.cos_ref) | copy-start | bytes 786436
  1.9 9.5 %collective-permute-start = (bf16[3,128,128]{2,1,0:T(8,128)(2,1)S(1)}, bf16[3,128,128]{2,1,0:T(8,128)(2,1)S(1)}, u32[]{:S(2)}, u32[]{:S(2)}) collective-permute-start(bf16[3,128,128]{2,1,0:T(8,128)(2,1)S(1)} %get-tuple-element.43), channel_id=1, source_target_pairs={{0,3},{1,2},{2,1},{3,0},{4,7},{5,6},{6,5},{7,4},{8,11},{9,10},{10,... | collective-permute-start | bytes 294920 | tf_op jit(solution)/shard_map/ppermute | solution.py:265
  7.0 6.4 %collective-permute-start.1 = (bf16[3,128,128]{2,1,0:T(8,128)(2,1)S(1)}, bf16[3,128,128]{2,1,0:T(8,128)(2,1)S(1)}, u32[]{:S(2)}, u32[]{:S(2)}) collective-permute-start(bf16[3,128,128]{2,1,0:T(8,128)(2,1)S(1)} %get-tuple-element.44), channel_id=1, source_target_pairs={{0,1},{1,0},{2,3},{3,2},{4,5},{5,4},{6,7},{7,6},{8,9},{9,8},{10,11... | collective-permute-start | bytes 294920 | tf_op jit(solution)/shard_map/ppermute | solution.py:265
  7.0 9.9 %collective-permute-start.2 = (bf16[3,128,128]{2,1,0:T(8,128)(2,1)S(1)}, bf16[3,128,128]{2,1,0:T(8,128)(2,1)S(1)}, u32[]{:S(2)}, u32[]{:S(2)}) collective-permute-start(bf16[3,128,128]{2,1,0:T(8,128)(2,1)S(1)} %get-tuple-element.45), channel_id=1, source_target_pairs={{0,2},{1,3},{2,0},{3,1},{4,6},{5,7},{6,4},{7,5},{8,10},{9,11},{10,... | collective-permute-start | bytes 294920 | tf_op jit(solution)/shard_map/ppermute | solution.py:265
  7.6 4.5 %copy-start.2 = (f32[4,128]{1,0:T(4,128)S(1)}, f32[4,128]{1,0:T(4,128)}, u32[]{:S(2)}) copy-start(f32[4,128]{1,0:T(4,128)} %refs_19_.1) | copy-start | bytes 6148
  7.6 10.3 %collective-permute-start.3 = (bf16[128,128]{1,0:T(8,128)(2,1)S(1)}, bf16[128,128]{1,0:T(8,128)(2,1)S(1)}, u32[]{:S(2)}, u32[]{:S(2)}) collective-permute-start(bf16[128,128]{1,0:T(8,128)(2,1)S(1)} %get-tuple-element.46), channel_id=1, source_target_pairs={{0,3},{1,2},{2,1},{3,0},{4,7},{5,6},{6,5},{7,4},{8,11},{9,10},{10,... | collective-permute-start | bytes 98312 | tf_op jit(solution)/shard_map/ppermute | solution.py:265
  11.4 6.5 %collective-permute-start.4 = (bf16[128,128]{1,0:T(8,128)(2,1)S(1)}, bf16[128,128]{1,0:T(8,128)(2,1)S(1)}, u32[]{:S(2)}, u32[]{:S(2)}) collective-permute-start(bf16[128,128]{1,0:T(8,128)(2,1)S(1)} %get-tuple-element.47), channel_id=1, source_target_pairs={{0,1},{1,0},{2,3},{3,2},{4,5},{5,4},{6,7},{7,6},{8,9},{9,8},{10,11... | collective-permute-start | bytes 98312 | tf_op jit(solution)/shard_map/ppermute | solution.py:265
  11.4 6.7 %collective-permute-start.5 = (bf16[128,128]{1,0:T(8,128)(2,1)S(1)}, bf16[128,128]{1,0:T(8,128)(2,1)S(1)}, u32[]{:S(2)}, u32[]{:S(2)}) collective-permute-start(bf16[128,128]{1,0:T(8,128)(2,1)S(1)} %get-tuple-element.48), channel_id=1, source_target_pairs={{0,2},{1,3},{2,0},{3,1},{4,6},{5,7},{6,4},{7,5},{8,10},{9,11},{10,... | collective-permute-start | bytes 98312 | tf_op jit(solution)/shard_map/ppermute | solution.py:265
  19.0 8.2 %collective-permute-start.6 = (bf16[528,128]{1,0:T(8,128)(2,1)S(1)}, bf16[528,128]{1,0:T(8,128)(2,1)S(1)}, u32[]{:S(2)}, u32[]{:S(2)}) collective-permute-start(bf16[528,128]{1,0:T(8,128)(2,1)S(1)} %get-tuple-element.66), channel_id=1, source_target_pairs={{0,3},{1,2},{2,1},{3,0},{4,7},{5,6},{6,5},{7,4},{8,11},{9,10},{10,... | collective-permute-start | bytes 405512 | tf_op jit(solution)/shard_map/ppermute | solution.py:265
  21.6 5.0 %collective-permute-start.10 = (f32[4,128]{1,0:T(4,128)S(1)}, f32[4,128]{1,0:T(4,128)S(1)}, u32[]{:S(2)}, u32[]{:S(2)}) collective-permute-start(f32[4,128]{1,0:T(4,128)S(1)} %get-tuple-element.70.refs_0_), channel_id=1, source_target_pairs={{0,1},{1,0},{2,3},{3,2},{4,5},{5,4},{6,7},{7,6},{8,9},{9,8},{10,11... | collective-permute-start | bytes 6152 | tf_op jit(solution)/shard_map/ppermute | solution.py:265
  21.6 5.5 %collective-permute-start.9 = (f32[4,128]{1,0:T(4,128)S(1)}, f32[4,128]{1,0:T(4,128)S(1)}, u32[]{:S(2)}, u32[]{:S(2)}) collective-permute-start(f32[4,128]{1,0:T(4,128)S(1)} %get-tuple-element.70.refs_0_), channel_id=1, source_target_pairs={{0,2},{1,3},{2,0},{3,1},{4,6},{5,7},{6,4},{7,5},{8,10},{9,11},{10,... | collective-permute-start | bytes 6152 | tf_op jit(solution)/shard_map/ppermute | solution.py:265
  23.5 8.5 %collective-permute-start.7 = (bf16[512,128]{1,0:T(8,128)(2,1)S(1)}, bf16[512,128]{1,0:T(8,128)(2,1)S(1)}, u32[]{:S(2)}, u32[]{:S(2)}) collective-permute-start(bf16[512,128]{1,0:T(8,128)(2,1)S(1)} %get-tuple-element.67), channel_id=1, source_target_pairs={{0,1},{1,0},{2,3},{3,2},{4,5},{5,4},{6,7},{7,6},{8,9},{9,8},{10,11... | collective-permute-start | bytes 393224 | tf_op jit(solution)/shard_map/ppermute | solution.py:265
  23.7 8.7 %collective-permute-start.8 = (bf16[512,128]{1,0:T(8,128)(2,1)S(1)}, bf16[512,128]{1,0:T(8,128)(2,1)S(1)}, u32[]{:S(2)}, u32[]{:S(2)}) collective-permute-start(bf16[512,128]{1,0:T(8,128)(2,1)S(1)} %get-tuple-element.68), channel_id=1, source_target_pairs={{0,2},{1,3},{2,0},{3,1},{4,6},{5,7},{6,4},{7,5},{8,10},{9,11},{10,... | collective-permute-start | bytes 393224 | tf_op jit(solution)/shard_map/ppermute | solution.py:265
  27.3 1.2 %collective-permute-start.11 = (f32[8,128]{1,0:T(8,128)S(1)}, f32[8,128]{1,0:T(8,128)S(1)}, u32[]{:S(2)}, u32[]{:S(2)}) collective-permute-start(f32[8,128]{1,0:T(8,128)S(1)} %gain_share.1), channel_id=1, source_target_pairs={{0,4},{4,0},{8,12},{12,8},{16,20},{20,16},{24,28},{28,24},{1,5},{5... | collective-permute-start | bytes 12296 | tf_op jit(solution)/shard_map/ppermute | solution.py:323
  28.4 4.8 %collective-permute-start.14 = (f32[8,128]{1,0:T(8,128)S(1)}, f32[8,128]{1,0:T(8,128)S(1)}, u32[]{:S(2)}, u32[]{:S(2)}) collective-permute-start(f32[8,128]{1,0:T(8,128)S(1)} %add.3.refs_0_), channel_id=1, source_target_pairs={{0,24},{4,28},{8,16},{12,20},{16,8},{20,12},{24,0},{28,4},{1,25},{... | collective-permute-start | bytes 12296 | tf_op jit(solution)/shard_map/ppermute | solution.py:326
  30.9 3.6 %collective-permute-start.13 = (f32[8,128]{1,0:T(8,128)S(1)}, f32[8,128]{1,0:T(8,128)S(1)}, u32[]{:S(2)}, u32[]{:S(2)}) collective-permute-start(f32[8,128]{1,0:T(8,128)S(1)} %add.3.refs_0_), channel_id=1, source_target_pairs={{0,8},{4,12},{8,0},{12,4},{16,24},{20,28},{24,16},{28,20},{1,9},{5... | collective-permute-start | bytes 12296 | tf_op jit(solution)/shard_map/ppermute | solution.py:326
  31.4 3.6 %collective-permute-start.12 = (f32[8,128]{1,0:T(8,128)S(1)}, f32[8,128]{1,0:T(8,128)S(1)}, u32[]{:S(2)}, u32[]{:S(2)}) collective-permute-start(f32[8,128]{1,0:T(8,128)S(1)} %add.3.refs_0_), channel_id=1, source_target_pairs={{0,16},{4,20},{8,24},{12,28},{16,0},{20,4},{24,8},{28,12},{1,17},{... | collective-permute-start | bytes 12296 | tf_op jit(solution)/shard_map/ppermute | solution.py:326
